TPU v7x, 256 devices: a whole 4x4x8 slice. The times are simulated.
256 devices in a mesh: mkt: 2 (over core), sku: 32 (over y, z), cat: 4 (over x).
Axes of the slice: x: 4, y: 4, z: 8, core: 2. Of those that a mesh axis runs over, the one named last changes fastest.
Arguments:
- features: bfloat16 [1024, 512], P('mkt'), may hold values from -8 to 8
- taste: bfloat16 [512, 4, 65536], P(None, 'cat', 'sku'), may hold values from -3 to 3
- price: float32 [4, 65536], P('cat', 'sku'), may hold values from 0.5 to 2
- alpha: float32 [1024], P('mkt'), may hold values from 0.3 to 1
- market_size: float32 [1024], P('mkt'), may hold values from 0.5 to 8
- store_brand: float32 [4, 128], P('cat'), may hold values from -4 to 4
- sub_scale: float32 [4, 128], P('cat'), may hold values from 0.45 to 0.85
- cat_scale: float32 [4, 16], P('cat'), may hold values from 0.85 to 1
- availability: int32 [1024, 4, 65536], P('mkt', 'cat', 'sku'), may hold values 0 or 1
- sku_subcat: int32 [4, 65536], P('cat', 'sku'), may hold values from 0 to 127, never falling along the last dimension, each value on 1 to 2048 neighbouring positions
- subcat_cat: int32 [4, 128], P('cat'), may hold values from 0 to 15, never falling along the last dimension, each value on 1 to 24 neighbouring positions
- cotangent: bfloat16 [1024, 4, 65536], P('mkt', 'cat', 'sku'), may hold values from -0.29882812 to 0.29882812
Outputs:
- log_demand: float32 [1024, 4, 65536], P('mkt', 'cat', 'sku')
- price_grad: float32 [4, 65536], P('cat', 'sku')
Inputs may be any that keep to these rules, and one draw needn't show every extreme that they name: `sku_subcat`: never falls along a group; every one of the 128 subcategories holds at least one SKU, at most 2048. `subcat_cat`: never falls along a group; every one of the 16 categories holds at least one subcategory.
All inputs are finite; a program needn't handle non-finite values. No bound on the sum of `availability` on one device may be relied on, other than what follows from the above.
Results may differ from a plain program's by a relative error of at most 0.0003.
Values sent between devices are 32-bit elements; how exact they have to be, the bound alone decides.
A program may use at most 128 MiB of HBM per device.

v0:
```python
import math

import jax
import jax.numpy as jnp
from jax import lax
from jax.sharding import PartitionSpec as P


def segment_peak(values, flags):
    rows = values.shape[0]
    block = math.gcd(rows, 32)
    grouped = values.reshape(rows // block, block, values.shape[1])

    def one_block(piece):
        return jnp.max(jnp.where(flags[None, :, :], piece[:, :, None], -jnp.inf), axis=1)

    peaks = lax.map(one_block, grouped)
    return peaks.reshape(rows, flags.shape[1])


def spread(table_values, table_back):
    return jnp.dot(table_values, table_back, precision=lax.Precision.HIGHEST)


def shards(
    features,
    taste,
    price,
    alpha,
    market_size,
    store_brand,
    sub_scale,
    cat_scale,
    availability,
    sku_subcat,
    subcat_cat,
    cotangent,
):
    members = sku_subcat[0]
    parents = subcat_cat[0]
    lam_sub = sub_scale[0]
    rho_cat = cat_scale[0]
    sub_count = lam_sub.shape[0]
    cat_count = rho_cat.shape[0]
    member_flags = members[:, None] == jnp.arange(sub_count)[None, :]
    member_table = member_flags.astype(jnp.float32)
    member_back = jnp.transpose(member_table)
    member_half = member_flags.astype(jnp.bfloat16)
    parent_flags = parents[:, None] == jnp.arange(cat_count)[None, :]
    parent_table = parent_flags.astype(jnp.float32)
    parent_back = jnp.transpose(parent_table)
    utility = (
        jnp.dot(features, taste[:, 0, :], preferred_element_type=jnp.float32)
        - alpha[:, None] * price[0][None, :]
    )
    lam_sku = jnp.dot(lam_sub, member_back, precision=lax.Precision.HIGHEST)
    scaled = utility / lam_sku[None, :]
    offered = availability[:, 0, :] == 1
    cot_half = jnp.where(offered, cotangent[:, 0, :], jnp.zeros_like(cotangent[:, 0, :]))
    cot = cot_half.astype(jnp.float32)
    local_cot = jnp.dot(cot_half, member_half, preferred_element_type=jnp.float32)
    store_scaled = store_brand[0] / lam_sub
    local_top = jnp.maximum(
        segment_peak(jnp.where(offered, scaled, -jnp.inf), member_flags), store_scaled[None, :]
    )
    sub_top = lax.pmax(local_top, "sku")
    weights = jnp.where(offered, jnp.exp(scaled - spread(sub_top, member_back)), 0.0)
    partial_sum = jnp.dot(weights, member_table, precision=lax.Precision.HIGH)
    total = lax.psum(partial_sum, "sku")
    total = total + jnp.exp(store_scaled[None, :] - sub_top)
    sub_value = lam_sub[None, :] * (sub_top + jnp.log(total))
    rho_sub = jnp.dot(rho_cat, parent_back, precision=lax.Precision.HIGHEST)
    ratio_sub = sub_value / rho_sub[None, :]
    cat_max = segment_peak(ratio_sub, parent_flags)
    cat_sum = jnp.dot(
        jnp.exp(ratio_sub - spread(cat_max, parent_back)),
        parent_table,
        precision=lax.Precision.HIGHEST,
    )
    cat_value = rho_cat[None, :] * (cat_max + jnp.log(cat_sum))
    group_peak = jnp.max(cat_value, axis=1)
    top_peak = lax.pmax(group_peak, "cat")
    group_total = jnp.sum(jnp.exp(cat_value - top_peak[:, None]), axis=1)
    grand = lax.psum(group_total, "cat")
    ceiling = jnp.maximum(top_peak, 0.0)
    inclusive = ceiling + jnp.log(jnp.exp(-ceiling) + grand * jnp.exp(top_peak - ceiling))
    log_within = scaled - spread(sub_value / lam_sub[None, :], member_back)
    log_sub = (sub_value - spread(cat_value, parent_back)) / rho_sub[None, :]
    log_cat = cat_value - inclusive[:, None]
    log_path = log_within + spread(log_sub + spread(log_cat, parent_back), member_back)
    log_demand = jnp.where(offered, jnp.log(market_size)[:, None] + log_path, 0.0)
    sub_cot = lax.psum(local_cot, "sku")
    cat_cot = jnp.dot(sub_cot, parent_table, precision=lax.Precision.HIGHEST)
    all_cot = lax.psum(jnp.sum(cat_cot, axis=1), "cat")
    d_cat = (1.0 - 1.0 / rho_cat[None, :]) * cat_cot - all_cot[:, None] * jnp.exp(log_cat)
    d_sub = (1.0 / rho_sub[None, :] - 1.0 / lam_sub[None, :]) * sub_cot + jnp.exp(log_sub) * spread(
        d_cat, parent_back
    )
    d_util = jnp.where(
        offered, cot / lam_sku[None, :] + jnp.exp(log_within) * spread(d_sub, member_back), 0.0
    )
    local_grad = -jnp.dot(alpha, d_util, precision=lax.Precision.HIGHEST)
    grad = lax.psum(local_grad, "mkt")
    return (log_demand[:, None, :], grad[None, :])


def solution(mesh):
    return jax.shard_map(
        shards,
        mesh=mesh,
        in_specs=(
            P("mkt", None),
            P(None, "cat", "sku"),
            P("cat", "sku"),
            P("mkt"),
            P("mkt"),
            P("cat", None),
            P("cat", None),
            P("cat", None),
            P("mkt", "cat", "sku"),
            P("cat", "sku"),
            P("cat", None),
            P("mkt", "cat", "sku"),
        ),
        out_specs=(P("mkt", "cat", "sku"), P("cat", "sku")),
        check_vma=False,
    )
```

profile of v0, /device:TPU:1, one launch (start us, length us, event | category | flops | bytes accessed | tf_op | source)
XLA Modules:
  0.0 574.3 jit_solution(6634561995395232480)
XLA Ops:
  7.2 1.3 fusion.30
  8.8 2.5 subtract_divide_fusion
  11.3 4.5 broadcast_select_fusion
  15.8 184.4 %while.22 = (s32[]{:T(128)}, f32[16,32,128]{2,1,0:T(8,128)S(1)}, f32[16,32,2048]{2,1,0:T(8,128)}, s32[2048]{0:T(1024)S(1)}, s32[]{:T(128)}) while((s32[]{:T(128)}, f32[16,32,128]{2,1,0:T(8,128)S(1)}, f32[16,32,2048]{2,1,0:T(8,128)}, s32[2048]{0:T(1024)S(1)}, s32[]{:T(128)}) %tuple.61), condition=%wide.region_2.3_spmd.clone, body=%wide.region_0.2_spmd.clone.sunk | while | flops 17035264 | bytes 1368133 | solution.py:17
  15.8 1.3 dynamic-slice_bitcast_fusion.4
  17.5 10.1 %select_reduce_fusion.4 = f32[32,128]{1,0:T(8,128)S(1)} fusion(f32[32,2048]{1,0:T(8,128)S(1)} %dynamic-slice_bitcast_fusion.4, pred[2048,128]{1,0:T(8,128)(4,1)S(1)} %iota_compare_fusion.22), kind=kLoop, calls=%fused_computation.2.clone.1 | loop fusion | flops 16773120 | bytes 540672 | tf_op jit(solution)/shard_map/while/body/eval_jaxpr/reduce_max | solution.py:15
  27.7 1.0 dynamic-slice_bitcast_fusion.4
  29.0 10.1 %select_reduce_fusion.4 = f32[32,128]{1,0:T(8,128)S(1)} fusion(f32[32,2048]{1,0:T(8,128)S(1)} %dynamic-slice_bitcast_fusion.4, pred[2048,128]{1,0:T(8,128)(4,1)S(1)} %iota_compare_fusion.22), kind=kLoop, calls=%fused_computation.2.clone.1 | loop fusion | flops 16773120 | bytes 540672 | tf_op jit(solution)/shard_map/while/body/eval_jaxpr/reduce_max | solution.py:15
  39.2 1.0 dynamic-slice_bitcast_fusion.4
  40.5 10.1 %select_reduce_fusion.4 = f32[32,128]{1,0:T(8,128)S(1)} fusion(f32[32,2048]{1,0:T(8,128)S(1)} %dynamic-slice_bitcast_fusion.4, pred[2048,128]{1,0:T(8,128)(4,1)S(1)} %iota_compare_fusion.22), kind=kLoop, calls=%fused_computation.2.clone.1 | loop fusion | flops 16773120 | bytes 540672 | tf_op jit(solution)/shard_map/while/body/eval_jaxpr/reduce_max | solution.py:15
  50.7 1.0 dynamic-slice_bitcast_fusion.4
  52.0 10.1 %select_reduce_fusion.4 = f32[32,128]{1,0:T(8,128)S(1)} fusion(f32[32,2048]{1,0:T(8,128)S(1)} %dynamic-slice_bitcast_fusion.4, pred[2048,128]{1,0:T(8,128)(4,1)S(1)} %iota_compare_fusion.22), kind=kLoop, calls=%fused_computation.2.clone.1 | loop fusion | flops 16773120 | bytes 540672 | tf_op jit(solution)/shard_map/while/body/eval_jaxpr/reduce_max | solution.py:15
  63.5 10.1 %select_reduce_fusion.4 = f32[32,128]{1,0:T(8,128)S(1)} fusion(f32[32,2048]{1,0:T(8,128)S(1)} %dynamic-slice_bitcast_fusion.4, pred[2048,128]{1,0:T(8,128)(4,1)S(1)} %iota_compare_fusion.22), kind=kLoop, calls=%fused_computation.2.clone.1 | loop fusion | flops 16773120 | bytes 540672 | tf_op jit(solution)/shard_map/while/body/eval_jaxpr/reduce_max | solution.py:15
  75.0 10.1 %select_reduce_fusion.4 = f32[32,128]{1,0:T(8,128)S(1)} fusion(f32[32,2048]{1,0:T(8,128)S(1)} %dynamic-slice_bitcast_fusion.4, pred[2048,128]{1,0:T(8,128)(4,1)S(1)} %iota_compare_fusion.22), kind=kLoop, calls=%fused_computation.2.clone.1 | loop fusion | flops 16773120 | bytes 540672 | tf_op jit(solution)/shard_map/while/body/eval_jaxpr/reduce_max | solution.py:15
  86.5 10.1 %select_reduce_fusion.4 = f32[32,128]{1,0:T(8,128)S(1)} fusion(f32[32,2048]{1,0:T(8,128)S(1)} %dynamic-slice_bitcast_fusion.4, pred[2048,128]{1,0:T(8,128)(4,1)S(1)} %iota_compare_fusion.22), kind=kLoop, calls=%fused_computation.2.clone.1 | loop fusion | flops 16773120 | bytes 540672 | tf_op jit(solution)/shard_map/while/body/eval_jaxpr/reduce_max | solution.py:15
  96.7 1.0 dynamic-slice_bitcast_fusion.4
  98.0 10.1 %select_reduce_fusion.4 = f32[32,128]{1,0:T(8,128)S(1)} fusion(f32[32,2048]{1,0:T(8,128)S(1)} %dynamic-slice_bitcast_fusion.4, pred[2048,128]{1,0:T(8,128)(4,1)S(1)} %iota_compare_fusion.22), kind=kLoop, calls=%fused_computation.2.clone.1 | loop fusion | flops 16773120 | bytes 540672 | tf_op jit(solution)/shard_map/while/body/eval_jaxpr/reduce_max | solution.py:15
  108.2 1.0 dynamic-slice_bitcast_fusion.4
  109.5 10.1 %select_reduce_fusion.4 = f32[32,128]{1,0:T(8,128)S(1)} fusion(f32[32,2048]{1,0:T(8,128)S(1)} %dynamic-slice_bitcast_fusion.4, pred[2048,128]{1,0:T(8,128)(4,1)S(1)} %iota_compare_fusion.22), kind=kLoop, calls=%fused_computation.2.clone.1 | loop fusion | flops 16773120 | bytes 540672 | tf_op jit(solution)/shard_map/while/body/eval_jaxpr/reduce_max | solution.py:15
  121.0 10.1 %select_reduce_fusion.4 = f32[32,128]{1,0:T(8,128)S(1)} fusion(f32[32,2048]{1,0:T(8,128)S(1)} %dynamic-slice_bitcast_fusion.4, pred[2048,128]{1,0:T(8,128)(4,1)S(1)} %iota_compare_fusion.22), kind=kLoop, calls=%fused_computation.2.clone.1 | loop fusion | flops 16773120 | bytes 540672 | tf_op jit(solution)/shard_map/while/body/eval_jaxpr/reduce_max | solution.py:15
  132.5 10.1 %select_reduce_fusion.4 = f32[32,128]{1,0:T(8,128)S(1)} fusion(f32[32,2048]{1,0:T(8,128)S(1)} %dynamic-slice_bitcast_fusion.4, pred[2048,128]{1,0:T(8,128)(4,1)S(1)} %iota_compare_fusion.22), kind=kLoop, calls=%fused_computation.2.clone.1 | loop fusion | flops 16773120 | bytes 540672 | tf_op jit(solution)/shard_map/while/body/eval_jaxpr/reduce_max | solution.py:15
  144.0 10.1 %select_reduce_fusion.4 = f32[32,128]{1,0:T(8,128)S(1)} fusion(f32[32,2048]{1,0:T(8,128)S(1)} %dynamic-slice_bitcast_fusion.4, pred[2048,128]{1,0:T(8,128)(4,1)S(1)} %iota_compare_fusion.22), kind=kLoop, calls=%fused_computation.2.clone.1 | loop fusion | flops 16773120 | bytes 540672 | tf_op jit(solution)/shard_map/while/body/eval_jaxpr/reduce_max | solution.py:15
  154.2 1.0 dynamic-slice_bitcast_fusion.4
  155.6 10.1 %select_reduce_fusion.4 = f32[32,128]{1,0:T(8,128)S(1)} fusion(f32[32,2048]{1,0:T(8,128)S(1)} %dynamic-slice_bitcast_fusion.4, pred[2048,128]{1,0:T(8,128)(4,1)S(1)} %iota_compare_fusion.22), kind=kLoop, calls=%fused_computation.2.clone.1 | loop fusion | flops 16773120 | bytes 540672 | tf_op jit(solution)/shard_map/while/body/eval_jaxpr/reduce_max | solution.py:15
  167.1 10.1 %select_reduce_fusion.4 = f32[32,128]{1,0:T(8,128)S(1)} fusion(f32[32,2048]{1,0:T(8,128)S(1)} %dynamic-slice_bitcast_fusion.4, pred[2048,128]{1,0:T(8,128)(4,1)S(1)} %iota_compare_fusion.22), kind=kLoop, calls=%fused_computation.2.clone.1 | loop fusion | flops 16773120 | bytes 540672 | tf_op jit(solution)/shard_map/while/body/eval_jaxpr/reduce_max | solution.py:15
  178.6 10.1 %select_reduce_fusion.4 = f32[32,128]{1,0:T(8,128)S(1)} fusion(f32[32,2048]{1,0:T(8,128)S(1)} %dynamic-slice_bitcast_fusion.4, pred[2048,128]{1,0:T(8,128)(4,1)S(1)} %iota_compare_fusion.22), kind=kLoop, calls=%fused_computation.2.clone.1 | loop fusion | flops 16773120 | bytes 540672 | tf_op jit(solution)/shard_map/while/body/eval_jaxpr/reduce_max | solution.py:15
  190.1 10.1 %select_reduce_fusion.4 = f32[32,128]{1,0:T(8,128)S(1)} fusion(f32[32,2048]{1,0:T(8,128)S(1)} %dynamic-slice_bitcast_fusion.4, pred[2048,128]{1,0:T(8,128)(4,1)S(1)} %iota_compare_fusion.22), kind=kLoop, calls=%fused_computation.2.clone.1 | loop fusion | flops 16773120 | bytes 540672 | tf_op jit(solution)/shard_map/while/body/eval_jaxpr/reduce_max | solution.py:15
  201.2 3.2 fusion.20
  204.4 140.6 %all-reduce.5.cloned.1.call-done = f32[512,128]{1,0:T(8,128)} async-done(((f32[512,128]{1,0:T(8,128)}), f32[512,128]{1,0:T(8,128)}) %all-reduce.5.cloned.1.call-update) | async-done | bytes 262160 | tf_op jit(solution)/shard_map/pmax | solution.py:66
  345.0 3.0 fusion.28
  348.1 2.2 fusion.11
  350.3 144.5 %all-reduce.7.cloned.1.call-done = (f32[512,128]{1,0:T(8,128)}, f32[512,128]{1,0:T(8,128)}) async-done(((f32[512,128]{1,0:T(8,128)}, f32[512,128]{1,0:T(8,128)}), (f32[512,128]{1,0:T(8,128)}, f32[512,128]{1,0:T(8,128)})) %all-reduce.7.cloned.1.call-update) | async-done | bytes 524304 | tf_op jit(solution)/shard_map/psum | solution.py:69
  494.8 1.8 broadcast_divide_fusion
  496.7 12.3 %while.23 = (s32[]{:T(128)}, f32[16,32,16]{2,1,0:T(8,128)}, f32[16,32,128]{2,1,0:T(8,128)S(1)}, s32[128]{0:T(128)S(1)}, s32[]{:T(128)}) while((s32[]{:T(128)}, f32[16,32,16]{2,1,0:T(8,128)}, f32[16,32,128]{2,1,0:T(8,128)S(1)}, s32[128]{0:T(128)S(1)}, s32[]{:T(128)}) %tuple.62), condition=%wide.region_7.8_spmd.clone, body=%wide.region_5.7_spmd.clone.sunk | while | flops 132610 | bytes 74817 | solution.py:17
  508.9 2.0 fusion.21
  510.9 1.0 copy.20
  512.0 1.3 fusion.71
  513.3 8.4 %pmax.15 = f32[512]{0:T(512)S(1)} all-reduce(f32[512]{0:T(512)S(1)} %get-tuple-element.100), channel_id=1, replica_groups=mesh['mkt'=2,'sku'=32,'cat'=4] {'cat'}, use_global_device_ids=true, to_apply=%region_9.10 | all-reduce | flops 512 | bytes 4096 | tf_op jit(solution)/shard_map/pmax | solution.py:82
  521.7 5.2 convolution_subtract_fusion
  526.9 1.1 fusion.23
  528.4 6.2 %all-reduce.1 = (f32[512]{0:T(512)S(1)}, f32[512]{0:T(512)S(1)}) all-reduce(f32[512]{0:T(512)S(1)} %exponential_reduce_fusion, f32[512]{0:T(512)S(1)} %get-tuple-element.102), channel_id=1, replica_groups=mesh['mkt'=2,'sku'=32,'cat'=4] {'cat'}, use_global_device_ids=true, to_apply=%region_11.12 | all-reduce | flops 1024 | bytes 8192 | tf_op jit(solution)/shard_map/psum | solution.py:84
  534.6 1.5 convolution_add_fusion
  536.1 1.5 fusion.22
  537.6 1.9 fusion.29
  539.6 5.2 fusion.4
  544.8 11.9 %psum.39 = f32[1,2048]{1,0:T(1,128)} all-reduce(f32[1,2048]{1,0:T(1,128)S(1)} %bitcast.80), channel_id=1, replica_groups=mesh['mkt'=2,'sku'=32,'cat'=4] {'mkt'}, use_global_device_ids=true, to_apply=%region_15.16 | all-reduce | flops 2048 | bytes 16384 | tf_op jit(solution)/shard_map/psum | solution.py:103
  556.7 4.5 select_bitcast_fusion
  561.1 6.3 %copy.19 = f32[512,1,2048]{2,1,0:T(1,128)} copy(f32[512,1,2048]{2,0,1:T(8,128)S(1)} %select_bitcast_fusion) | data formatting | bytes 8388608
  (150 shorter events, 28.1 us)
Async XLA Ops:
  7.2 1.6 copy-start
  7.2 337.8 %all-reduce.5.cloned.1.call-start = ((), (), s32[]{:S(2)}) async-start(), calls=%async_computation | async-start | bytes 524288 | tf_op jit(solution)/shard_map/pmax | solution.py:66
  8.8 2.5 copy-start.5
  11.3 4.5 copy-start.1
  11.3 4.5 copy-start.8
  15.8 523.8 %copy-start.4 = (pred[512,2048]{1,0:T(32,128)(4,1)}, pred[512,2048]{1,0:T(32,128)(4,1)S(1)}, u32[]{:S(2)}) copy-start(pred[512,2048]{1,0:T(32,128)(4,1)S(1)} %get-tuple-element.97) | copy-start | bytes 3145732
  15.8 184.5 %copy-start.9 = (s32[1,128]{1,0:T(1,128)S(1)}, s32[1,128]{1,0:T(1,128)}, u32[]{:S(2)}) copy-start(s32[1,128]{1,0:T(1,128)} %param.26) | copy-start | bytes 1540
  15.8 184.5 %copy-start.12 = (f32[1,16]{1,0:T(1,128)S(1)}, f32[1,16]{1,0:T(1,128)}, u32[]{:S(2)}) copy-start(f32[1,16]{1,0:T(1,128)} %param.23) | copy-start | bytes 196
  15.8 184.6 %copy-start.10 = (f32[1,128]{1,0:T(1,128)S(1)}, f32[1,128]{1,0:T(1,128)}, u32[]{:S(2)}) copy-start(f32[1,128]{1,0:T(1,128)} %param.22) | copy-start | bytes 1540
  15.8 184.6 %copy-start.13 = (f32[1,128]{1,0:T(1,128)S(1)}, f32[1,128]{1,0:T(1,128)}, u32[]{:S(2)}) copy-start(f32[1,128]{1,0:T(1,128)} %param.21) | copy-start | bytes 1540
  201.2 293.7 %all-reduce.7.cloned.1.call-start = ((), (), s32[]{:S(2)}) async-start(), calls=%async_computation.1 | async-start | bytes 1048576 | tf_op jit(solution)/shard_map/psum | solution.py:69
  345.0 3.1 copy-start.2
  348.1 2.2 copy-start.11
  521.7 5.2 copy-start.6
  521.7 6.3 %copy-start.7 = (f32[512,128]{1,0:T(8,128)S(1)}, f32[512,128]{1,0:T(8,128)}, u32[]{:S(2)}) copy-start(f32[512,128]{1,0:T(8,128)} %get-tuple-element.91) | copy-start | bytes 786436
  526.9 12.7 %copy-start.14 = (f32[512]{0:T(512)S(1)}, f32[512]{0:T(512)}, u32[]{:S(2)}) copy-start(f32[512]{0:T(512)} %param.19) | copy-start | bytes 6148
  534.6 5.0 copy-start.3
Sparse Core Ops, SparseCore 0:
  201.3 143.6 all-reduce.4
  350.4 144.3 all-reduce.6
where the time goes:
time: 575 us; the launch traced here: 574 us
  waiting for transfers between devices  285 us (50%)
  other arithmetic  177 us (31%)
  matrix products  36.8 us (6%)
  local copies, waits for them, and re-layouts  33.5 us (6%)
  blocking collectives  26.5 us (5%)
  between operations  14.3 us (2%)
    reduce_max x32, other arithmetic, one_block(): jnp.max(jnp.where(flags[None, :, :], piece[:, :, None], -jnp.inf), axis=1)  165 us
    psum x1, waiting for transfers between devices, shards(): total = lax.psum(partial_sum, 'sku')  145 us
    pmax x1, waiting for transfers between devices, shards(): sub_top = lax.pmax(local_top, 'sku')  141 us
    dot_general x8, matrix products, spread(): return jnp.dot(table_values, table_back, precision=lax.Precision.HIGHEST)  20.8 us
    broadcast_in_dim x32, local copies, waits for them, and re-layouts, one_block(): jnp.where(flags[None, :, :], piece[:, :, None], -jnp.inf)  15.9 us
    psum x1, blocking collectives, shards(): grad = lax.psum(local_grad, 'mkt')  11.9 us
  transfers between devices with their start and end apart: 2, of which 2 were waited for; matrix products, arithmetic and copies ran while one was open for 1% of the time, Pallas kernels for 0%

commit v1 on v0

v1 whole, which is shorter than its diff:
```python
import functools

import jax
import jax.numpy as jnp
from jax import lax
from jax.experimental import pallas as pl
from jax.experimental.pallas import tpu as pltpu
from jax.sharding import PartitionSpec as P

F32 = jnp.float32
BF16 = jnp.bfloat16
NEG = -1e30
EMPTY = -1e29
SAFE = 60.0
LANES = 128
CHUNK = 256
MESH = pl.DeviceIdType.MESH
NT = (((1,), (1,)), ((), ()))


def dot(a, b):
    return jnp.dot(a, b, preferred_element_type=F32)


def dot_nt(a, b):
    return lax.dot_general(a, b, NT, preferred_element_type=F32)


def iota(shape, dim):
    return lax.broadcasted_iota(jnp.int32, shape, dim)


def lse2(a, b):
    top = jnp.maximum(a, b)
    return top + jnp.log(1.0 + jnp.exp(jnp.minimum(a, b) - top))


def halves(x):
    high = x.astype(BF16)
    return high, (x - high.astype(F32)).astype(BF16)


def thirds(x):
    high = x.astype(BF16)
    rest = x - high.astype(F32)
    mid = rest.astype(BF16)
    return high, mid, (rest - mid.astype(F32)).astype(BF16)


def column(row):
    n = row.shape[1]
    return jnp.sum(jnp.where(iota((n, n), 0) == iota((n, n), 1), row, 0.0), axis=1, keepdims=True)


def nest_columns(lam_ref, store_ref, rho_ref, par_ref):
    lam = column(lam_ref[...])
    store = column(store_ref[...]) / lam
    par = column(par_ref[...].astype(F32))
    subs, cats = lam_ref.shape[1], rho_ref.shape[1]
    mine = par == iota((subs, cats), 1).astype(F32)
    rho = jnp.sum(jnp.where(mine, rho_ref[...], 0.0), axis=1, keepdims=True)
    return lam, 1.0 / lam, store, par, 1.0 / rho


def local_kernel(
    feat_ref, taste_ref, price_ref, alpha_ref, lam_ref, store_ref, rho_ref, par_ref, avail_ref, mem_ref, cot_ref,
    ms_ref, wh_ref, wl_ref, lst_ref, r_ref, c_ref, part_ref, left_ref, right_ref, own_ref, cg_ref,
    table, inv_ref, cols, acc, cotacc, sums,
):
    step = pl.program_id(0)
    subs = lam_ref.shape[1]
    cats = rho_ref.shape[1]
    width = mem_ref.shape[1]
    tiles = width // LANES

    @pl.when(step == 0)
    def _():
        lam, ilam, store, par, irho = nest_columns(lam_ref, store_ref, rho_ref, par_ref)
        cols[0] = jnp.broadcast_to(lam, (subs, LANES))
        cols[1] = jnp.broadcast_to(store, (subs, LANES))
        cols[2] = jnp.broadcast_to(par, (subs, LANES))
        cols[3] = jnp.broadcast_to(irho, (subs, LANES))
        for k in range(width // CHUNK):
            at = pl.ds(k * CHUNK, CHUNK)
            hit = iota((subs, CHUNK), 0) == mem_ref[:, at]
            table[:, at] = jnp.where(hit, 1.0, 0.0).astype(BF16)
            lam_j = jnp.sum(jnp.where(hit, lam, 0.0), axis=0, keepdims=True)
            inv = 1.0 / lam_j
            inv_ref[0:1, at] = inv
            inv_ref[1:2, at] = inv * price_ref[:, at]
        acc[...] = jnp.zeros_like(acc)

    alpha_row = alpha_ref[...]
    alpha = jnp.transpose(jnp.broadcast_to(alpha_row, (LANES, LANES)))
    alpha2 = jnp.concatenate([alpha, alpha], axis=1)
    ah, al = halves(alpha_row)
    pick = iota((16, LANES), 0)
    alpha_rows = jnp.where(pick == 0, ah.astype(F32), jnp.where(pick == 1, al.astype(F32), 0.0)).astype(BF16)
    feats = feat_ref[...]
    worst = jnp.zeros((8, CHUNK), F32)
    total = jnp.zeros((subs, 2 * LANES), F32)
    cot_total = jnp.zeros((subs, LANES), F32)
    for k in range(width // CHUNK):
        at = pl.ds(k * CHUNK, CHUNK)
        util = dot(feats, taste_ref[:, at])
        scaled = util * inv_ref[0:1, at] - alpha2 * inv_ref[1:2, at]
        open_ = jnp.concatenate(
            [avail_ref[pl.ds(k * (CHUNK // LANES) + t, LANES, stride=tiles), :] for t in range(CHUNK // LANES)], axis=1
        )
        masked = jnp.where(open_ == 1, scaled, NEG)
        ms_ref[:, at] = masked
        worst = jnp.maximum(worst, jnp.max(jnp.abs(scaled).reshape(LANES // 8, 8, CHUNK), axis=0))
        wh, wl = halves(jnp.exp(masked))
        wh_ref[:, at] = wh
        wl_ref[:, at] = wl
        cotm = cot_ref[:, at] * open_.astype(F32).astype(BF16)
        total = total + dot_nt(table[:, at], jnp.concatenate([wh, wl], axis=0))
        cot_total = cot_total + dot_nt(table[:, at], cotm)
        acc[:, at] += dot(alpha_rows, cotm)
    sums[...] = total[:, :LANES] + total[:, LANES:]
    r_ref[...] = jnp.zeros_like(r_ref)

    @pl.when(jnp.max(worst) > SAFE)
    def _():
        lane = iota((1, LANES), 1)
        carry = jnp.full((LANES, 1), NEG, F32)
        carry_id = jnp.full((1, 1), -1, jnp.int32)
        peak = jnp.zeros((LANES, subs), F32)
        for t in range(tiles):
            at = pl.ds(t * LANES, LANES)
            ids = mem_ref[:, at]
            run = ms_ref[:, at]
            shift = 1
            while shift < LANES:
                same = (pltpu.roll(ids, shift, 1) == ids) & (lane >= shift)
                run = jnp.where(same, jnp.maximum(run, pltpu.roll(run, shift, 1)), run)
                shift *= 2
            run = jnp.where(ids == carry_id, jnp.maximum(run, carry), run)
            carry = run[:, LANES - 1 :]
            carry_id = ids[:, LANES - 1 :]
            if t + 1 < tiles:
                following = mem_ref[:, pl.ds((t + 1) * LANES, LANES)][:, 0:1]
            else:
                following = jnp.full((1, 1), -1, jnp.int32)
            nxt = jnp.where(lane == LANES - 1, following, pltpu.roll(ids, LANES - 1, 1))
            ends = jnp.where((iota((subs, LANES), 0) == ids) & (ids != nxt), 1.0, 0.0).astype(BF16)
            peak = peak + dot_nt(run.astype(BF16), ends)
        peak = jnp.where(peak < EMPTY, 0.0, peak)
        r_ref[...] = jnp.transpose(peak)
        peak_half = peak.astype(BF16)
        total = jnp.zeros((subs, 2 * LANES), F32)
        for t in range(tiles):
            at = pl.ds(t * LANES, LANES)
            wh, wl = halves(jnp.exp(ms_ref[:, at] - dot(peak_half, table[:, at])))
            wh_ref[:, at] = wh
            wl_ref[:, at] = wl
            total = total + dot_nt(table[:, at], jnp.concatenate([wh, wl], axis=0))
        sums[...] = total[:, :LANES] + total[:, LANES:]

    total = sums[...]
    raw = jnp.where(total > 0.0, r_ref[...] + jnp.log(jnp.where(total > 0.0, total, 1.0)), NEG)
    lam, store, par, irho = cols[0], cols[1], cols[2], cols[3]
    full = lse2(raw, store)
    lst_ref[...] = full
    c_ref[...] = cot_total
    row = iota((subs, LANES), 0)
    ids = mem_ref[...]
    first, last = ids[:, 0:1], ids[:, width - 1 :]
    is_first, is_last = row == first, row == last
    factor = lam * irho
    ratio = jnp.where((row > first) & (row < last), full * factor, NEG)
    spread = jnp.full((subs, LANES), NEG, F32)
    tops = []
    for c in range(cats):
        hit = par == c
        top = jnp.max(jnp.where(hit, ratio, NEG), axis=0, keepdims=True)
        tops.append(top)
        spread = jnp.where(hit, top, spread)
    terms = jnp.where(ratio > EMPTY, jnp.exp(ratio - spread), 0.0)
    for c in range(cats):
        hit = par == c
        amount = jnp.sum(jnp.where(hit, terms, 0.0), axis=0, keepdims=True)
        part_ref[0, c : c + 1, :] = jnp.where(amount > 0.0, tops[c] + jnp.log(jnp.maximum(amount, 1.0)), NEG)
        part_ref[0, cats + c : cats + c + 1, :] = jnp.sum(jnp.where(hit, cot_total, 0.0), axis=0, keepdims=True)

    def at_row(mask, values):
        return jnp.sum(jnp.where(mask, values, 0.0), axis=0, keepdims=True)

    first_id = jnp.broadcast_to(first.astype(F32), (1, LANES))
    last_id = jnp.broadcast_to(last.astype(F32), (1, LANES))
    blank = jnp.zeros((5, LANES), F32)
    left_ref[0] = jnp.concatenate([at_row(is_first, raw), at_row(is_first, cot_total), first_id, blank], axis=0)
    right_ref[0] = jnp.concatenate([at_row(is_last, raw), at_row(is_last, cot_total), last_id, blank], axis=0)
    own_ref[0] = jnp.concatenate(
        [
            at_row(is_first, store), at_row(is_first, factor), at_row(is_first, par),
            at_row(is_last, store), at_row(is_last, factor), at_row(is_last, par),
            first_id, last_id,
        ],
        axis=0,
    )

    @pl.when(step == pl.num_programs(0) - 1)
    def _():
        cg_ref[...] = jnp.sum(acc[...], axis=0, keepdims=True) * inv_ref[0:1, :]


def merge(logs):
    top = functools.reduce(jnp.maximum, logs)
    return top + jnp.log(sum(jnp.exp(value - top) for value in logs))


def swap_kernel(
    ny, nz, nx, part_ref, left_ref, right_ref, own_ref, rho_ref,
    cv_ref, nbl_ref, nbr_ref,
    pq, ybuf, qbuf, zbuf, xsrc, xbuf, cvs,
    nb_send, nb_recv, y_send, y_recv, z_send, z_recv, x_send, x_recv, g_send, g_recv,
):
    cats = rho_ref.shape[1]
    sku = lax.axis_index("sku")
    cat = lax.axis_index("cat")
    y, z = sku // nz, sku % nz
    n = ny * nz
    to_right, to_left = (sku + 1) % n, (sku + n - 1) % n
    along_y = [((y + k) % ny) * nz + z for k in range(1, ny)]
    along_z = [y * nz + (z + k) % nz for k in range(1, nz)]
    along_x = [(cat + k) % nx for k in range(1, nx)]

    barrier = pltpu.get_barrier_semaphore()
    for other in [to_right, to_left] + along_y + along_z:
        pl.semaphore_signal(barrier, inc=1, device_id={"sku": other}, device_id_type=MESH)
    for other in along_x:
        pl.semaphore_signal(barrier, inc=1, device_id={"cat": other}, device_id_type=MESH)
    pl.semaphore_wait(barrier, 2 + len(along_y) + len(along_z) + len(along_x))

    def send(src, dst, send_sem, recv_sem, device):
        copy = pltpu.make_async_remote_copy(
            src_ref=src, dst_ref=dst, send_sem=send_sem, recv_sem=recv_sem, device_id=device, device_id_type=MESH
        )
        copy.start()
        return copy

    rounds = [
        send(right_ref, nbl_ref, nb_send.at[0], nb_recv.at[0], {"sku": to_right}),
        send(left_ref, nbr_ref, nb_send.at[1], nb_recv.at[1], {"sku": to_left}),
    ]
    for copy in rounds:
        copy.wait_recv()
    own = own_ref[...]
    from_left, from_right = nbl_ref[...], nbr_ref[...]
    first_id, last_id = own[:, 6:7], own[:, 7:8]
    first = left_ref[:, 0:1, :]
    first = jnp.where(from_left[:, 2:3] == first_id, lse2(first, from_left[:, 0:1]), first)
    first = lse2(first, own[:, 0:1]) * own[:, 1:2]
    last = lse2(right_ref[:, 0:1, :], own[:, 3:4]) * own[:, 4:5]
    last = jnp.where((from_right[:, 2:3] == last_id) | (first_id == last_id), NEG, last)
    which = iota((ny, cats, LANES), 1).astype(F32)
    pq[:, 0:cats, :] = merge(
        [
            part_ref[:, 0:cats, :],
            jnp.where(which == own[:, 2:3], first, NEG),
            jnp.where(which == own[:, 5:6], last, NEG),
        ]
    )
    pq[:, cats:, :] = part_ref[:, cats:, :]

    copies = []
    for k in range(1, ny):
        copies.append(send(pq.at[(y + k) % ny], ybuf.at[k], y_send.at[k], y_recv.at[k], {"sku": along_y[k - 1]}))
    for copy in copies:
        copy.wait_recv()
    rounds += copies
    pieces = [pq[y]] + [ybuf[k] for k in range(1, ny)]
    qbuf[0:cats, :] = merge([piece[0:cats] for piece in pieces])
    qbuf[cats:, :] = sum(piece[cats:] for piece in pieces)

    copies = []
    for k in range(1, nz):
        copies.append(send(qbuf, zbuf.at[k], z_send.at[k], z_recv.at[k], {"sku": along_z[k - 1]}))
    for copy in copies:
        copy.wait_recv()
    rounds += copies
    pieces = [qbuf[...]] + [zbuf[k] for k in range(1, nz)]
    rho = column(rho_ref[...])
    value = rho * merge([piece[0:cats] for piece in pieces])
    cat_cot = sum(piece[cats:] for piece in pieces)
    top = jnp.max(value, axis=0, keepdims=True)
    group = top + jnp.log(jnp.sum(jnp.exp(value - top), axis=0, keepdims=True))
    xsrc[...] = jnp.concatenate(
        [group, jnp.sum(cat_cot, axis=0, keepdims=True), jnp.zeros((6, LANES), F32)], axis=0
    )

    copies = []
    for k in range(1, nx):
        copies.append(send(xsrc, xbuf.at[k], x_send.at[k], x_recv.at[k], {"cat": along_x[k - 1]}))
    for copy in copies:
        copy.wait_recv()
    rounds += copies
    pieces = [xsrc[...]] + [xbuf[k] for k in range(1, nx)]
    inclusive = merge([jnp.zeros((1, LANES), F32)] + [piece[0:1] for piece in pieces])
    all_cot = sum(piece[1:2] for piece in pieces)
    cvs[0:cats, :] = value
    cvs[cats : 2 * cats, :] = (1.0 - 1.0 / rho) * cat_cot - all_cot * jnp.exp(value - inclusive)
    cvs[2 * cats :, :] = jnp.broadcast_to(inclusive, (8, LANES))
    cv_ref[y] = cvs[...]

    copies = []
    for k in range(1, ny):
        copies.append(send(cvs, cv_ref.at[y], g_send.at[k], g_recv.at[k], {"sku": along_y[k - 1]}))
    for k, copy in enumerate(copies):
        copy.wait_recv()
    rounds += copies
    for copy in rounds:
        copy.wait_send()


def slope_kernel(
    wh_ref, wl_ref, lst_ref, r_ref, c_ref, cv_ref, nbl_ref, nbr_ref, own_ref, cg_ref, mem_ref, alpha_ref, size_ref,
    lam_ref, store_ref, rho_ref, par_ref,
    grad_ref, path_ref,
    hs,
):
    subs, cats = lam_ref.shape[1], rho_ref.shape[1]
    blocks = cv_ref.shape[0]
    width = mem_ref.shape[1]
    lam, ilam, _, par, irho = nest_columns(lam_ref, store_ref, rho_ref, par_ref)
    parents = jnp.where((iota((subs, 3 * cats), 1) % cats).astype(F32) == par, 1.0, 0.0).astype(BF16)
    row = iota((subs, LANES), 0).astype(F32)
    for b in range(blocks):
        at = pl.ds(b * LANES, LANES)
        own, from_left, from_right = own_ref[b], nbl_ref[b], nbr_ref[b]
        cv = cv_ref[b]
        left_hit = (row == own[6:7]) & (from_left[2:3] == own[6:7])
        right_hit = (row == own[7:8]) & (from_right[2:3] == own[7:8])
        extra = jnp.where(left_hit, from_left[0:1], jnp.where(right_hit, from_right[0:1], NEG))
        level = lse2(lst_ref[:, at], extra)
        sub_cot = c_ref[:, at] + jnp.where(left_hit, from_left[1:2], jnp.where(right_hit, from_right[1:2], 0.0))
        cat_value = dot(parents, jnp.concatenate(thirds(cv[0:cats]), axis=0))
        d_cat = dot(parents, jnp.concatenate(thirds(cv[cats : 2 * cats]), axis=0))
        inclusive = cv[2 * cats : 2 * cats + 1]
        log_sub = (lam * level - cat_value) * irho
        path = jnp.log(size_ref[:, at]) - level + log_sub + (cat_value - inclusive)
        d_sub = (irho - ilam) * sub_cot + jnp.exp(log_sub) * d_cat
        slope = alpha_ref[:, at] * jnp.exp(r_ref[:, at] - level) * d_sub
        hs[0:subs, at], hs[subs:, at] = halves(slope)
        ph, plo = halves(jnp.transpose(path))
        path_ref[at, 0:subs] = ph
        path_ref[at, subs:] = plo
    for k in range(width // CHUNK):
        at = pl.ds(k * CHUNK, CHUNK)
        both = dot(hs[...], wh_ref[:, at])
        found = both[0:subs] + both[subs:] + dot(hs[0:subs, :], wl_ref[:, at])
        hit = iota((subs, CHUNK), 0) == mem_ref[:, at]
        grad_ref[:, at] = -(jnp.sum(jnp.where(hit, found, 0.0), axis=0, keepdims=True) + cg_ref[:, at])


def demand_kernel(ms_ref, path_ref, mem_ref, out_ref, table):
    width = mem_ref.shape[1]
    depth = path_ref.shape[1]
    tiles = width // LANES
    step = pl.program_id(0)

    @pl.when(step == 0)
    def _():
        for k in range(width // CHUNK):
            at = pl.ds(k * CHUNK, CHUNK)
            hit = iota((depth, CHUNK), 0) % (depth // 2) == mem_ref[:, at]
            table[:, at] = jnp.where(hit, 1.0, 0.0).astype(BF16)

    rows = pl.ds(pl.multiple_of(step * LANES, LANES), LANES)
    path = path_ref[rows, :]
    for k in range(width // CHUNK):
        at = pl.ds(k * CHUNK, CHUNK)
        masked = ms_ref[rows, at]
        value = jnp.where(masked > EMPTY, masked + dot(path, table[:, at]), 0.0)
        for t in range(CHUNK // LANES):
            out_ref[pl.ds(k * (CHUNK // LANES) + t, LANES, stride=tiles), :] = value[:, t * LANES : (t + 1) * LANES]


def whole(shape=None):
    return pl.BlockSpec(memory_space=pltpu.VMEM)


def shards(
    n_sku, n_cat, features, taste, price, alpha, market_size, store_brand, sub_scale, cat_scale, availability,
    sku_subcat, subcat_cat, cotangent,
):
    markets, depth = features.shape
    width = price.shape[1]
    subs, cats = sub_scale.shape[1], cat_scale.shape[1]
    tiles = width // LANES
    blocks = markets // LANES
    ny, nz = blocks, n_sku // blocks
    alpha_row = alpha.reshape(1, markets)
    size_row = market_size.reshape(1, markets)
    avail = availability.reshape(markets * tiles, LANES)
    taste2 = taste.reshape(depth, width)
    cot2 = cotangent.reshape(markets, width)

    def fixed(shape):
        return pl.BlockSpec(shape, lambda i: (0,) * len(shape))

    row_block = pl.BlockSpec((LANES, width), lambda i: (i, 0))
    col_block = pl.BlockSpec((subs, LANES), lambda i: (0, i))
    tile_block = pl.BlockSpec((1, 8, LANES), lambda i: (i, 0, 0))
    sds = jax.ShapeDtypeStruct
    ms, wh, wl, lst, r, c, part, left, right, own, cg = pl.pallas_call(
        local_kernel,
        grid=(blocks,),
        in_specs=[
            pl.BlockSpec((LANES, depth), lambda i: (i, 0)),
            fixed((depth, width)),
            fixed((1, width)),
            pl.BlockSpec((1, LANES), lambda i: (0, i)),
            fixed((1, subs)),
            fixed((1, subs)),
            fixed((1, cats)),
            fixed((1, subs)),
            pl.BlockSpec((LANES * tiles, LANES), lambda i: (i, 0)),
            fixed((1, width)),
            row_block,
        ],
        out_shape=[
            sds((markets, width), F32),
            sds((markets, width), BF16),
            sds((markets, width), BF16),
            sds((subs, markets), F32),
            sds((subs, markets), F32),
            sds((subs, markets), F32),
            sds((blocks, 2 * cats, LANES), F32),
            sds((blocks, 8, LANES), F32),
            sds((blocks, 8, LANES), F32),
            sds((blocks, 8, LANES), F32),
            sds((1, width), F32),
        ],
        out_specs=[
            row_block, row_block, row_block, col_block, col_block, col_block,
            pl.BlockSpec((1, 2 * cats, LANES), lambda i: (i, 0, 0)),
            tile_block, tile_block, tile_block, fixed((1, width)),
        ],
        scratch_shapes=[
            pltpu.VMEM((subs, width), BF16),
            pltpu.VMEM((8, width), F32),
            pltpu.VMEM((4, subs, LANES), F32),
            pltpu.VMEM((16, width), F32),
            pltpu.VMEM((8, LANES), F32),
            pltpu.VMEM((subs, LANES), F32),
        ],
        compiler_params=pltpu.CompilerParams(vmem_limit_bytes=28 * 1024 * 1024),
        name="local_nests",
    )(
        features, taste2, price, alpha_row, sub_scale, store_brand, cat_scale, subcat_cat, avail, sku_subcat, cot2
    )

    cv, nbl, nbr = pl.pallas_call(
        functools.partial(swap_kernel, ny, nz, n_cat),
        in_specs=[whole()] * 5,
        out_specs=[whole()] * 3,
        out_shape=[
            sds((ny, 2 * cats + 8, LANES), F32),
            sds((ny, 8, LANES), F32),
            sds((ny, 8, LANES), F32),
        ],
        scratch_shapes=[
            pltpu.VMEM((ny, 2 * cats, LANES), F32),
            pltpu.VMEM((ny, 2 * cats, LANES), F32),
            pltpu.VMEM((2 * cats, LANES), F32),
            pltpu.VMEM((nz, 2 * cats, LANES), F32),
            pltpu.VMEM((8, LANES), F32),
            pltpu.VMEM((n_cat, 8, LANES), F32),
            pltpu.VMEM((2 * cats + 8, LANES), F32),
        ]
        + [pltpu.SemaphoreType.DMA((count,)) for count in (2, ny, nz, n_cat, ny) for _ in range(2)],
        compiler_params=pltpu.CompilerParams(
            collective_id=0, has_side_effects=True, vmem_limit_bytes=8 * 1024 * 1024
        ),
        name="swap_nests",
    )(part, left, right, own, cat_scale)

    grad, path = pl.pallas_call(
        slope_kernel,
        in_specs=[whole()] * 17,
        out_specs=[whole()] * 2,
        out_shape=[sds((1, width), F32), sds((markets, 2 * subs), BF16)],
        scratch_shapes=[pltpu.VMEM((2 * subs, markets), BF16)],
        compiler_params=pltpu.CompilerParams(vmem_limit_bytes=16 * 1024 * 1024),
        name="price_slope",
    )(
        wh, wl, lst, r, c, cv, nbl, nbr, own, cg, sku_subcat, alpha_row, size_row, sub_scale, store_brand, cat_scale,
        subcat_cat,
    )
    other = lax.ppermute(grad, "mkt", [(0, 1), (1, 0)])

    demand = pl.pallas_call(
        demand_kernel,
        grid=(blocks,),
        in_specs=[whole(), whole(), whole()],
        out_specs=pl.BlockSpec((LANES * tiles, LANES), lambda i: (i, 0)),
        out_shape=sds((markets * tiles, LANES), F32),
        scratch_shapes=[pltpu.VMEM((2 * subs, width), BF16)],
        compiler_params=pltpu.CompilerParams(vmem_limit_bytes=16 * 1024 * 1024),
        cost_estimate=pl.CostEstimate(
            flops=2 * markets * width * 2 * subs, bytes_accessed=8 * markets * width, transcendentals=0
        ),
        name="log_demand",
    )(ms, path, sku_subcat)
    return demand.reshape(markets, 1, width), grad + other


def solution(mesh):
    return jax.shard_map(
        functools.partial(shards, mesh.shape["sku"], mesh.shape["cat"]),
        mesh=mesh,
        in_specs=(
            P("mkt", None),
            P(None, "cat", "sku"),
            P("cat", "sku"),
            P("mkt"),
            P("mkt"),
            P("cat", None),
            P("cat", None),
            P("cat", None),
            P("mkt", "cat", "sku"),
            P("cat", "sku"),
            P("cat", None),
            P("mkt", "cat", "sku"),
        ),
        out_specs=(P("mkt", "cat", "sku"), P("cat", "sku")),
        check_vma=False,
    )
```

time: 575 us -> 61.6 us (0.11)
  waiting for transfers between devices: 285 us -> 0.01 us
  other arithmetic: 177 us -> 0.61 us
  Pallas kernels: 0 us -> 40.5 us
  matrix products: 36.8 us -> 0 us
  blocking collectives: 26.5 us -> 0 us
  local copies, waits for them, and re-layouts: 33.5 us -> 11.1 us
  between operations: 14.3 us -> 0.69 us
  starting transfers between devices: 0.08 us -> 8.36 us
    reduce_max x32 -> x0, other arithmetic: 165 us -> none  [one_block(): jnp.max(jnp.where(flags[None, :, :], piece[:, :, None], -jnp.inf), axis=1)]
    psum x1 -> x0, waiting for transfers between devices: 145 us -> none  [shards(): total = lax.psum(partial_sum, 'sku')]
    pmax x1 -> x0, waiting for transfers between devices: 141 us -> none  [shards(): sub_top = lax.pmax(local_top, 'sku')]
    pallas_call x0 -> x4, Pallas kernels: none -> 40.5 us  [the longest x1 26.2 us: shards(): pl.pallas_call(functools.partial(swap_kernel, ny, nz, n_cat), in_specs=[w...]
    dot_general x16 -> x0, matrix products: 36.8 us -> none  [the longest x8 20.8 us: spread(): return jnp.dot(table_values, table_back, precision=lax.Precision.HIGHEST)]
    psum x2 -> x0, blocking collectives: 18.1 us -> none  [the longest x1 11.9 us: shards(): grad = lax.psum(local_grad, 'mkt')]
    broadcast_in_dim x32 -> x0, local copies, waits for them, and re-layouts: 15.9 us -> none  [one_block(): jnp.where(flags[None, :, :], piece[:, :, None], -jnp.inf)]
    dynamic_update_slice x32 -> x0, local copies, waits for them, and re-layouts: 9.83 us -> none  [segment_peak(): peaks = lax.map(one_block, grouped)]
  transfers between devices with their start and end apart: 2 -> 1, of which waited for: 2 -> 0; matrix products, arithmetic and copies ran while one was open for 1% -> 0% of each run, Pallas kernels for 0% -> 6%
where the time goes in v1:
time: 61.6 us; the launch traced here: 61.3 us
  Pallas kernels  40.5 us (66%)
  local copies, waits for them, and re-layouts  11.1 us (18%)
  starting transfers between devices  8.36 us (14%)
  between operations  0.69 us (1%)
    pallas_call x1, Pallas kernels, shards(): pl.pallas_call(functools.partial(swap_kernel, ny, nz, n_cat), in_specs=[w...  26.2 us
    unnamed x24, local copies, waits for them, and re-layouts  11.1 us
    pallas_call x1, Pallas kernels, shards(): pl.pallas_call(local_kernel, grid=(blocks,), in_specs=[pl.BlockSpec((LANE...  9.03 us
    ppermute x1, starting transfers between devices, shards(): other = lax.ppermute(grad, 'mkt', [(0, 1), (1, 0)])  8.36 us
    pallas_call x1, Pallas kernels, shards(): pl.pallas_call(demand_kernel, grid=(blocks,), in_specs=[whole(), whole(),...  3.8 us
    pallas_call x1, Pallas kernels, shards(): pl.pallas_call(slope_kernel, in_specs=[whole()] * 17, out_specs=[whole()]...  1.48 us
  transfers between devices with their start and end apart: 1, of which 0 were waited for; matrix products, arithmetic and copies ran while one was open for 0% of the time, Pallas kernels for 6%

profile of v1, /device:TPU:1, one launch (start us, length us, event | category | flops | bytes accessed | tf_op | source)
XLA Modules:
  0.0 61.3 jit_solution(14946251426453104975)
XLA Ops:
  0.6 0.0 copy-start
  0.6 2.2 %copy-done = s32[512,1,2048]{2,1,0:T(1,128)S(1)} copy-done((s32[512,1,2048]{2,1,0:T(1,128)S(1)}, s32[512,1,2048]{2,1,0:T(1,128)}, u32[]{:S(2)}) %copy-start) | copy-done | bytes 4194328
  2.8 0.0 copy-start.1
  2.8 1.6 %copy-done.1 = bf16[512,1,2048]{2,0,1:T(8,128)(2,1)S(1)} copy-done((bf16[512,1,2048]{2,0,1:T(8,128)(2,1)S(1)}, bf16[512,1,2048]{2,0,1:T(8,128)(2,1)}, u32[]{:S(2)}) %copy-start.1) | copy-done | bytes 2097176
  4.4 0.0 copy-start.2
  4.4 1.6 %copy-done.2 = bf16[512,1,2048]{2,0,1:T(8,128)(2,1)S(1)} copy-done((bf16[512,1,2048]{2,0,1:T(8,128)(2,1)S(1)}, bf16[512,1,2048]{2,0,1:T(8,128)(2,1)}, u32[]{:S(2)}) %copy-start.2) | copy-done | bytes 2097176
  6.0 0.0 copy-start.3
  6.0 1.0 %copy-done.3 = bf16[512,512]{1,0:T(8,128)(2,1)S(1)} copy-done((bf16[512,512]{1,0:T(8,128)(2,1)S(1)}, bf16[512,512]{1,0:T(8,128)(2,1)}, u32[]{:S(2)}) %copy-start.3) | copy-done | bytes 524312
  7.0 0.0 copy-start.4
  7.1 0.7 %copy-done.4 = s32[1,2048]{1,0:T(1,128)S(1)} copy-done((s32[1,2048]{1,0:T(1,128)S(1)}, s32[1,2048]{1,0:T(1,128)}, u32[]{:S(2)}) %copy-start.4) | copy-done | bytes 8216
  7.7 0.0 copy-start.5
  7.7 0.7 %copy-done.5 = f32[1,2048]{1,0:T(1,128)S(1)} copy-done((f32[1,2048]{1,0:T(1,128)S(1)}, f32[1,2048]{1,0:T(1,128)}, u32[]{:S(2)}) %copy-start.5) | copy-done | bytes 8216
  8.4 0.0 copy-start.6
  8.4 0.7 %copy-done.6 = f32[512]{0:T(512)S(1)} copy-done((f32[512]{0:T(512)S(1)}, f32[512]{0:T(512)}, u32[]{:S(2)}) %copy-start.6) | copy-done | bytes 2072
  9.1 0.0 copy-start.7
  9.1 0.7 %copy-done.7 = f32[1,16]{1,0:T(1,128)S(1)} copy-done((f32[1,16]{1,0:T(1,128)S(1)}, f32[1,16]{1,0:T(1,128)}, u32[]{:S(2)}) %copy-start.7) | copy-done | bytes 88
  9.8 0.0 copy-start.9
  9.8 0.7 %copy-done.9 = f32[1,128]{1,0:T(1,128)S(1)} copy-done((f32[1,128]{1,0:T(1,128)S(1)}, f32[1,128]{1,0:T(1,128)}, u32[]{:S(2)}) %copy-start.9) | copy-done | bytes 536
  10.4 0.0 copy-start.10
  10.4 0.7 %copy-done.10 = f32[1,128]{1,0:T(1,128)S(1)} copy-done((f32[1,128]{1,0:T(1,128)S(1)}, f32[1,128]{1,0:T(1,128)}, u32[]{:S(2)}) %copy-start.10) | copy-done | bytes 536
  11.1 0.0 copy-start.11
  11.1 0.7 %copy-done.11 = s32[1,128]{1,0:T(1,128)S(1)} copy-done((s32[1,128]{1,0:T(1,128)S(1)}, s32[1,128]{1,0:T(1,128)}, u32[]{:S(2)}) %copy-start.11) | copy-done | bytes 536
  11.7 0.0 copy-start.8
  11.8 9.0 %local_nests.1 = (f32[512,2048]{1,0:T(8,128)S(1)}, bf16[512,2048]{1,0:T(8,128)(2,1)S(1)}, bf16[512,2048]{1,0:T(8,128)(2,1)S(1)}, f32[128,512]{1,0:T(8,128)S(1)},...) custom-call(bf16[512,512]{1,0:T(8,128)(2,1)S(1)} %copy-done.3, ...), custom_call_target="tpu_custom_call" | custom-call | tf_op jit(solution)/shard_map/local_nests/pallas_call | solution.py:407
  20.8 26.2 %swap_nests.1 = (f32[4,40,128]{2,1,0:T(8,128)S(1)}, f32[4,8,128]{2,1,0:T(8,128)S(1)}, f32[4,8,128]{2,1,0:T(8,128)S(1)}) custom-call(f32[4,32,128]{2,1,0:T(8,128)S(1)} %get-tuple-element.24.part_ref, f32[4,8,128]{2,1,0:T(8,128)S(1)} %get-tuple-element.25.left_ref, f32[4,8,128]{2,1,0:T(8,128)S(1)} %get-tuple-element.26.right_ref, ...), custom_call_target="tpu_custom_call" | custom-call | tf_op jit(solution)/shard_map/swap_nests/pallas_call | solution.py:455
  47.0 0.0 copy-done.8
  47.0 1.5 %price_slope.1 = (f32[1,2048]{1,0:T(1,128)S(1)}, bf16[512,256]{1,0:T(8,128)(2,1)S(1)}) custom-call(bf16[512,2048]{1,0:T(8,128)(2,1)S(1)} %get-tuple-element.19.wh_ref, bf16[512,2048]{1,0:T(8,128)(2,1)S(1)} %get-tuple-element.20.wl_ref, f32[128,512]{1,0:T(8,128)S(1)} %get-tuple-element.21.lst_ref, f32[128,512]{1,0:T(8,128)S(1)} %get-tuple-element.22.r_ref, ...), custom_call_target="tpu_custom_call" | custom-call | tf_op jit(solution)/shard_map/price_slope/pallas_call | solution.py:480
  48.5 8.4 %collective-permute-start = (f32[1,2048]{1,0:T(1,128)S(1)}, f32[1,2048]{1,0:T(1,128)S(1)}, u32[]{:S(2)}, u32[]{:S(2)}) collective-permute-start(f32[1,2048]{1,0:T(1,128)S(1)} %get-tuple-element.33), channel_id=1, source_target_pairs={{0,128},{128,0},{1,129},{129,1},{2,130},{130,2},{3,131},{131,3},{4... | collective-permute-start | bytes 24584 | tf_op jit(solution)/shard_map/ppermute | solution.py:492
  56.8 3.8 %log_demand.1 = f32[8192,128]{1,0:T(8,128)} custom-call(f32[512,2048]{1,0:T(8,128)S(1)} %get-tuple-element.18.ms_ref, bf16[512,256]{1,0:T(8,128)(2,1)S(1)} %get-tuple-element.32.path_ref, s32[1,2048]{1,0:T(1,128)S(1)} %copy-done.4), custom_call_target="tpu_custom_call" | custom-call | flops 536870912 | bytes 8388608 | tf_op jit(solution)/shard_map/log_demand/pallas_call | solution.py:494
  60.6 0.0 collective-permute-done
  60.6 0.6 add.3
Async XLA Ops:
  0.6 2.2 %copy-start = (s32[512,1,2048]{2,1,0:T(1,128)S(1)}, s32[512,1,2048]{2,1,0:T(1,128)}, u32[]{:S(2)}) copy-start(s32[512,1,2048]{2,1,0:T(1,128)} %param.20) | copy-start | bytes 12582916
  2.8 1.6 %copy-start.1 = (bf16[512,1,2048]{2,0,1:T(8,128)(2,1)S(1)}, bf16[512,1,2048]{2,0,1:T(8,128)(2,1)}, u32[]{:S(2)}) copy-start(bf16[512,1,2048]{2,0,1:T(8,128)(2,1)} %param.13) | copy-start | bytes 6291460
  4.4 1.6 %copy-start.2 = (bf16[512,1,2048]{2,0,1:T(8,128)(2,1)S(1)}, bf16[512,1,2048]{2,0,1:T(8,128)(2,1)}, u32[]{:S(2)}) copy-start(bf16[512,1,2048]{2,0,1:T(8,128)(2,1)} %param.23) | copy-start | bytes 6291460
  6.0 1.0 %copy-start.3 = (bf16[512,512]{1,0:T(8,128)(2,1)S(1)}, bf16[512,512]{1,0:T(8,128)(2,1)}, u32[]{:S(2)}) copy-start(bf16[512,512]{1,0:T(8,128)(2,1)} %feat_ref.1) | copy-start | bytes 1572868
  7.0 0.7 %copy-start.4 = (s32[1,2048]{1,0:T(1,128)S(1)}, s32[1,2048]{1,0:T(1,128)}, u32[]{:S(2)}) copy-start(s32[1,2048]{1,0:T(1,128)} %mem_ref.5) | copy-start | bytes 24580
  7.7 0.7 %copy-start.5 = (f32[1,2048]{1,0:T(1,128)S(1)}, f32[1,2048]{1,0:T(1,128)}, u32[]{:S(2)}) copy-start(f32[1,2048]{1,0:T(1,128)} %price_ref.1) | copy-start | bytes 24580
  8.4 0.7 %copy-start.6 = (f32[512]{0:T(512)S(1)}, f32[512]{0:T(512)}, u32[]{:S(2)}) copy-start(f32[512]{0:T(512)} %param.15) | copy-start | bytes 6148
  9.1 0.7 %copy-start.7 = (f32[1,16]{1,0:T(1,128)S(1)}, f32[1,16]{1,0:T(1,128)}, u32[]{:S(2)}) copy-start(f32[1,16]{1,0:T(1,128)} %rho_ref.5) | copy-start | bytes 196
  9.8 0.7 %copy-start.9 = (f32[1,128]{1,0:T(1,128)S(1)}, f32[1,128]{1,0:T(1,128)}, u32[]{:S(2)}) copy-start(f32[1,128]{1,0:T(1,128)} %lam_ref.3) | copy-start | bytes 1540
  10.4 0.7 %copy-start.10 = (f32[1,128]{1,0:T(1,128)S(1)}, f32[1,128]{1,0:T(1,128)}, u32[]{:S(2)}) copy-start(f32[1,128]{1,0:T(1,128)} %store_ref.3) | copy-start | bytes 1540
  11.1 0.7 %copy-start.11 = (s32[1,128]{1,0:T(1,128)S(1)}, s32[1,128]{1,0:T(1,128)}, u32[]{:S(2)}) copy-start(s32[1,128]{1,0:T(1,128)} %par_ref.3) | copy-start | bytes 1540
  11.7 35.2 %copy-start.8 = (f32[512]{0:T(512)S(1)}, f32[512]{0:T(512)}, u32[]{:S(2)}) copy-start(f32[512]{0:T(512)} %param.16) | copy-start | bytes 6148
  48.5 12.2 %collective-permute-start = (f32[1,2048]{1,0:T(1,128)S(1)}, f32[1,2048]{1,0:T(1,128)S(1)}, u32[]{:S(2)}, u32[]{:S(2)}) collective-permute-start(f32[1,2048]{1,0:T(1,128)S(1)} %get-tuple-element.33), channel_id=1, source_target_pairs={{0,128},{128,0},{1,129},{129,1},{2,130},{130,2},{3,131},{131,3},{4... | collective-permute-start | bytes 24584 | tf_op jit(solution)/shard_map/ppermute | solution.py:492

commit v2 on v0

v2 whole, which is shorter than its diff:
```python
import functools

import jax
import jax.numpy as jnp
from jax import lax
from jax.experimental import pallas as pl
from jax.experimental.pallas import tpu as pltpu
from jax.sharding import PartitionSpec as P

F32 = jnp.float32
BF16 = jnp.bfloat16
NEG = -1e30
EMPTY = -1e29
SAFE = 60.0
LANES = 128
CHUNK = 256
MESH = pl.DeviceIdType.MESH
NT = (((1,), (1,)), ((), ()))


def dot(a, b):
    return jnp.dot(a, b, preferred_element_type=F32)


def dot_nt(a, b):
    return lax.dot_general(a, b, NT, preferred_element_type=F32)


def iota(shape, dim):
    return lax.broadcasted_iota(jnp.int32, shape, dim)


def lse2(a, b):
    top = jnp.maximum(a, b)
    return top + jnp.log(1.0 + jnp.exp(jnp.minimum(a, b) - top))


def halves(x):
    high = x.astype(BF16)
    return high, (x - high.astype(F32)).astype(BF16)


def thirds(x):
    high = x.astype(BF16)
    rest = x - high.astype(F32)
    mid = rest.astype(BF16)
    return high, mid, (rest - mid.astype(F32)).astype(BF16)


def column(row):
    n = row.shape[1]
    return jnp.sum(jnp.where(iota((n, n), 0) == iota((n, n), 1), row, 0.0), axis=1, keepdims=True)


def nest_columns(lam_ref, store_ref, rho_ref, par_ref):
    lam = column(lam_ref[...])
    store = column(store_ref[...]) / lam
    par = column(par_ref[...].astype(F32))
    subs, cats = lam_ref.shape[1], rho_ref.shape[1]
    mine = par == iota((subs, cats), 1).astype(F32)
    rho = jnp.sum(jnp.where(mine, rho_ref[...], 0.0), axis=1, keepdims=True)
    return lam, 1.0 / lam, store, par, 1.0 / rho


def pack(low, high):
    left = iota(low.shape, 1) < LANES // 2
    return jnp.where(left, low, turn(high)), jnp.where(left, turn(low), high)


def turn(x):
    return pltpu.roll(x, LANES // 2, 1)


def local_kernel(
    feat_hbm, taste_hbm, price_hbm, alpha_hbm, size_hbm, lam_hbm, store_hbm, rho_hbm, par_hbm, avail_hbm, mem_hbm,
    cot_hbm,
    ms_ref, wh_ref, wl_ref, cotm_ref, sums, peaks, table, table_t, cols, rows_ref, rho_rows, ids_ref, inv_ref,
    feat, taste, price, lam_row, store_row, rho_row, par_row, avail, size, worst,
    small_sem, big_sem, avail_sem, cot_sem,
):
    subs = lam_row.shape[1]
    cats = rho_row.shape[1]
    width = ids_ref.shape[1]
    blocks = ms_ref.shape[0] // LANES
    tiles = width // LANES
    small = [
        (mem_hbm, ids_ref), (lam_hbm, lam_row), (price_hbm, price), (store_hbm, store_row), (rho_hbm, rho_row),
        (par_hbm, par_row), (alpha_hbm, rows_ref.at[0:1]), (size_hbm, size),
    ]
    small = [pltpu.make_async_copy(src, dst, small_sem.at[k]) for k, (src, dst) in enumerate(small)]
    big = [
        pltpu.make_async_copy(src, dst, big_sem.at[k])
        for k, (src, dst) in enumerate([(feat_hbm, feat), (taste_hbm, taste)])
    ]

    def fetch(b):
        rows = pl.ds(pl.multiple_of(b * LANES, LANES), LANES)
        return (
            pltpu.make_async_copy(avail_hbm.at[rows, 0, :], avail.at[rows], avail_sem.at[b]),
            pltpu.make_async_copy(cot_hbm.at[rows], cotm_ref.at[rows], cot_sem.at[b]),
        )

    for copy in small + big:
        copy.start()
    for b in range(blocks):
        for copy in fetch(b):
            copy.start()
    for copy in small:
        copy.wait()

    lam = column(lam_row[...])
    for k in range(width // CHUNK):
        at = pl.ds(k * CHUNK, CHUNK)
        hit = iota((subs, CHUNK), 0) == ids_ref[:, at]
        ones = jnp.where(hit, 1.0, 0.0)
        table[:, at] = ones.astype(BF16)
        table_t[at, :] = jnp.transpose(ones).astype(BF16)
        inv = 1.0 / jnp.sum(jnp.where(hit, lam, 0.0), axis=0, keepdims=True)
        inv_ref[0:1, at] = inv
        inv_ref[1:2, at] = inv * price[:, at]
    _, ilam, store, par, irho = nest_columns(lam_row, store_row, rho_row, par_row)
    for k, col in enumerate((lam, store, par, irho, ilam)):
        cols[k] = jnp.broadcast_to(col, (subs, LANES))
    rho = jnp.broadcast_to(column(rho_row[...]), (cats, LANES))
    rho_rows[0:8, :] = jnp.where(iota((8, LANES), 1) < LANES // 2, rho[0:8], rho[8:16])
    rho_rows[8:24, :] = rho
    rows_ref[1:2, :] = jnp.log(size[...])
    worst[...] = jnp.zeros_like(worst)
    peaks[...] = jnp.zeros_like(peaks)
    for copy in big:
        copy.wait()

    @pl.loop(0, blocks)
    def _(b):
        mine = pl.ds(pl.multiple_of(b * LANES, LANES), LANES)
        for copy in fetch(b):
            copy.wait()
        alpha = jnp.transpose(jnp.broadcast_to(rows_ref[0:1, mine], (LANES, LANES)))
        alpha2 = jnp.concatenate([alpha, alpha], axis=1)
        total = jnp.zeros((2 * LANES, subs), F32)
        most = jnp.zeros((8, CHUNK), F32)
        for k in range(width // CHUNK):
            at = pl.ds(k * CHUNK, CHUNK)
            util = dot(feat[mine, :], taste[:, at])
            scaled = util * inv_ref[0:1, at] - alpha2 * inv_ref[1:2, at]
            open_ = avail[mine, at]
            masked = jnp.where(open_ == 1, scaled, NEG)
            ms_ref[mine, at] = masked
            most = jnp.maximum(most, jnp.max(jnp.abs(scaled).reshape(LANES // 8, 8, CHUNK), axis=0))
            wh, wl = halves(jnp.exp(masked))
            wh_ref[mine, at] = wh
            wl_ref[mine, at] = wl
            cotm_ref[mine, at] = cotm_ref[mine, at] * open_.astype(F32).astype(BF16)
            total = total + dot(jnp.concatenate([wh, wl], axis=0), table_t[at, :])
        sums[:, mine] = jnp.transpose(total[:LANES] + total[LANES:])
        worst[...] = jnp.maximum(worst[...], most)

    @pl.when(jnp.max(worst[...]) > SAFE)
    def _():
        lane = iota((1, LANES), 1)

        @pl.loop(0, blocks)
        def _(b):
            mine = pl.ds(pl.multiple_of(b * LANES, LANES), LANES)
            carry = jnp.full((LANES, 1), NEG, F32)
            carry_id = jnp.full((1, 1), -1, jnp.int32)
            peak = jnp.zeros((LANES, subs), F32)
            for t in range(tiles):
                at = pl.ds(t * LANES, LANES)
                ids = ids_ref[:, at]
                run = ms_ref[mine, at]
                shift = 1
                while shift < LANES:
                    same = (pltpu.roll(ids, shift, 1) == ids) & (lane >= shift)
                    run = jnp.where(same, jnp.maximum(run, pltpu.roll(run, shift, 1)), run)
                    shift *= 2
                run = jnp.where(ids == carry_id, jnp.maximum(run, carry), run)
                carry = run[:, LANES - 1 :]
                carry_id = ids[:, LANES - 1 :]
                if t + 1 < tiles:
                    following = ids_ref[:, pl.ds((t + 1) * LANES, LANES)][:, 0:1]
                else:
                    following = jnp.full((1, 1), -1, jnp.int32)
                nxt = jnp.where(lane == LANES - 1, following, pltpu.roll(ids, LANES - 1, 1))
                ends = jnp.where((iota((subs, LANES), 0) == ids) & (ids != nxt), 1.0, 0.0).astype(BF16)
                peak = peak + dot_nt(run.astype(BF16), ends)
            peak = jnp.where(peak < EMPTY, 0.0, peak)
            peaks[:, mine] = jnp.transpose(peak)
            peak_half = peak.astype(BF16)
            total = jnp.zeros((2 * LANES, subs), F32)
            for t in range(tiles):
                at = pl.ds(t * LANES, LANES)
                wh, wl = halves(jnp.exp(ms_ref[mine, at] - dot(peak_half, table[:, at])))
                wh_ref[mine, at] = wh
                wl_ref[mine, at] = wl
                total = total + dot(jnp.concatenate([wh, wl], axis=0), table_t[at, :])
            sums[:, mine] = jnp.transpose(total[:LANES] + total[LANES:])


def condense(b, sums, peaks, cotm_ref, table_t, cols, ids_ref, part_ref, left_ref, right_ref, lst_ref, c_ref):
    cats = 16
    subs = sums.shape[0]
    width = ids_ref.shape[1]
    mine = pl.ds(b * LANES, LANES)
    total = sums[:, mine]
    raw = jnp.where(total > 0.0, peaks[:, mine] + jnp.log(jnp.where(total > 0.0, total, 1.0)), NEG)
    lam, store, par, irho = cols[0], cols[1], cols[2], cols[3]
    cot_total = jnp.transpose(dot(cotm_ref[mine, :], table_t[...]))
    full = lse2(raw, store)
    lst_ref[:, mine] = full
    c_ref[:, mine] = cot_total
    row = iota((subs, LANES), 0)
    first, last = ids_ref[:, 0:1], ids_ref[:, width - 1 :]
    is_first, is_last = row == first, row == last
    factor = lam * irho
    ratio_all = full * factor
    ratio = jnp.where((row > first) & (row < last), ratio_all, NEG)
    spread = jnp.full((subs, LANES), NEG, F32)
    tops = []
    for c in range(cats):
        hit = par == c
        top = jnp.max(jnp.where(hit, ratio, NEG), axis=0, keepdims=True)
        tops.append(top)
        spread = jnp.where(hit, top, spread)
    tops = jnp.concatenate(tops, axis=0)
    terms = jnp.where(ratio > EMPTY, jnp.exp(ratio - spread), 0.0)
    children = jnp.where(iota((subs, LANES), 1).astype(F32) == par, 1.0, 0.0)
    children = jnp.transpose(children)[0:cats].astype(BF16)
    found = dot(children, jnp.concatenate(halves(terms) + thirds(cot_total), axis=1))
    amount = found[:, 0:LANES] + found[:, LANES : 2 * LANES]
    cat_cot = found[:, 2 * LANES : 3 * LANES] + found[:, 3 * LANES : 4 * LANES] + found[:, 4 * LANES :]
    logs = jnp.where(amount > 0.0, tops + jnp.log(jnp.where(amount > 0.0, amount, 1.0)), NEG)

    def at_row(mask, values):
        return jnp.sum(jnp.where(mask, values, 0.0), axis=0, keepdims=True)

    first_id = jnp.broadcast_to(first.astype(F32), (1, LANES))
    last_id = jnp.broadcast_to(last.astype(F32), (1, LANES))
    blank = jnp.zeros((5, LANES), F32)
    low = at_row(is_first, raw)
    left_ref[b] = jnp.concatenate([low, at_row(is_first, cot_total), first_id, blank], axis=0)
    right_ref[b] = jnp.concatenate([at_row(is_last, raw), at_row(is_last, cot_total), last_id, blank], axis=0)
    ends = jnp.concatenate(
        [
            low, at_row(is_last, full), at_row(is_first, ratio_all), first_id, last_id,
            at_row(is_last, factor), at_row(is_first, par), at_row(is_last, par),
        ],
        axis=0,
    )
    pairs = ((logs[0:8], logs[8:16]), (cat_cot[0:8], cat_cot[8:16]), (ends, pltpu.roll(ends, 4, 0)))
    for k, pair in enumerate(pairs):
        part_ref[2 * b, 8 * k : 8 * k + 8], part_ref[2 * b + 1, 8 * k : 8 * k + 8] = pack(*pair)


ROWS = 20


def unpack_ends(buf, count):
    left = iota((count, LANES), 1) < LANES // 2
    front, back = [], []
    for k in range(4):
        line = jnp.concatenate([buf[d, 16 + k : 17 + k, :] for d in range(count)], axis=0)
        other = turn(line)
        front.append(jnp.where(left, line, other))
        back.append(jnp.where(left, other, line))
    return front + back


def join(buf, count, inner, single):
    low, high, alone, first_id, last_id, factor, first_cat, last_cat = unpack_ends(buf, count)
    place = iota((count, LANES), 0)
    joined = (last_id == pltpu.roll(first_id, count - 1, 0)) & (place < count - 1)
    taken = (first_id == pltpu.roll(last_id, 1, 0)) & (place > 0)
    first = jnp.where(taken, NEG, alone)
    last = jnp.where(joined, lse2(high, pltpu.roll(low, count - 1, 0)), high) * factor
    if single:
        last = jnp.where(first_id == last_id, NEG, last)
    here = iota((8, LANES), 0) + jnp.where(iota((8, LANES), 1) < LANES // 2, 0, 8)
    here = here.astype(F32)
    parts = [buf[d, 0:8, :] for d in range(count)]
    for d in range(count):
        if d > 0 or not inner:
            parts.append(jnp.where(first_cat[d : d + 1] == here, first[d : d + 1], NEG))
        if d < count - 1 or not inner:
            parts.append(jnp.where(last_cat[d : d + 1] == here, last[d : d + 1], NEG))
    top = functools.reduce(jnp.maximum, parts)
    logs = top + jnp.log(sum(jnp.exp(part - top) for part in parts))
    return logs, sum(buf[d, 8:16, :] for d in range(count))


def swap_kernel(
    ny, nz, nx, sums, peaks, cotm_ref, table_t, cols, rows_ref, rho_ref, ids_ref, inv_ref,
    cv_ref, top_ref, nbl_ref, nbr_ref, left_ref, right_ref, lst_ref, c_ref, cg_ref,
    part_ref, zbuf, line, ybuf, xsrc, xbuf, values, tops,
    nb_send, nb_recv, z_send, z_recv, y_send, y_recv, x_send, x_recv, g_send, g_recv, t_send, t_recv,
):
    sku = lax.axis_index("sku")
    cat = lax.axis_index("cat")
    y, z = sku // nz, sku % nz
    n = ny * nz
    to_right, to_left = (sku + 1) % n, (sku + n - 1) % n
    next_z = [(z + k) % nz for k in range(1, nz)]
    along_z = [y * nz + other for other in next_z]
    along_y = [(y + k) % ny * nz + z for k in range(1, ny)]
    along_x = [(cat + k) % nx for k in range(1, nx)]

    barrier = pltpu.get_barrier_semaphore()
    for other in along_z + along_y + [to_right, to_left]:
        pl.semaphore_signal(barrier, inc=1, device_id={"sku": other}, device_id_type=MESH)
    for other in along_x:
        pl.semaphore_signal(barrier, inc=1, device_id={"cat": other}, device_id_type=MESH)
    for b in range(left_ref.shape[0]):
        condense(b, sums, peaks, cotm_ref, table_t, cols, ids_ref, part_ref, left_ref, right_ref, lst_ref, c_ref)
    pl.semaphore_wait(barrier, nz + ny + nx - 1)

    def send(src, dst, send_sem, recv_sem, device):
        copy = pltpu.make_async_remote_copy(
            src_ref=src, dst_ref=dst, send_sem=send_sem, recv_sem=recv_sem, device_id=device, device_id_type=MESH
        )
        copy.start()
        return copy

    used = pl.ds(0, ROWS)
    by_z = [
        send(part_ref.at[next_z[k], used], zbuf.at[z, used], z_send.at[k], z_recv.at[k], {"sku": other})
        for k, other in enumerate(along_z)
    ]
    near = [
        send(right_ref, nbl_ref, nb_send.at[0], nb_recv.at[0], {"sku": to_right}),
        send(left_ref, nbr_ref, nb_send.at[1], nb_recv.at[1], {"sku": to_left}),
    ]
    zbuf[z] = part_ref[z]
    ah, al = halves(rows_ref[0:1, :])
    pick = iota((16, ah.shape[1]), 0)
    weights = jnp.where(pick == 0, ah.astype(F32), jnp.where(pick == 1, al.astype(F32), 0.0)).astype(BF16)
    for k in range(cg_ref.shape[1] // CHUNK):
        at = pl.ds(k * CHUNK, CHUNK)
        cg_ref[:, at] = jnp.sum(dot(weights, cotm_ref[:, at]), axis=0, keepdims=True) * inv_ref[0:1, at]
    for copy in by_z:
        copy.wait_recv()

    line[0:8, :], line[8:16, :] = join(zbuf, nz, True, True)
    begin, end = zbuf[0, 16:24, :], zbuf[nz - 1, 16:24, :]
    row, left = iota((8, LANES), 0), iota((8, LANES), 1) < LANES // 2
    from_begin = (row == 2) | (left & ((row == 0) | (row == 3)))
    one = end[3:4] == turn(end)[0:1]
    end = jnp.where(left & (row == 1) & one, NEG, end)
    line[16:24, :] = jnp.where(from_begin, begin, end)

    by_y = [
        send(line.at[used], ybuf.at[y, used], y_send.at[k], y_recv.at[k], {"sku": other})
        for k, other in enumerate(along_y)
    ]
    ybuf[y] = line[...]
    for copy in by_y:
        copy.wait_recv()
    logs, cot = join(ybuf, ny, False, False)
    value = rho_ref[0:8, :] * logs
    values[0:8, :] = value
    values[8:16, :] = cot
    top = jnp.max(value, axis=0, keepdims=True)
    top = jnp.maximum(top, turn(top))
    total = jnp.sum(jnp.exp(value - top), axis=0, keepdims=True)
    cot = jnp.sum(cot, axis=0, keepdims=True)
    xsrc[0:1, :] = top + jnp.log(total + turn(total))
    xsrc[1:2, :] = cot + turn(cot)
    xsrc[2:8, :] = jnp.zeros((6, LANES), F32)

    by_x = [send(xsrc, xbuf.at[k], x_send.at[k], x_recv.at[k], {"cat": other}) for k, other in enumerate(along_x)]
    gather = [
        send(values, cv_ref.at[z], g_send.at[k], g_recv.at[k], {"sku": other}) for k, other in enumerate(along_z)
    ]
    cv_ref[z] = values[...]
    for copy in by_x:
        copy.wait_recv()
    groups = [xsrc[0:1, :]] + [xbuf[k, 0:1, :] for k in range(nx - 1)]
    top = functools.reduce(jnp.maximum, groups + [jnp.zeros((1, LANES), F32)])
    tops[0:1, :] = top + jnp.log(jnp.exp(-top) + sum(jnp.exp(group - top) for group in groups))
    tops[1:2, :] = xsrc[1:2, :] + sum(xbuf[k, 1:2, :] for k in range(nx - 1))
    tops[2:8, :] = jnp.zeros((6, LANES), F32)
    last = [send(tops, top_ref.at[z], t_send.at[k], t_recv.at[k], {"sku": other}) for k, other in enumerate(along_z)]
    top_ref[z] = tops[...]
    for copy in near + gather + last:
        copy.wait_recv()
    for copy in by_z + near + by_y + by_x + gather + last:
        copy.wait_send()


def slope_kernel(
    wh_ref, wl_ref, lst_ref, r_ref, c_ref, cv_ref, top_ref, nbl_ref, nbr_ref, left_ref, right_ref, cg_ref, ids_ref,
    rows_ref, cols, rho_ref, grad_ref, path_ref, hs,
):
    subs = lst_ref.shape[0]
    blocks = nbl_ref.shape[0]
    width = ids_ref.shape[1]
    lam, par, irho, ilam = cols[0], cols[2], cols[3], cols[4]
    cats = 16
    spot = iota((subs, LANES), 1)
    parents = jnp.where(((spot % cats).astype(F32) == par) & (spot < 3 * cats), 1.0, 0.0).astype(BF16)[:, : 3 * cats]
    row = iota((subs, LANES), 0).astype(F32)
    for b in range(blocks):
        at = pl.ds(b * LANES, LANES)
        from_left, from_right = nbl_ref[b], nbr_ref[b]
        first_id, last_id = left_ref[b, 2:3, :], right_ref[b, 2:3, :]
        values, cots = [
            jnp.concatenate(pack(cv_ref[2 * b, 8 * k : 8 * k + 8, :], cv_ref[2 * b + 1, 8 * k : 8 * k + 8, :]), axis=0)
            for k in range(2)
        ]
        top = jnp.where(iota((8, LANES), 1) < LANES // 2, top_ref[2 * b], top_ref[2 * b + 1])
        inclusive = top[0:1]
        slopes = (1.0 - 1.0 / rho_ref[8:24, :]) * cots - top[1:2] * jnp.exp(values - inclusive)
        left_hit = (row == first_id) & (from_left[2:3] == first_id)
        right_hit = (row == last_id) & (from_right[2:3] == last_id)
        extra = jnp.where(left_hit, from_left[0:1], jnp.where(right_hit, from_right[0:1], NEG))
        level = lse2(lst_ref[:, at], extra)
        sub_cot = c_ref[:, at] + jnp.where(left_hit, from_left[1:2], jnp.where(right_hit, from_right[1:2], 0.0))
        cat_value = dot(parents, jnp.concatenate(thirds(values), axis=0))
        d_cat = dot(parents, jnp.concatenate(thirds(slopes), axis=0))
        log_sub = (lam * level - cat_value) * irho
        path = rows_ref[1:2, at] - level + log_sub + (cat_value - inclusive)
        d_sub = (irho - ilam) * sub_cot + jnp.exp(log_sub) * d_cat
        slope = rows_ref[0:1, at] * jnp.exp(r_ref[:, at] - level) * d_sub
        hs[0:subs, at], hs[subs:, at] = halves(slope)
        ph, plo = halves(jnp.transpose(path))
        path_ref[at, 0:subs] = ph
        path_ref[at, subs:] = plo
    for k in range(width // CHUNK):
        at = pl.ds(k * CHUNK, CHUNK)
        both = dot(hs[...], wh_ref[:, at])
        found = both[0:subs] + both[subs:] + dot(hs[0:subs, :], wl_ref[:, at])
        hit = iota((subs, CHUNK), 0) == ids_ref[:, at]
        grad_ref[:, at] = -(jnp.sum(jnp.where(hit, found, 0.0), axis=0, keepdims=True) + cg_ref[:, at])


def demand_kernel(ms_ref, path_ref, table, out_hbm, value_ref, sem):
    markets, width = ms_ref.shape

    def flush(b):
        rows = pl.ds(b * LANES, LANES)
        return pltpu.make_async_copy(value_ref.at[rows], out_hbm.at[rows, 0, :], sem.at[b])

    for b in range(markets // LANES):
        rows = pl.ds(b * LANES, LANES)
        for k in range(width // CHUNK):
            at = pl.ds(k * CHUNK, CHUNK)
            masked = ms_ref[rows, at]
            hits = table[:, at]
            path = dot(path_ref[rows, :], jnp.concatenate([hits, hits], axis=0))
            value_ref[rows, at] = jnp.where(masked > EMPTY, masked + path, 0.0)
        flush(b).start()
    for b in range(markets // LANES):
        flush(b).wait()


def whole():
    return pl.BlockSpec(memory_space=pltpu.VMEM)


def shards(
    n_sku, n_cat, features, taste, price, alpha, market_size, store_brand, sub_scale, cat_scale, availability,
    sku_subcat, subcat_cat, cotangent,
):
    markets, depth = features.shape
    width = price.shape[1]
    subs, cats = sub_scale.shape[1], cat_scale.shape[1]
    blocks = markets // LANES
    operands = (
        features,
        taste.reshape(depth, width),
        price,
        alpha.reshape(1, markets),
        market_size.reshape(1, markets),
        sub_scale,
        store_brand,
        cat_scale,
        subcat_cat,
        availability,
        sku_subcat,
        cotangent.reshape(markets, width),
    )
    operands = [pltpu.with_memory_space_constraint(x, pltpu.HBM) for x in operands]
    sds = jax.ShapeDtypeStruct
    vmem, dma = pltpu.VMEM, pltpu.SemaphoreType.DMA
    ms, wh, wl, cotm, sums, peaks, table, table_t, cols, rows, rho_rows, ids, inv = pl.pallas_call(
        local_kernel,
        in_specs=[pl.BlockSpec(memory_space=pl.ANY)] * 12,
        out_specs=[whole()] * 13,
        out_shape=[
            sds((markets, width), F32),
            sds((markets, width), BF16),
            sds((markets, width), BF16),
            sds((markets, width), BF16),
            sds((subs, markets), F32),
            sds((subs, markets), F32),
            sds((subs, width), BF16),
            sds((width, subs), BF16),
            sds((5, subs, LANES), F32),
            sds((8, markets), F32),
            sds((24, LANES), F32),
            sds((1, width), jnp.int32),
            sds((8, width), F32),
        ],
        scratch_shapes=[
            vmem((markets, depth), BF16),
            vmem((depth, width), BF16),
            vmem((1, width), F32),
            vmem((1, subs), F32),
            vmem((1, subs), F32),
            vmem((1, cats), F32),
            vmem((1, subs), jnp.int32),
            vmem((markets, width), jnp.int32),
            vmem((1, markets), F32),
            vmem((8, CHUNK), F32),
            dma((8,)),
            dma((2,)),
            dma((blocks,)),
            dma((blocks,)),
        ],
        compiler_params=pltpu.CompilerParams(vmem_limit_bytes=32 * 1024 * 1024),
        name="local_nests",
    )(*operands)

    nz = 2 * blocks
    ny = n_sku // nz
    cv, top, nbl, nbr, left, right, lst, c, cg = pl.pallas_call(
        functools.partial(swap_kernel, ny, nz, n_cat),
        in_specs=[whole()] * 9,
        out_specs=[whole()] * 9,
        out_shape=[sds((nz, 16, LANES), F32), sds((nz, 8, LANES), F32)]
        + [sds((blocks, 8, LANES), F32)] * 4
        + [sds((subs, markets), F32)] * 2
        + [sds((1, width), F32)],
        scratch_shapes=[
            vmem((nz, 24, LANES), F32),
            vmem((nz, 24, LANES), F32),
            vmem((24, LANES), F32),
            vmem((ny, 24, LANES), F32),
            vmem((8, LANES), F32),
            vmem((n_cat - 1, 8, LANES), F32),
            vmem((16, LANES), F32),
            vmem((8, LANES), F32),
        ]
        + [dma((count,)) for count in (2, nz - 1, ny - 1, n_cat - 1, nz - 1, nz - 1) for _ in range(2)],
        compiler_params=pltpu.CompilerParams(
            collective_id=0, has_side_effects=True, vmem_limit_bytes=16 * 1024 * 1024
        ),
        name="swap_nests",
    )(sums, peaks, cotm, table_t, cols, rows, rho_rows, ids, inv)

    grad, path = pl.pallas_call(
        slope_kernel,
        in_specs=[whole()] * 16,
        out_specs=[whole()] * 2,
        out_shape=[sds((1, width), F32), sds((markets, 2 * subs), BF16)],
        scratch_shapes=[vmem((2 * subs, markets), BF16)],
        compiler_params=pltpu.CompilerParams(vmem_limit_bytes=16 * 1024 * 1024),
        name="price_slope",
    )(wh, wl, lst, peaks, c, cv, top, nbl, nbr, left, right, cg, ids, rows, cols, rho_rows)
    other = lax.ppermute(grad, "mkt", [(0, 1), (1, 0)])

    demand = pl.pallas_call(
        demand_kernel,
        in_specs=[whole()] * 3,
        out_specs=pl.BlockSpec(memory_space=pl.ANY),
        out_shape=sds((markets, 1, width), F32),
        scratch_shapes=[vmem((markets, width), F32), dma((blocks,))],
        compiler_params=pltpu.CompilerParams(vmem_limit_bytes=16 * 1024 * 1024),
        cost_estimate=pl.CostEstimate(
            flops=2 * markets * width * 2 * subs, bytes_accessed=8 * markets * width, transcendentals=0
        ),
        name="log_demand",
    )(ms, path, table)
    return demand, grad + other


def solution(mesh):
    return jax.shard_map(
        functools.partial(shards, mesh.shape["sku"], mesh.shape["cat"]),
        mesh=mesh,
        in_specs=(
            P("mkt", None),
            P(None, "cat", "sku"),
            P("cat", "sku"),
            P("mkt"),
            P("mkt"),
            P("cat", None),
            P("cat", None),
            P("cat", None),
            P("mkt", "cat", "sku"),
            P("cat", "sku"),
            P("cat", None),
            P("mkt", "cat", "sku"),
        ),
        out_specs=(P("mkt", "cat", "sku"), P("cat", "sku")),
        check_vma=False,
    )
```

time: 575 us -> 55.4 us (0.10)
  waiting for transfers between devices: 285 us -> 0.01 us
  other arithmetic: 177 us -> 0.61 us
  matrix products: 36.8 us -> 0 us
  Pallas kernels: 0 us -> 35.8 us
  local copies, waits for them, and re-layouts: 33.5 us -> 0 us
  blocking collectives: 26.5 us -> 0 us
  starting transfers between devices: 0.08 us -> 18.2 us
  between operations: 14.3 us -> 0.67 us
    reduce_max x32 -> x0, other arithmetic: 165 us -> none  [one_block(): jnp.max(jnp.where(flags[None, :, :], piece[:, :, None], -jnp.inf), axis=1)]
    psum x1 -> x0, waiting for transfers between devices: 145 us -> none  [shards(): total = lax.psum(partial_sum, 'sku')]
    pmax x1 -> x0, waiting for transfers between devices: 141 us -> none  [shards(): sub_top = lax.pmax(local_top, 'sku')]
    dot_general x16 -> x0, matrix products: 36.8 us -> none  [the longest x8 20.8 us: spread(): return jnp.dot(table_values, table_back, precision=lax.Precision.HIGHEST)]
    pallas_call x0 -> x4, Pallas kernels: none -> 35.8 us  [the longest x1 24.8 us: shards(): pl.pallas_call(functools.partial(swap_kernel, ny, nz, n_cat), in_specs=[w...]
    ppermute x0 -> x1, starting transfers between devices: none -> 18.2 us  [shards(): other = lax.ppermute(grad, 'mkt', [(0, 1), (1, 0)])]
    psum x2 -> x0, blocking collectives: 18.1 us -> none  [the longest x1 11.9 us: shards(): grad = lax.psum(local_grad, 'mkt')]
    broadcast_in_dim x32 -> x0, local copies, waits for them, and re-layouts: 15.9 us -> none  [one_block(): jnp.where(flags[None, :, :], piece[:, :, None], -jnp.inf)]
  transfers between devices with their start and end apart: 2 -> 1, of which waited for: 2 -> 0; matrix products, arithmetic and copies ran while one was open for 1% -> 0% of each run, Pallas kernels for 0% -> 4%
where the time goes in v2:
time: 55.4 us; the launch traced here: 55.3 us
  Pallas kernels  35.8 us (65%)
  starting transfers between devices  18.2 us (33%)
  between operations  0.67 us (1%)
  other arithmetic  0.61 us (1%)
    pallas_call x1, Pallas kernels, shards(): pl.pallas_call(functools.partial(swap_kernel, ny, nz, n_cat), in_specs=[w...  24.8 us
    ppermute x1, starting transfers between devices, shards(): other = lax.ppermute(grad, 'mkt', [(0, 1), (1, 0)])  18.2 us
    pallas_call x1, Pallas kernels, shards(): pl.pallas_call(local_kernel, in_specs=[pl.BlockSpec(memory_space=pl.ANY)]...  7.24 us
    pallas_call x1, Pallas kernels, shards(): pl.pallas_call(demand_kernel, in_specs=[whole()] * 3, out_specs=pl.BlockS...  2.35 us
    pallas_call x1, Pallas kernels, shards(): pl.pallas_call(slope_kernel, in_specs=[whole()] * 16, out_specs=[whole()]...  1.45 us
  transfers between devices with their start and end apart: 1, of which 0 were waited for; matrix products, arithmetic and copies ran while one was open for 0% of the time, Pallas kernels for 4%

profile of v2, /device:TPU:1, one launch (start us, length us, event | category | flops | bytes accessed | tf_op | source)
XLA Modules:
  0.0 55.3 jit_solution(16023926830490488209)
XLA Ops:
  0.6 7.2 %local_nests.1 = (f32[512,2048]{1,0:T(8,128)S(1)}, bf16[512,2048]{1,0:T(8,128)(2,1)S(1)}, bf16[512,2048]{1,0:T(8,128)(2,1)S(1)}, bf16[512,2048]{1,0:T(8,128)(2,1...) custom-call(bf16[512,512]{1,0:T(8,128)(2,1)} %feat_hbm.1, ...), custom_call_target="tpu_custom_call" | custom-call | tf_op jit(solution)/shard_map/local_nests/pallas_call | solution.py:484
  7.9 24.8 %swap_nests.1 = (f32[8,16,128]{2,1,0:T(8,128)S(1)}, f32[8,8,128]{2,1,0:T(8,128)S(1)}, f32[4,8,128]{2,1,0:T(8,128)S(1)}, f32[4,8,128]{2,1,0:T(8,128)S(1)}, f32[4,...) custom-call(f32[128,512]{1,0:T(8,128)S(1)} %get-tuple-element.29.sum, ...), custom_call_target="tpu_custom_call" | custom-call | tf_op jit(solution)/shard_map/swap_nests/pallas_call | solution.py:525
  32.7 1.5 %price_slope.1 = (f32[1,2048]{1,0:T(1,128)S(1)}, bf16[512,256]{1,0:T(8,128)(2,1)S(1)}) custom-call(bf16[512,2048]{1,0:T(8,128)(2,1)S(1)} %get-tuple-element.27.wh_ref, bf16[512,2048]{1,0:T(8,128)(2,1)S(1)} %get-tuple-element.28.wl_ref, f32[128,512]{1,0:T(8,128)S(1)} %get-tuple-element.38.lst_ref, f32[128,512]{1,0:T(8,128)S(1)} %get-tuple-element.30.peaks.r_ref, ...), custom_call_target="tpu_custom_call" | custom-call | tf_op jit(solution)/shard_map/price_slope/pallas_call | solution.py:550
  34.1 18.2 %collective-permute-start = (f32[1,2048]{1,0:T(1,128)S(1)}, f32[1,2048]{1,0:T(1,128)S(1)}, u32[]{:S(2)}, u32[]{:S(2)}) collective-permute-start(f32[1,2048]{1,0:T(1,128)S(1)} %get-tuple-element.49), channel_id=1, source_target_pairs={{0,128},{128,0},{1,129},{129,1},{2,130},{130,2},{3,131},{131,3},{4... | collective-permute-start | bytes 24584 | tf_op jit(solution)/shard_map/ppermute | solution.py:559
  52.3 2.4 %log_demand.1 = f32[512,1,2048]{2,1,0:T(1,128)} custom-call(f32[512,2048]{1,0:T(8,128)S(1)} %get-tuple-element.26.ms_ref, bf16[512,256]{1,0:T(8,128)(2,1)S(1)} %get-tuple-element.47.path_ref, bf16[128,2048]{1,0:T(8,128)(2,1)S(1)} %get-tuple-element.48.table), custom_call_target="tpu_custom_call" | custom-call | flops 536870912 | bytes 8388608 | tf_op jit(solution)/shard_map/log_demand/pallas_call | solution.py:561
  54.6 0.0 collective-permute-done
  54.7 0.6 %add.3 = f32[1,2048]{1,0:T(1,128)} add(f32[1,2048]{1,0:T(1,128)S(1)} %get-tuple-element.49, f32[1,2048]{1,0:T(1,128)S(1)} %collective-permute-done) | non-fusion elementwise | flops 2048 | bytes 24576 | tf_op jit(solution)/shard_map/add | solution.py:573
Async XLA Ops:
  34.1 20.5 %collective-permute-start = (f32[1,2048]{1,0:T(1,128)S(1)}, f32[1,2048]{1,0:T(1,128)S(1)}, u32[]{:S(2)}, u32[]{:S(2)}) collective-permute-start(f32[1,2048]{1,0:T(1,128)S(1)} %get-tuple-element.49), channel_id=1, source_target_pairs={{0,128},{128,0},{1,129},{129,1},{2,130},{130,2},{3,131},{131,3},{4... | collective-permute-start | bytes 24584 | tf_op jit(solution)/shard_map/ppermute | solution.py:559

commit v3 on v2

--- a/solution.py
+++ b/solution.py
@@ -71,53 +71,51 @@
     return pltpu.roll(x, LANES // 2, 1)
 
 
+AHEAD = 3
+ROW_BLOCK = 256
+
+
 def local_kernel(
     feat_hbm, taste_hbm, price_hbm, alpha_hbm, size_hbm, lam_hbm, store_hbm, rho_hbm, par_hbm, avail_hbm, mem_hbm,
     cot_hbm,
     ms_ref, wh_ref, wl_ref, cotm_ref, sums, peaks, table, table_t, cols, rows_ref, rho_rows, ids_ref, inv_ref,
-    feat, taste, price, lam_row, store_row, rho_row, par_row, avail, size, worst,
-    small_sem, big_sem, avail_sem, cot_sem,
+    feat, taste, price, lam_row, store_row, rho_row, par_row, avail, size, worst, alpha, totals,
+    small_sem, feat_sem, taste_sem, avail_sem, cot_sem,
 ):
     subs = lam_row.shape[1]
     cats = rho_row.shape[1]
-    width = ids_ref.shape[1]
-    blocks = ms_ref.shape[0] // LANES
+    markets, width = ms_ref.shape
+    blocks = markets // LANES
     tiles = width // LANES
+    chunks = width // CHUNK
     small = [
-        (mem_hbm, ids_ref), (lam_hbm, lam_row), (price_hbm, price), (store_hbm, store_row), (rho_hbm, rho_row),
-        (par_hbm, par_row), (alpha_hbm, rows_ref.at[0:1]), (size_hbm, size),
+        (mem_hbm, ids_ref), (lam_hbm, lam_row), (price_hbm, price), (alpha_hbm, rows_ref.at[0:1]),
+        (store_hbm, store_row), (rho_hbm, rho_row), (par_hbm, par_row), (size_hbm, size),
     ]
     small = [pltpu.make_async_copy(src, dst, small_sem.at[k]) for k, (src, dst) in enumerate(small)]
-    big = [
-        pltpu.make_async_copy(src, dst, big_sem.at[k])
-        for k, (src, dst) in enumerate([(feat_hbm, feat), (taste_hbm, taste)])
-    ]
-
-    def fetch(b):
-        rows = pl.ds(pl.multiple_of(b * LANES, LANES), LANES)
+    whole_feat = pltpu.make_async_copy(feat_hbm, feat, feat_sem)
+
+    def fetch(k):
+        at = pl.ds(pl.multiple_of(k * CHUNK, CHUNK), CHUNK)
         return (
-            pltpu.make_async_copy(avail_hbm.at[rows, 0, :], avail.at[rows], avail_sem.at[b]),
-            pltpu.make_async_copy(cot_hbm.at[rows], cotm_ref.at[rows], cot_sem.at[b]),
+            pltpu.make_async_copy(taste_hbm.at[:, at], taste.at[:, at], taste_sem.at[k]),
+            pltpu.make_async_copy(avail_hbm.at[:, 0, at], avail.at[:, at], avail_sem.at[k]),
+            pltpu.make_async_copy(cot_hbm.at[:, at], cotm_ref.at[:, at], cot_sem.at[k]),
         )
 
-    for copy in small + big:
+    for copy in small:
         copy.start()
-    for b in range(blocks):
-        for copy in fetch(b):
+    whole_feat.start()
+    for k in range(AHEAD):
+        for copy in fetch(k):
             copy.start()
     for copy in small:
         copy.wait()
 
     lam = column(lam_row[...])
-    for k in range(width // CHUNK):
-        at = pl.ds(k * CHUNK, CHUNK)
-        hit = iota((subs, CHUNK), 0) == ids_ref[:, at]
-        ones = jnp.where(hit, 1.0, 0.0)
-        table[:, at] = ones.astype(BF16)
-        table_t[at, :] = jnp.transpose(ones).astype(BF16)
-        inv = 1.0 / jnp.sum(jnp.where(hit, lam, 0.0), axis=0, keepdims=True)
-        inv_ref[0:1, at] = inv
-        inv_ref[1:2, at] = inv * price[:, at]
+    for b in range(blocks):
+        mine = pl.ds(b * LANES, LANES)
+        alpha[mine, :] = jnp.transpose(jnp.broadcast_to(rows_ref[0:1, mine], (LANES, LANES)))
     _, ilam, store, par, irho = nest_columns(lam_row, store_row, rho_row, par_row)
     for k, col in enumerate((lam, store, par, irho, ilam)):
         cols[k] = jnp.broadcast_to(col, (subs, LANES))
@@ -127,33 +125,50 @@
     rows_ref[1:2, :] = jnp.log(size[...])
     worst[...] = jnp.zeros_like(worst)
     peaks[...] = jnp.zeros_like(peaks)
-    for copy in big:
-        copy.wait()
-
-    @pl.loop(0, blocks)
-    def _(b):
-        mine = pl.ds(pl.multiple_of(b * LANES, LANES), LANES)
-        for copy in fetch(b):
+    totals[...] = jnp.zeros_like(totals)
+    whole_feat.wait()
+
+    @pl.loop(0, chunks)
+    def _(k):
+        at = pl.ds(pl.multiple_of(k * CHUNK, CHUNK), CHUNK)
+
+        @pl.when(k + AHEAD < chunks)
+        def _():
+            for copy in fetch(k + AHEAD):
+                copy.start()
+
+        scale = jnp.concatenate([cols[0], cols[0]], axis=1)
+        hit = iota((subs, CHUNK), 0) == ids_ref[:, at]
+        ones = jnp.where(hit, 1.0, 0.0)
+        table[:, at] = ones.astype(BF16)
+        turned = jnp.transpose(ones).astype(BF16)
+        table_t[at, :] = turned
+        inv = 1.0 / jnp.sum(jnp.where(hit, scale, 0.0), axis=0, keepdims=True)
+        cost = inv * price[:, at]
+        inv_ref[0:1, at] = inv
+        for copy in fetch(k):
             copy.wait()
-        alpha = jnp.transpose(jnp.broadcast_to(rows_ref[0:1, mine], (LANES, LANES)))
-        alpha2 = jnp.concatenate([alpha, alpha], axis=1)
-        total = jnp.zeros((2 * LANES, subs), F32)
-        most = jnp.zeros((8, CHUNK), F32)
-        for k in range(width // CHUNK):
-            at = pl.ds(k * CHUNK, CHUNK)
-            util = dot(feat[mine, :], taste[:, at])
-            scaled = util * inv_ref[0:1, at] - alpha2 * inv_ref[1:2, at]
-            open_ = avail[mine, at]
+        most = worst[...]
+        for h in range(markets // ROW_BLOCK):
+            rows = pl.ds(h * ROW_BLOCK, ROW_BLOCK)
+            util = dot(feat[rows, :], taste[:, at])
+            weight = alpha[rows, :]
+            scaled = util * inv - jnp.concatenate([weight, weight], axis=1) * cost
+            open_ = avail[rows, at]
             masked = jnp.where(open_ == 1, scaled, NEG)
-            ms_ref[mine, at] = masked
-            most = jnp.maximum(most, jnp.max(jnp.abs(scaled).reshape(LANES // 8, 8, CHUNK), axis=0))
+            ms_ref[rows, at] = masked
+            most = jnp.maximum(most, jnp.max(jnp.abs(scaled).reshape(ROW_BLOCK // 8, 8, CHUNK), axis=0))
             wh, wl = halves(jnp.exp(masked))
-            wh_ref[mine, at] = wh
-            wl_ref[mine, at] = wl
-            cotm_ref[mine, at] = cotm_ref[mine, at] * open_.astype(F32).astype(BF16)
-            total = total + dot(jnp.concatenate([wh, wl], axis=0), table_t[at, :])
-        sums[:, mine] = jnp.transpose(total[:LANES] + total[LANES:])
-        worst[...] = jnp.maximum(worst[...], most)
+            wh_ref[rows, at] = wh
+            wl_ref[rows, at] = wl
+            cotm_ref[rows, at] = cotm_ref[rows, at] * open_.astype(F32).astype(BF16)
+            both = dot(jnp.concatenate([wh, wl], axis=0), turned)
+            totals[rows, :] += both[:ROW_BLOCK] + both[ROW_BLOCK:]
+        worst[...] = most
+
+    for b in range(blocks):
+        mine = pl.ds(b * LANES, LANES)
+        sums[:, mine] = jnp.transpose(totals[mine, :])
 
     @pl.when(jnp.max(worst[...]) > SAFE)
     def _():
@@ -435,21 +450,21 @@
 def demand_kernel(ms_ref, path_ref, table, out_hbm, value_ref, sem):
     markets, width = ms_ref.shape
 
-    def flush(b):
-        rows = pl.ds(b * LANES, LANES)
-        return pltpu.make_async_copy(value_ref.at[rows], out_hbm.at[rows, 0, :], sem.at[b])
-
-    for b in range(markets // LANES):
-        rows = pl.ds(b * LANES, LANES)
-        for k in range(width // CHUNK):
-            at = pl.ds(k * CHUNK, CHUNK)
+    def flush(k):
+        at = pl.ds(k * CHUNK, CHUNK)
+        return pltpu.make_async_copy(value_ref.at[:, at], out_hbm.at[:, 0, at], sem.at[k])
+
+    for k in range(width // CHUNK):
+        at = pl.ds(k * CHUNK, CHUNK)
+        hits = table[:, at]
+        hits = jnp.concatenate([hits, hits], axis=0)
+        for h in range(markets // ROW_BLOCK):
+            rows = pl.ds(h * ROW_BLOCK, ROW_BLOCK)
             masked = ms_ref[rows, at]
-            hits = table[:, at]
-            path = dot(path_ref[rows, :], jnp.concatenate([hits, hits], axis=0))
-            value_ref[rows, at] = jnp.where(masked > EMPTY, masked + path, 0.0)
-        flush(b).start()
-    for b in range(markets // LANES):
-        flush(b).wait()
+            value_ref[rows, at] = jnp.where(masked > EMPTY, masked + dot(path_ref[rows, :], hits), 0.0)
+        flush(k).start()
+    for k in range(width // CHUNK):
+        flush(k).wait()
 
 
 def whole():
@@ -511,10 +526,13 @@
             vmem((markets, width), jnp.int32),
             vmem((1, markets), F32),
             vmem((8, CHUNK), F32),
+            vmem((markets, LANES), F32),
+            vmem((markets, subs), F32),
             dma((8,)),
-            dma((2,)),
-            dma((blocks,)),
-            dma((blocks,)),
+            dma,
+            dma((width // CHUNK,)),
+            dma((width // CHUNK,)),
+            dma((width // CHUNK,)),
         ],
         compiler_params=pltpu.CompilerParams(vmem_limit_bytes=32 * 1024 * 1024),
         name="local_nests",
@@ -563,7 +581,7 @@
         in_specs=[whole()] * 3,
         out_specs=pl.BlockSpec(memory_space=pl.ANY),
         out_shape=sds((markets, 1, width), F32),
-        scratch_shapes=[vmem((markets, width), F32), dma((blocks,))],
+        scratch_shapes=[vmem((markets, width), F32), dma((width // CHUNK,))],
         compiler_params=pltpu.CompilerParams(vmem_limit_bytes=16 * 1024 * 1024),
         cost_estimate=pl.CostEstimate(
             flops=2 * markets * width * 2 * subs, bytes_accessed=8 * markets * width, transcendentals=0

time: 55.4 us -> 56.5 us (1.020)
  Pallas kernels: 35.8 us -> 37 us
    pallas_call x1, Pallas kernels: 7.24 us -> 8.04 us  [shards(): pl.pallas_call(local_kernel, in_specs=[pl.BlockSpec(memory_space=pl.ANY)]...]
  transfers between devices with their start and end apart: 1 -> 1, of which waited for: 0 -> 0; matrix products, arithmetic and copies ran while one was open for 0% -> 0% of each run, Pallas kernels for 4% -> 5%
where the time goes in v3:
time: 56.5 us; the launch traced here: 56.4 us
  Pallas kernels  37 us (65%)
  starting transfers between devices  18.2 us (32%)
  between operations  0.67 us (1%)
  other arithmetic  0.61 us (1%)
    pallas_call x1, Pallas kernels, shards(): pl.pallas_call(functools.partial(swap_kernel, ny, nz, n_cat), in_specs=[w...  24.8 us
    ppermute x1, starting transfers between devices, shards(): other = lax.ppermute(grad, 'mkt', [(0, 1), (1, 0)])  18.2 us
    pallas_call x1, Pallas kernels, shards(): pl.pallas_call(local_kernel, in_specs=[pl.BlockSpec(memory_space=pl.ANY)]...  8.04 us
    pallas_call x1, Pallas kernels, shards(): pl.pallas_call(demand_kernel, in_specs=[whole()] * 3, out_specs=pl.BlockS...  2.7 us
    pallas_call x1, Pallas kernels, shards(): pl.pallas_call(slope_kernel, in_specs=[whole()] * 16, out_specs=[whole()]...  1.45 us
  transfers between devices with their start and end apart: 1, of which 0 were waited for; matrix products, arithmetic and copies ran while one was open for 0% of the time, Pallas kernels for 5%

profile of v3, /device:TPU:1, one launch (start us, length us, event | category | flops | bytes accessed | tf_op | source)
XLA Modules:
  0.0 56.4 jit_solution(4523472698467494739)
XLA Ops:
  0.6 8.0 %local_nests.1 = (f32[512,2048]{1,0:T(8,128)S(1)}, bf16[512,2048]{1,0:T(8,128)(2,1)S(1)}, bf16[512,2048]{1,0:T(8,128)(2,1)S(1)}, bf16[512,2048]{1,0:T(8,128)(2,1...) custom-call(bf16[512,512]{1,0:T(8,128)(2,1)} %feat_hbm.1, ...), custom_call_target="tpu_custom_call" | custom-call | tf_op jit(solution)/shard_map/local_nests/pallas_call | solution.py:499
  8.7 24.8 %swap_nests.1 = (f32[8,16,128]{2,1,0:T(8,128)S(1)}, f32[8,8,128]{2,1,0:T(8,128)S(1)}, f32[4,8,128]{2,1,0:T(8,128)S(1)}, f32[4,8,128]{2,1,0:T(8,128)S(1)}, f32[4,...) custom-call(f32[128,512]{1,0:T(8,128)S(1)} %get-tuple-element.29.sum, ...), custom_call_target="tpu_custom_call" | custom-call | tf_op jit(solution)/shard_map/swap_nests/pallas_call | solution.py:543
  33.5 1.4 %price_slope.1 = (f32[1,2048]{1,0:T(1,128)S(1)}, bf16[512,256]{1,0:T(8,128)(2,1)S(1)}) custom-call(bf16[512,2048]{1,0:T(8,128)(2,1)S(1)} %get-tuple-element.27.wh_ref, bf16[512,2048]{1,0:T(8,128)(2,1)S(1)} %get-tuple-element.28.wl_ref, f32[128,512]{1,0:T(8,128)S(1)} %get-tuple-element.38.lst_ref, f32[128,512]{1,0:T(8,128)S(1)} %get-tuple-element.30.peaks.r_ref, ...), custom_call_target="tpu_custom_call" | custom-call | tf_op jit(solution)/shard_map/price_slope/pallas_call | solution.py:568
  34.9 18.2 %collective-permute-start = (f32[1,2048]{1,0:T(1,128)S(1)}, f32[1,2048]{1,0:T(1,128)S(1)}, u32[]{:S(2)}, u32[]{:S(2)}) collective-permute-start(f32[1,2048]{1,0:T(1,128)S(1)} %get-tuple-element.49), channel_id=1, source_target_pairs={{0,128},{128,0},{1,129},{129,1},{2,130},{130,2},{3,131},{131,3},{4... | collective-permute-start | bytes 24584 | tf_op jit(solution)/shard_map/ppermute | solution.py:577
  53.1 2.7 %log_demand.1 = f32[512,1,2048]{2,1,0:T(1,128)} custom-call(f32[512,2048]{1,0:T(8,128)S(1)} %get-tuple-element.26.ms_ref, bf16[512,256]{1,0:T(8,128)(2,1)S(1)} %get-tuple-element.47.path_ref, bf16[128,2048]{1,0:T(8,128)(2,1)S(1)} %get-tuple-element.48.table), custom_call_target="tpu_custom_call" | custom-call | flops 536870912 | bytes 8388608 | tf_op jit(solution)/shard_map/log_demand/pallas_call | solution.py:579
  55.8 0.0 collective-permute-done
  55.8 0.6 %add.3 = f32[1,2048]{1,0:T(1,128)} add(f32[1,2048]{1,0:T(1,128)S(1)} %get-tuple-element.49, f32[1,2048]{1,0:T(1,128)S(1)} %collective-permute-done) | non-fusion elementwise | flops 2048 | bytes 24576 | tf_op jit(solution)/shard_map/add | solution.py:591
Async XLA Ops:
  34.9 20.9 %collective-permute-start = (f32[1,2048]{1,0:T(1,128)S(1)}, f32[1,2048]{1,0:T(1,128)S(1)}, u32[]{:S(2)}, u32[]{:S(2)}) collective-permute-start(f32[1,2048]{1,0:T(1,128)S(1)} %get-tuple-element.49), channel_id=1, source_target_pairs={{0,128},{128,0},{1,129},{129,1},{2,130},{130,2},{3,131},{131,3},{4... | collective-permute-start | bytes 24584 | tf_op jit(solution)/shard_map/ppermute | solution.py:577

commit v4 on v2

--- a/solution.py
+++ b/solution.py
@@ -74,42 +74,47 @@
 def local_kernel(
     feat_hbm, taste_hbm, price_hbm, alpha_hbm, size_hbm, lam_hbm, store_hbm, rho_hbm, par_hbm, avail_hbm, mem_hbm,
     cot_hbm,
-    ms_ref, wh_ref, wl_ref, cotm_ref, sums, peaks, table, table_t, cols, rows_ref, rho_rows, ids_ref, inv_ref,
+    ms_ref, wh_ref, wl_ref, cot_ref, sums, peaks, table, table_t, cols, rows_ref, rho_rows, ids_ref, inv_ref,
     feat, taste, price, lam_row, store_row, rho_row, par_row, avail, size, worst,
-    small_sem, big_sem, avail_sem, cot_sem,
+    small_sem, feat_sem, taste_sem, avail_sem, cot_sem,
 ):
     subs = lam_row.shape[1]
     cats = rho_row.shape[1]
     width = ids_ref.shape[1]
     blocks = ms_ref.shape[0] // LANES
     tiles = width // LANES
+    chunks = width // CHUNK
     small = [
-        (mem_hbm, ids_ref), (lam_hbm, lam_row), (price_hbm, price), (store_hbm, store_row), (rho_hbm, rho_row),
-        (par_hbm, par_row), (alpha_hbm, rows_ref.at[0:1]), (size_hbm, size),
+        (mem_hbm, ids_ref), (lam_hbm, lam_row), (price_hbm, price), (alpha_hbm, rows_ref.at[0:1]),
+        (store_hbm, store_row), (rho_hbm, rho_row), (par_hbm, par_row), (size_hbm, size),
     ]
     small = [pltpu.make_async_copy(src, dst, small_sem.at[k]) for k, (src, dst) in enumerate(small)]
-    big = [
-        pltpu.make_async_copy(src, dst, big_sem.at[k])
-        for k, (src, dst) in enumerate([(feat_hbm, feat), (taste_hbm, taste)])
-    ]
+    whole_feat = pltpu.make_async_copy(feat_hbm, feat, feat_sem)
+    whole_cot = pltpu.make_async_copy(cot_hbm, cot_ref, cot_sem)
+    tastes = []
+    for k in range(chunks):
+        at = pl.ds(k * CHUNK, CHUNK)
+        tastes.append(pltpu.make_async_copy(taste_hbm.at[:, at], taste.at[:, at], taste_sem.at[k]))
 
     def fetch(b):
         rows = pl.ds(pl.multiple_of(b * LANES, LANES), LANES)
-        return (
-            pltpu.make_async_copy(avail_hbm.at[rows, 0, :], avail.at[rows], avail_sem.at[b]),
-            pltpu.make_async_copy(cot_hbm.at[rows], cotm_ref.at[rows], cot_sem.at[b]),
-        )
-
-    for copy in small + big:
+        return pltpu.make_async_copy(avail_hbm.at[rows, 0, :], avail.at[rows], avail_sem.at[b])
+
+    for copy in small:
         copy.start()
-    for b in range(blocks):
-        for copy in fetch(b):
-            copy.start()
+    whole_feat.start()
+    tastes[0].start()
+    fetch(0).start()
+    for copy in tastes[1:]:
+        copy.start()
+    for b in range(1, blocks):
+        fetch(b).start()
+    whole_cot.start()
     for copy in small:
         copy.wait()
 
     lam = column(lam_row[...])
-    for k in range(width // CHUNK):
+    for k in range(chunks):
         at = pl.ds(k * CHUNK, CHUNK)
         hit = iota((subs, CHUNK), 0) == ids_ref[:, at]
         ones = jnp.where(hit, 1.0, 0.0)
@@ -118,6 +123,39 @@
         inv = 1.0 / jnp.sum(jnp.where(hit, lam, 0.0), axis=0, keepdims=True)
         inv_ref[0:1, at] = inv
         inv_ref[1:2, at] = inv * price[:, at]
+    worst[...] = jnp.zeros_like(worst)
+
+    def block(b, mine, arrive):
+        fetch(b).wait()
+        alpha = jnp.transpose(jnp.broadcast_to(rows_ref[0:1, mine], (LANES, LANES)))
+        alpha2 = jnp.concatenate([alpha, alpha], axis=1)
+        total = jnp.zeros((LANES, subs), F32)
+        most = jnp.zeros((8, CHUNK), F32)
+        for k in range(chunks):
+            at = pl.ds(k * CHUNK, CHUNK)
+            if arrive:
+                tastes[k].wait()
+            util = dot(feat[mine, :], taste[:, at])
+            scaled = util * inv_ref[0:1, at] - alpha2 * inv_ref[1:2, at]
+            masked = jnp.where(avail[mine, at] == 1, scaled, NEG)
+            ms_ref[mine, at] = masked
+            most = jnp.maximum(most, jnp.max(jnp.abs(scaled).reshape(LANES // 8, 8, CHUNK), axis=0))
+            wh, wl = halves(jnp.exp(masked))
+            wh_ref[mine, at] = wh
+            wl_ref[mine, at] = wl
+            hits = table_t[at, :]
+            total = total + dot(jnp.concatenate([wh, wl], axis=1), jnp.concatenate([hits, hits], axis=0))
+        sums[:, mine] = jnp.transpose(total)
+        worst[...] = jnp.maximum(worst[...], most)
+
+    whole_feat.wait()
+    block(0, pl.ds(0, LANES), True)
+
+    @pl.loop(1, blocks)
+    def _(b):
+        block(b, pl.ds(pl.multiple_of(b * LANES, LANES), LANES), False)
+
+    peaks[...] = jnp.zeros_like(peaks)
     _, ilam, store, par, irho = nest_columns(lam_row, store_row, rho_row, par_row)
     for k, col in enumerate((lam, store, par, irho, ilam)):
         cols[k] = jnp.broadcast_to(col, (subs, LANES))
@@ -125,35 +163,7 @@
     rho_rows[0:8, :] = jnp.where(iota((8, LANES), 1) < LANES // 2, rho[0:8], rho[8:16])
     rho_rows[8:24, :] = rho
     rows_ref[1:2, :] = jnp.log(size[...])
-    worst[...] = jnp.zeros_like(worst)
-    peaks[...] = jnp.zeros_like(peaks)
-    for copy in big:
-        copy.wait()
-
-    @pl.loop(0, blocks)
-    def _(b):
-        mine = pl.ds(pl.multiple_of(b * LANES, LANES), LANES)
-        for copy in fetch(b):
-            copy.wait()
-        alpha = jnp.transpose(jnp.broadcast_to(rows_ref[0:1, mine], (LANES, LANES)))
-        alpha2 = jnp.concatenate([alpha, alpha], axis=1)
-        total = jnp.zeros((2 * LANES, subs), F32)
-        most = jnp.zeros((8, CHUNK), F32)
-        for k in range(width // CHUNK):
-            at = pl.ds(k * CHUNK, CHUNK)
-            util = dot(feat[mine, :], taste[:, at])
-            scaled = util * inv_ref[0:1, at] - alpha2 * inv_ref[1:2, at]
-            open_ = avail[mine, at]
-            masked = jnp.where(open_ == 1, scaled, NEG)
-            ms_ref[mine, at] = masked
-            most = jnp.maximum(most, jnp.max(jnp.abs(scaled).reshape(LANES // 8, 8, CHUNK), axis=0))
-            wh, wl = halves(jnp.exp(masked))
-            wh_ref[mine, at] = wh
-            wl_ref[mine, at] = wl
-            cotm_ref[mine, at] = cotm_ref[mine, at] * open_.astype(F32).astype(BF16)
-            total = total + dot(jnp.concatenate([wh, wl], axis=0), table_t[at, :])
-        sums[:, mine] = jnp.transpose(total[:LANES] + total[LANES:])
-        worst[...] = jnp.maximum(worst[...], most)
+    whole_cot.wait()
 
     @pl.when(jnp.max(worst[...]) > SAFE)
     def _():
@@ -197,11 +207,14 @@
             sums[:, mine] = jnp.transpose(total[:LANES] + total[LANES:])
 
 
-def condense(b, sums, peaks, cotm_ref, table_t, cols, ids_ref, part_ref, left_ref, right_ref, lst_ref, c_ref):
+def condense(b, sums, peaks, ms_ref, cot_ref, cotm_ref, table_t, cols, ids_ref, part_ref, left_ref, right_ref, lst_ref, c_ref):
     cats = 16
     subs = sums.shape[0]
     width = ids_ref.shape[1]
     mine = pl.ds(b * LANES, LANES)
+    for k in range(width // CHUNK):
+        at = pl.ds(k * CHUNK, CHUNK)
+        cotm_ref[mine, at] = cot_ref[mine, at] * jnp.where(ms_ref[mine, at] > EMPTY, 1.0, 0.0).astype(BF16)
     total = sums[:, mine]
     raw = jnp.where(total > 0.0, peaks[:, mine] + jnp.log(jnp.where(total > 0.0, total, 1.0)), NEG)
     lam, store, par, irho = cols[0], cols[1], cols[2], cols[3]
@@ -259,7 +272,7 @@
     left = iota((count, LANES), 1) < LANES // 2
     front, back = [], []
     for k in range(4):
-        line = jnp.concatenate([buf[d, 16 + k : 17 + k, :] for d in range(count)], axis=0)
+        line = buf[pl.ds(16 + k, count, stride=24), :]
         other = turn(line)
         front.append(jnp.where(left, line, other))
         back.append(jnp.where(left, other, line))
@@ -277,7 +290,7 @@
         last = jnp.where(first_id == last_id, NEG, last)
     here = iota((8, LANES), 0) + jnp.where(iota((8, LANES), 1) < LANES // 2, 0, 8)
     here = here.astype(F32)
-    parts = [buf[d, 0:8, :] for d in range(count)]
+    parts = [buf[24 * d : 24 * d + 8, :] for d in range(count)]
     for d in range(count):
         if d > 0 or not inner:
             parts.append(jnp.where(first_cat[d : d + 1] == here, first[d : d + 1], NEG))
@@ -285,13 +298,13 @@
             parts.append(jnp.where(last_cat[d : d + 1] == here, last[d : d + 1], NEG))
     top = functools.reduce(jnp.maximum, parts)
     logs = top + jnp.log(sum(jnp.exp(part - top) for part in parts))
-    return logs, sum(buf[d, 8:16, :] for d in range(count))
+    return logs, sum(buf[24 * d + 8 : 24 * d + 16, :] for d in range(count))
 
 
 def swap_kernel(
-    ny, nz, nx, sums, peaks, cotm_ref, table_t, cols, rows_ref, rho_ref, ids_ref, inv_ref,
+    ny, nz, nx, sums, peaks, ms_ref, cot_ref, table_t, cols, rows_ref, rho_ref, ids_ref, inv_ref,
     cv_ref, top_ref, nbl_ref, nbr_ref, left_ref, right_ref, lst_ref, c_ref, cg_ref,
-    part_ref, zbuf, line, ybuf, xsrc, xbuf, values, tops,
+    cotm_ref, part_ref, zbuf, line, ybuf, xsrc, xbuf, values, tops,
     nb_send, nb_recv, z_send, z_recv, y_send, y_recv, x_send, x_recv, g_send, g_recv, t_send, t_recv,
 ):
     sku = lax.axis_index("sku")
@@ -310,7 +323,10 @@
     for other in along_x:
         pl.semaphore_signal(barrier, inc=1, device_id={"cat": other}, device_id_type=MESH)
     for b in range(left_ref.shape[0]):
-        condense(b, sums, peaks, cotm_ref, table_t, cols, ids_ref, part_ref, left_ref, right_ref, lst_ref, c_ref)
+        condense(
+            b, sums, peaks, ms_ref, cot_ref, cotm_ref, table_t, cols, ids_ref, part_ref, left_ref, right_ref, lst_ref,
+            c_ref,
+        )
     pl.semaphore_wait(barrier, nz + ny + nx - 1)
 
     def send(src, dst, send_sem, recv_sem, device):
@@ -321,15 +337,19 @@
         return copy
 
     used = pl.ds(0, ROWS)
+
+    def slot(k, size):
+        return pl.ds(pl.multiple_of(k * 24, 8), size)
+
     by_z = [
-        send(part_ref.at[next_z[k], used], zbuf.at[z, used], z_send.at[k], z_recv.at[k], {"sku": other})
+        send(part_ref.at[next_z[k], used], zbuf.at[slot(z, ROWS)], z_send.at[k], z_recv.at[k], {"sku": other})
         for k, other in enumerate(along_z)
     ]
     near = [
         send(right_ref, nbl_ref, nb_send.at[0], nb_recv.at[0], {"sku": to_right}),
         send(left_ref, nbr_ref, nb_send.at[1], nb_recv.at[1], {"sku": to_left}),
     ]
-    zbuf[z] = part_ref[z]
+    zbuf[slot(z, 24), :] = part_ref[z]
     ah, al = halves(rows_ref[0:1, :])
     pick = iota((16, ah.shape[1]), 0)
     weights = jnp.where(pick == 0, ah.astype(F32), jnp.where(pick == 1, al.astype(F32), 0.0)).astype(BF16)
@@ -340,7 +360,7 @@
         copy.wait_recv()
 
     line[0:8, :], line[8:16, :] = join(zbuf, nz, True, True)
-    begin, end = zbuf[0, 16:24, :], zbuf[nz - 1, 16:24, :]
+    begin, end = zbuf[16:24, :], zbuf[24 * nz - 8 : 24 * nz, :]
     row, left = iota((8, LANES), 0), iota((8, LANES), 1) < LANES // 2
     from_begin = (row == 2) | (left & ((row == 0) | (row == 3)))
     one = end[3:4] == turn(end)[0:1]
@@ -348,10 +368,10 @@
     line[16:24, :] = jnp.where(from_begin, begin, end)
 
     by_y = [
-        send(line.at[used], ybuf.at[y, used], y_send.at[k], y_recv.at[k], {"sku": other})
+        send(line.at[used], ybuf.at[slot(y, ROWS)], y_send.at[k], y_recv.at[k], {"sku": other})
         for k, other in enumerate(along_y)
     ]
-    ybuf[y] = line[...]
+    ybuf[slot(y, 24), :] = line[...]
     for copy in by_y:
         copy.wait_recv()
     logs, cot = join(ybuf, ny, False, False)
@@ -432,15 +452,18 @@
         grad_ref[:, at] = -(jnp.sum(jnp.where(hit, found, 0.0), axis=0, keepdims=True) + cg_ref[:, at])
 
 
+ROW_BLOCK = 64
+
+
 def demand_kernel(ms_ref, path_ref, table, out_hbm, value_ref, sem):
     markets, width = ms_ref.shape
 
     def flush(b):
-        rows = pl.ds(b * LANES, LANES)
+        rows = pl.ds(b * ROW_BLOCK, ROW_BLOCK)
         return pltpu.make_async_copy(value_ref.at[rows], out_hbm.at[rows, 0, :], sem.at[b])
 
-    for b in range(markets // LANES):
-        rows = pl.ds(b * LANES, LANES)
+    for b in range(markets // ROW_BLOCK):
+        rows = pl.ds(b * ROW_BLOCK, ROW_BLOCK)
         for k in range(width // CHUNK):
             at = pl.ds(k * CHUNK, CHUNK)
             masked = ms_ref[rows, at]
@@ -448,7 +471,7 @@
             path = dot(path_ref[rows, :], jnp.concatenate([hits, hits], axis=0))
             value_ref[rows, at] = jnp.where(masked > EMPTY, masked + path, 0.0)
         flush(b).start()
-    for b in range(markets // LANES):
+    for b in range(markets // ROW_BLOCK):
         flush(b).wait()
 
 
@@ -481,7 +504,7 @@
     operands = [pltpu.with_memory_space_constraint(x, pltpu.HBM) for x in operands]
     sds = jax.ShapeDtypeStruct
     vmem, dma = pltpu.VMEM, pltpu.SemaphoreType.DMA
-    ms, wh, wl, cotm, sums, peaks, table, table_t, cols, rows, rho_rows, ids, inv = pl.pallas_call(
+    ms, wh, wl, cot, sums, peaks, table, table_t, cols, rows, rho_rows, ids, inv = pl.pallas_call(
         local_kernel,
         in_specs=[pl.BlockSpec(memory_space=pl.ANY)] * 12,
         out_specs=[whole()] * 13,
@@ -512,9 +535,10 @@
             vmem((1, markets), F32),
             vmem((8, CHUNK), F32),
             dma((8,)),
-            dma((2,)),
+            dma,
+            dma((width // CHUNK,)),
             dma((blocks,)),
-            dma((blocks,)),
+            dma,
         ],
         compiler_params=pltpu.CompilerParams(vmem_limit_bytes=32 * 1024 * 1024),
         name="local_nests",
@@ -524,17 +548,18 @@
     ny = n_sku // nz
     cv, top, nbl, nbr, left, right, lst, c, cg = pl.pallas_call(
         functools.partial(swap_kernel, ny, nz, n_cat),
-        in_specs=[whole()] * 9,
+        in_specs=[whole()] * 10,
         out_specs=[whole()] * 9,
         out_shape=[sds((nz, 16, LANES), F32), sds((nz, 8, LANES), F32)]
         + [sds((blocks, 8, LANES), F32)] * 4
         + [sds((subs, markets), F32)] * 2
         + [sds((1, width), F32)],
         scratch_shapes=[
+            vmem((markets, width), BF16),
             vmem((nz, 24, LANES), F32),
-            vmem((nz, 24, LANES), F32),
+            vmem((nz * 24, LANES), F32),
             vmem((24, LANES), F32),
-            vmem((ny, 24, LANES), F32),
+            vmem((ny * 24, LANES), F32),
             vmem((8, LANES), F32),
             vmem((n_cat - 1, 8, LANES), F32),
             vmem((16, LANES), F32),
@@ -545,7 +570,7 @@
             collective_id=0, has_side_effects=True, vmem_limit_bytes=16 * 1024 * 1024
         ),
         name="swap_nests",
-    )(sums, peaks, cotm, table_t, cols, rows, rho_rows, ids, inv)
+    )(sums, peaks, ms, cot, table_t, cols, rows, rho_rows, ids, inv)
 
     grad, path = pl.pallas_call(
         slope_kernel,
@@ -563,7 +588,7 @@
         in_specs=[whole()] * 3,
         out_specs=pl.BlockSpec(memory_space=pl.ANY),
         out_shape=sds((markets, 1, width), F32),
-        scratch_shapes=[vmem((markets, width), F32), dma((blocks,))],
+        scratch_shapes=[vmem((markets, width), F32), dma((markets // ROW_BLOCK,))],
         compiler_params=pltpu.CompilerParams(vmem_limit_bytes=16 * 1024 * 1024),
         cost_estimate=pl.CostEstimate(
             flops=2 * markets * width * 2 * subs, bytes_accessed=8 * markets * width, transcendentals=0

time: 55.4 us -> 57.7 us (1.042)
  Pallas kernels: 35.8 us -> 38.2 us
    pallas_call x1, Pallas kernels: 7.24 us -> 8.65 us  [shards(): pl.pallas_call(local_kernel, in_specs=[pl.BlockSpec(memory_space=pl.ANY)]...]
    pallas_call x1, Pallas kernels: 2.35 us -> 3.27 us  [shards(): pl.pallas_call(demand_kernel, in_specs=[whole()] * 3, out_specs=pl.BlockS...]
  transfers between devices with their start and end apart: 1 -> 1, of which waited for: 0 -> 0; matrix products, arithmetic and copies ran while one was open for 0% -> 0% of each run, Pallas kernels for 4% -> 6%
where the time goes in v4:
time: 57.7 us; the launch traced here: 57.6 us
  Pallas kernels  38.2 us (66%)
  starting transfers between devices  18.2 us (32%)
  between operations  0.67 us (1%)
  other arithmetic  0.61 us (1%)
    pallas_call x1, Pallas kernels, shards(): pl.pallas_call(functools.partial(swap_kernel, ny, nz, n_cat), in_specs=[w...  24.8 us
    ppermute x1, starting transfers between devices, shards(): other = lax.ppermute(grad, 'mkt', [(0, 1), (1, 0)])  18.2 us
    pallas_call x1, Pallas kernels, shards(): pl.pallas_call(local_kernel, in_specs=[pl.BlockSpec(memory_space=pl.ANY)]...  8.65 us
    pallas_call x1, Pallas kernels, shards(): pl.pallas_call(demand_kernel, in_specs=[whole()] * 3, out_specs=pl.BlockS...  3.27 us
    pallas_call x1, Pallas kernels, shards(): pl.pallas_call(slope_kernel, in_specs=[whole()] * 16, out_specs=[whole()]...  1.44 us
  transfers between devices with their start and end apart: 1, of which 0 were waited for; matrix products, arithmetic and copies ran while one was open for 0% of the time, Pallas kernels for 6%

profile of v4, /device:TPU:1, one launch (start us, length us, event | category | flops | bytes accessed | tf_op | source)
XLA Modules:
  0.0 57.6 jit_solution(9649576134101603080)
XLA Ops:
  0.6 8.7 %local_nests.1 = (f32[512,2048]{1,0:T(8,128)S(1)}, bf16[512,2048]{1,0:T(8,128)(2,1)S(1)}, bf16[512,2048]{1,0:T(8,128)(2,1)S(1)}, bf16[512,2048]{1,0:T(8,128)(2,1...) custom-call(bf16[512,512]{1,0:T(8,128)(2,1)} %feat_hbm.1, ...), custom_call_target="tpu_custom_call" | custom-call | tf_op jit(solution)/shard_map/local_nests/pallas_call | solution.py:507
  9.3 24.8 %swap_nests.1 = (f32[8,16,128]{2,1,0:T(8,128)S(1)}, f32[8,8,128]{2,1,0:T(8,128)S(1)}, f32[4,8,128]{2,1,0:T(8,128)S(1)}, f32[4,8,128]{2,1,0:T(8,128)S(1)}, f32[4,...) custom-call(f32[128,512]{1,0:T(8,128)S(1)} %get-tuple-element.29.sum, ...), custom_call_target="tpu_custom_call" | custom-call | tf_op jit(solution)/shard_map/swap_nests/pallas_call | solution.py:549
  34.1 1.4 %price_slope.1 = (f32[1,2048]{1,0:T(1,128)S(1)}, bf16[512,256]{1,0:T(8,128)(2,1)S(1)}) custom-call(bf16[512,2048]{1,0:T(8,128)(2,1)S(1)} %get-tuple-element.27.wh_ref, bf16[512,2048]{1,0:T(8,128)(2,1)S(1)} %get-tuple-element.28.wl_ref, f32[128,512]{1,0:T(8,128)S(1)} %get-tuple-element.38.lst_ref, f32[128,512]{1,0:T(8,128)S(1)} %get-tuple-element.30.peaks.r_ref, ...), custom_call_target="tpu_custom_call" | custom-call | tf_op jit(solution)/shard_map/price_slope/pallas_call | solution.py:575
  35.5 18.2 %collective-permute-start = (f32[1,2048]{1,0:T(1,128)S(1)}, f32[1,2048]{1,0:T(1,128)S(1)}, u32[]{:S(2)}, u32[]{:S(2)}) collective-permute-start(f32[1,2048]{1,0:T(1,128)S(1)} %get-tuple-element.49), channel_id=1, source_target_pairs={{0,128},{128,0},{1,129},{129,1},{2,130},{130,2},{3,131},{131,3},{4... | collective-permute-start | bytes 24584 | tf_op jit(solution)/shard_map/ppermute | solution.py:584
  53.7 3.3 %log_demand.1 = f32[512,1,2048]{2,1,0:T(1,128)} custom-call(f32[512,2048]{1,0:T(8,128)S(1)} %get-tuple-element.26.ms_ref, bf16[512,256]{1,0:T(8,128)(2,1)S(1)} %get-tuple-element.47.path_ref, bf16[128,2048]{1,0:T(8,128)(2,1)S(1)} %get-tuple-element.48.table), custom_call_target="tpu_custom_call" | custom-call | flops 536870912 | bytes 8388608 | tf_op jit(solution)/shard_map/log_demand/pallas_call | solution.py:586
  57.0 0.0 collective-permute-done
  57.0 0.6 %add.3 = f32[1,2048]{1,0:T(1,128)} add(f32[1,2048]{1,0:T(1,128)S(1)} %get-tuple-element.49, f32[1,2048]{1,0:T(1,128)S(1)} %collective-permute-done) | non-fusion elementwise | flops 2048 | bytes 24576 | tf_op jit(solution)/shard_map/add | solution.py:598
Async XLA Ops:
  35.5 21.4 %collective-permute-start = (f32[1,2048]{1,0:T(1,128)S(1)}, f32[1,2048]{1,0:T(1,128)S(1)}, u32[]{:S(2)}, u32[]{:S(2)}) collective-permute-start(f32[1,2048]{1,0:T(1,128)S(1)} %get-tuple-element.49), channel_id=1, source_target_pairs={{0,128},{128,0},{1,129},{129,1},{2,130},{130,2},{3,131},{131,3},{4... | collective-permute-start | bytes 24584 | tf_op jit(solution)/shard_map/ppermute | solution.py:584

commit v5 on v4

--- a/solution.py
+++ b/solution.py
@@ -125,35 +125,32 @@
         inv_ref[1:2, at] = inv * price[:, at]
     worst[...] = jnp.zeros_like(worst)
 
-    def block(b, mine, arrive):
+    whole_feat.wait()
+    for k in range(chunks):
+        at = pl.ds(k * CHUNK, CHUNK)
+        tastes[k].wait()
+        ms_ref[:, at] = dot(feat[...], taste[:, at])
+
+    @pl.loop(0, blocks)
+    def _(b):
+        mine = pl.ds(pl.multiple_of(b * LANES, LANES), LANES)
         fetch(b).wait()
         alpha = jnp.transpose(jnp.broadcast_to(rows_ref[0:1, mine], (LANES, LANES)))
         alpha2 = jnp.concatenate([alpha, alpha], axis=1)
-        total = jnp.zeros((LANES, subs), F32)
+        total = jnp.zeros((2 * LANES, subs), F32)
         most = jnp.zeros((8, CHUNK), F32)
         for k in range(chunks):
             at = pl.ds(k * CHUNK, CHUNK)
-            if arrive:
-                tastes[k].wait()
-            util = dot(feat[mine, :], taste[:, at])
-            scaled = util * inv_ref[0:1, at] - alpha2 * inv_ref[1:2, at]
+            scaled = ms_ref[mine, at] * inv_ref[0:1, at] - alpha2 * inv_ref[1:2, at]
             masked = jnp.where(avail[mine, at] == 1, scaled, NEG)
             ms_ref[mine, at] = masked
             most = jnp.maximum(most, jnp.max(jnp.abs(scaled).reshape(LANES // 8, 8, CHUNK), axis=0))
             wh, wl = halves(jnp.exp(masked))
             wh_ref[mine, at] = wh
             wl_ref[mine, at] = wl
-            hits = table_t[at, :]
-            total = total + dot(jnp.concatenate([wh, wl], axis=1), jnp.concatenate([hits, hits], axis=0))
-        sums[:, mine] = jnp.transpose(total)
+            total = total + dot(jnp.concatenate([wh, wl], axis=0), table_t[at, :])
+        sums[:, mine] = jnp.transpose(total[:LANES] + total[LANES:])
         worst[...] = jnp.maximum(worst[...], most)
-
-    whole_feat.wait()
-    block(0, pl.ds(0, LANES), True)
-
-    @pl.loop(1, blocks)
-    def _(b):
-        block(b, pl.ds(pl.multiple_of(b * LANES, LANES), LANES), False)
 
     peaks[...] = jnp.zeros_like(peaks)
     _, ilam, store, par, irho = nest_columns(lam_row, store_row, rho_row, par_row)
@@ -452,7 +449,7 @@
         grad_ref[:, at] = -(jnp.sum(jnp.where(hit, found, 0.0), axis=0, keepdims=True) + cg_ref[:, at])
 
 
-ROW_BLOCK = 64
+ROW_BLOCK = 128
 
 
 def demand_kernel(ms_ref, path_ref, table, out_hbm, value_ref, sem):

time: 57.7 us -> 56.8 us (0.984)
  Pallas kernels: 38.2 us -> 37.2 us
    pallas_call x1, Pallas kernels: 3.27 us -> 2.35 us  [shards(): pl.pallas_call(demand_kernel, in_specs=[whole()] * 3, out_specs=pl.BlockS...]
  transfers between devices with their start and end apart: 1 -> 1, of which waited for: 0 -> 0; matrix products, arithmetic and copies ran while one was open for 0% -> 0% of each run, Pallas kernels for 6% -> 4%
where the time goes in v5:
time: 56.8 us; the launch traced here: 56.6 us
  Pallas kernels  37.2 us (65%)
  starting transfers between devices  18.2 us (32%)
  between operations  0.67 us (1%)
  other arithmetic  0.61 us (1%)
    pallas_call x1, Pallas kernels, shards(): pl.pallas_call(functools.partial(swap_kernel, ny, nz, n_cat), in_specs=[w...  24.8 us
    ppermute x1, starting transfers between devices, shards(): other = lax.ppermute(grad, 'mkt', [(0, 1), (1, 0)])  18.2 us
    pallas_call x1, Pallas kernels, shards(): pl.pallas_call(local_kernel, in_specs=[pl.BlockSpec(memory_space=pl.ANY)]...  8.58 us
    pallas_call x1, Pallas kernels, shards(): pl.pallas_call(demand_kernel, in_specs=[whole()] * 3, out_specs=pl.BlockS...  2.35 us
    pallas_call x1, Pallas kernels, shards(): pl.pallas_call(slope_kernel, in_specs=[whole()] * 16, out_specs=[whole()]...  1.45 us
  transfers between devices with their start and end apart: 1, of which 0 were waited for; matrix products, arithmetic and copies ran while one was open for 0% of the time, Pallas kernels for 4%

profile of v5, /device:TPU:1, one launch (start us, length us, event | category | flops | bytes accessed | tf_op | source)
XLA Modules:
  0.0 56.6 jit_solution(16379397743261894905)
XLA Ops:
  0.6 8.6 %local_nests.1 = (f32[512,2048]{1,0:T(8,128)S(1)}, bf16[512,2048]{1,0:T(8,128)(2,1)S(1)}, bf16[512,2048]{1,0:T(8,128)(2,1)S(1)}, bf16[512,2048]{1,0:T(8,128)(2,1...) custom-call(bf16[512,512]{1,0:T(8,128)(2,1)} %feat_hbm.1, ...), custom_call_target="tpu_custom_call" | custom-call | tf_op jit(solution)/shard_map/local_nests/pallas_call | solution.py:504
  9.2 24.8 %swap_nests.1 = (f32[8,16,128]{2,1,0:T(8,128)S(1)}, f32[8,8,128]{2,1,0:T(8,128)S(1)}, f32[4,8,128]{2,1,0:T(8,128)S(1)}, f32[4,8,128]{2,1,0:T(8,128)S(1)}, f32[4,...) custom-call(f32[128,512]{1,0:T(8,128)S(1)} %get-tuple-element.29.sum, ...), custom_call_target="tpu_custom_call" | custom-call | tf_op jit(solution)/shard_map/swap_nests/pallas_call | solution.py:546
  34.0 1.4 %price_slope.1 = (f32[1,2048]{1,0:T(1,128)S(1)}, bf16[512,256]{1,0:T(8,128)(2,1)S(1)}) custom-call(bf16[512,2048]{1,0:T(8,128)(2,1)S(1)} %get-tuple-element.27.wh_ref, bf16[512,2048]{1,0:T(8,128)(2,1)S(1)} %get-tuple-element.28.wl_ref, f32[128,512]{1,0:T(8,128)S(1)} %get-tuple-element.38.lst_ref, f32[128,512]{1,0:T(8,128)S(1)} %get-tuple-element.30.peaks.r_ref, ...), custom_call_target="tpu_custom_call" | custom-call | tf_op jit(solution)/shard_map/price_slope/pallas_call | solution.py:572
  35.5 18.2 %collective-permute-start = (f32[1,2048]{1,0:T(1,128)S(1)}, f32[1,2048]{1,0:T(1,128)S(1)}, u32[]{:S(2)}, u32[]{:S(2)}) collective-permute-start(f32[1,2048]{1,0:T(1,128)S(1)} %get-tuple-element.49), channel_id=1, source_target_pairs={{0,128},{128,0},{1,129},{129,1},{2,130},{130,2},{3,131},{131,3},{4... | collective-permute-start | bytes 24584 | tf_op jit(solution)/shard_map/ppermute | solution.py:581
  53.7 2.4 %log_demand.1 = f32[512,1,2048]{2,1,0:T(1,128)} custom-call(f32[512,2048]{1,0:T(8,128)S(1)} %get-tuple-element.26.ms_ref, bf16[512,256]{1,0:T(8,128)(2,1)S(1)} %get-tuple-element.47.path_ref, bf16[128,2048]{1,0:T(8,128)(2,1)S(1)} %get-tuple-element.48.table), custom_call_target="tpu_custom_call" | custom-call | flops 536870912 | bytes 8388608 | tf_op jit(solution)/shard_map/log_demand/pallas_call | solution.py:583
  56.0 0.0 collective-permute-done
  56.0 0.6 %add.3 = f32[1,2048]{1,0:T(1,128)} add(f32[1,2048]{1,0:T(1,128)S(1)} %get-tuple-element.49, f32[1,2048]{1,0:T(1,128)S(1)} %collective-permute-done) | non-fusion elementwise | flops 2048 | bytes 24576 | tf_op jit(solution)/shard_map/add | solution.py:595
Async XLA Ops:
  35.5 20.5 %collective-permute-start = (f32[1,2048]{1,0:T(1,128)S(1)}, f32[1,2048]{1,0:T(1,128)S(1)}, u32[]{:S(2)}, u32[]{:S(2)}) collective-permute-start(f32[1,2048]{1,0:T(1,128)S(1)} %get-tuple-element.49), channel_id=1, source_target_pairs={{0,128},{128,0},{1,129},{129,1},{2,130},{130,2},{3,131},{131,3},{4... | collective-permute-start | bytes 24584 | tf_op jit(solution)/shard_map/ppermute | solution.py:581

commit v6 on v4

--- a/solution.py
+++ b/solution.py
@@ -71,12 +71,23 @@
     return pltpu.roll(x, LANES // 2, 1)
 
 
+WINDOW = 32
+
+
+def reach(ids):
+    ends = ids.astype(F32)
+    first = jnp.min(ends[:, :LANES]).astype(jnp.int32)
+    last = jnp.max(ends[:, ends.shape[1] - LANES :]).astype(jnp.int32)
+    base = jnp.minimum(first // 8 * 8, LANES - WINDOW)
+    return pl.multiple_of(base, 8), last < base + WINDOW
+
+
 def local_kernel(
     feat_hbm, taste_hbm, price_hbm, alpha_hbm, size_hbm, lam_hbm, store_hbm, rho_hbm, par_hbm, avail_hbm, mem_hbm,
     cot_hbm,
-    ms_ref, wh_ref, wl_ref, cot_ref, sums, peaks, table, table_t, cols, rows_ref, rho_rows, ids_ref, inv_ref,
-    feat, taste, price, lam_row, store_row, rho_row, par_row, avail, size, worst,
-    small_sem, feat_sem, taste_sem, avail_sem, cot_sem,
+    ms_ref, wh_ref, wl_ref, cot_ref, sums, peaks, table, cols, rows_ref, rho_rows, ids_ref, inv_ref,
+    feat, taste, price, lam_row, store_row, rho_row, par_row, avail, size, worst, near,
+    small_sem, big_sem, avail_sem, cot_sem,
 ):
     subs = lam_row.shape[1]
     cats = rho_row.shape[1]
@@ -89,23 +100,17 @@
         (store_hbm, store_row), (rho_hbm, rho_row), (par_hbm, par_row), (size_hbm, size),
     ]
     small = [pltpu.make_async_copy(src, dst, small_sem.at[k]) for k, (src, dst) in enumerate(small)]
-    whole_feat = pltpu.make_async_copy(feat_hbm, feat, feat_sem)
+    big = [
+        pltpu.make_async_copy(src, dst, big_sem.at[k])
+        for k, (src, dst) in enumerate([(taste_hbm, taste), (feat_hbm, feat)])
+    ]
     whole_cot = pltpu.make_async_copy(cot_hbm, cot_ref, cot_sem)
-    tastes = []
-    for k in range(chunks):
-        at = pl.ds(k * CHUNK, CHUNK)
-        tastes.append(pltpu.make_async_copy(taste_hbm.at[:, at], taste.at[:, at], taste_sem.at[k]))
 
     def fetch(b):
         rows = pl.ds(pl.multiple_of(b * LANES, LANES), LANES)
         return pltpu.make_async_copy(avail_hbm.at[rows, 0, :], avail.at[rows], avail_sem.at[b])
 
-    for copy in small:
-        copy.start()
-    whole_feat.start()
-    tastes[0].start()
-    fetch(0).start()
-    for copy in tastes[1:]:
+    for copy in small[:3] + big + [fetch(0)] + small[3:]:
         copy.start()
     for b in range(1, blocks):
         fetch(b).start()
@@ -113,28 +118,39 @@
     for copy in small:
         copy.wait()
 
+    base, narrow = reach(ids_ref[...])
     lam = column(lam_row[...])
     for k in range(chunks):
         at = pl.ds(k * CHUNK, CHUNK)
         hit = iota((subs, CHUNK), 0) == ids_ref[:, at]
-        ones = jnp.where(hit, 1.0, 0.0)
-        table[:, at] = ones.astype(BF16)
-        table_t[at, :] = jnp.transpose(ones).astype(BF16)
+        table[:, at] = jnp.where(hit, 1.0, 0.0).astype(BF16)
+        near[:, at] = jnp.where(iota((WINDOW, CHUNK), 0) + base == ids_ref[:, at], 1.0, 0.0).astype(BF16)
         inv = 1.0 / jnp.sum(jnp.where(hit, lam, 0.0), axis=0, keepdims=True)
         inv_ref[0:1, at] = inv
         inv_ref[1:2, at] = inv * price[:, at]
     worst[...] = jnp.zeros_like(worst)
-
-    def block(b, mine, arrive):
+    sums[...] = jnp.zeros_like(sums)
+    peaks[...] = jnp.zeros_like(peaks)
+    _, ilam, store, par, irho = nest_columns(lam_row, store_row, rho_row, par_row)
+    for k, col in enumerate((lam, store, par, irho, ilam)):
+        cols[k] = jnp.broadcast_to(col, (subs, LANES))
+    rho = jnp.broadcast_to(column(rho_row[...]), (cats, LANES))
+    rho_rows[0:8, :] = jnp.where(iota((8, LANES), 1) < LANES // 2, rho[0:8], rho[8:16])
+    rho_rows[8:24, :] = rho
+    rows_ref[1:2, :] = jnp.log(size[...])
+    for copy in big:
+        copy.wait()
+
+    @pl.loop(0, blocks)
+    def _(b):
+        mine = pl.ds(pl.multiple_of(b * LANES, LANES), LANES)
         fetch(b).wait()
         alpha = jnp.transpose(jnp.broadcast_to(rows_ref[0:1, mine], (LANES, LANES)))
         alpha2 = jnp.concatenate([alpha, alpha], axis=1)
-        total = jnp.zeros((LANES, subs), F32)
+        total = jnp.zeros((WINDOW, 2 * LANES), F32)
         most = jnp.zeros((8, CHUNK), F32)
         for k in range(chunks):
             at = pl.ds(k * CHUNK, CHUNK)
-            if arrive:
-                tastes[k].wait()
             util = dot(feat[mine, :], taste[:, at])
             scaled = util * inv_ref[0:1, at] - alpha2 * inv_ref[1:2, at]
             masked = jnp.where(avail[mine, at] == 1, scaled, NEG)
@@ -143,26 +159,17 @@
             wh, wl = halves(jnp.exp(masked))
             wh_ref[mine, at] = wh
             wl_ref[mine, at] = wl
-            hits = table_t[at, :]
-            total = total + dot(jnp.concatenate([wh, wl], axis=1), jnp.concatenate([hits, hits], axis=0))
-        sums[:, mine] = jnp.transpose(total)
+            total = total + dot_nt(near[:, at], jnp.concatenate([wh, wl], axis=0))
+        sums[pl.ds(base, WINDOW), mine] = total[:, :LANES] + total[:, LANES:]
         worst[...] = jnp.maximum(worst[...], most)
 
-    whole_feat.wait()
-    block(0, pl.ds(0, LANES), True)
-
-    @pl.loop(1, blocks)
-    def _(b):
-        block(b, pl.ds(pl.multiple_of(b * LANES, LANES), LANES), False)
-
-    peaks[...] = jnp.zeros_like(peaks)
-    _, ilam, store, par, irho = nest_columns(lam_row, store_row, rho_row, par_row)
-    for k, col in enumerate((lam, store, par, irho, ilam)):
-        cols[k] = jnp.broadcast_to(col, (subs, LANES))
-    rho = jnp.broadcast_to(column(rho_row[...]), (cats, LANES))
-    rho_rows[0:8, :] = jnp.where(iota((8, LANES), 1) < LANES // 2, rho[0:8], rho[8:16])
-    rho_rows[8:24, :] = rho
-    rows_ref[1:2, :] = jnp.log(size[...])
+    @pl.when(jnp.logical_not(narrow))
+    def _():
+        @pl.loop(0, blocks)
+        def _(b):
+            mine = pl.ds(pl.multiple_of(b * LANES, LANES), LANES)
+            sums[:, mine] = dot_nt(table[...], wh_ref[mine, :]) + dot_nt(table[...], wl_ref[mine, :])
+
     whole_cot.wait()
 
     @pl.when(jnp.max(worst[...]) > SAFE)
@@ -197,17 +204,17 @@
             peak = jnp.where(peak < EMPTY, 0.0, peak)
             peaks[:, mine] = jnp.transpose(peak)
             peak_half = peak.astype(BF16)
-            total = jnp.zeros((2 * LANES, subs), F32)
+            total = jnp.zeros((subs, 2 * LANES), F32)
             for t in range(tiles):
                 at = pl.ds(t * LANES, LANES)
                 wh, wl = halves(jnp.exp(ms_ref[mine, at] - dot(peak_half, table[:, at])))
                 wh_ref[mine, at] = wh
                 wl_ref[mine, at] = wl
-                total = total + dot(jnp.concatenate([wh, wl], axis=0), table_t[at, :])
-            sums[:, mine] = jnp.transpose(total[:LANES] + total[LANES:])
-
-
-def condense(b, sums, peaks, ms_ref, cot_ref, cotm_ref, table_t, cols, ids_ref, part_ref, left_ref, right_ref, lst_ref, c_ref):
+                total = total + dot_nt(table[:, at], jnp.concatenate([wh, wl], axis=0))
+            sums[:, mine] = total[:, :LANES] + total[:, LANES:]
+
+
+def condense(b, sums, peaks, ms_ref, cot_ref, cotm_ref, table, cols, ids_ref, part_ref, left_ref, right_ref, lst_ref, c_ref):
     cats = 16
     subs = sums.shape[0]
     width = ids_ref.shape[1]
@@ -218,7 +225,7 @@
     total = sums[:, mine]
     raw = jnp.where(total > 0.0, peaks[:, mine] + jnp.log(jnp.where(total > 0.0, total, 1.0)), NEG)
     lam, store, par, irho = cols[0], cols[1], cols[2], cols[3]
-    cot_total = jnp.transpose(dot(cotm_ref[mine, :], table_t[...]))
+    cot_total = dot_nt(table[...], cotm_ref[mine, :])
     full = lse2(raw, store)
     lst_ref[:, mine] = full
     c_ref[:, mine] = cot_total
@@ -302,7 +309,7 @@
 
 
 def swap_kernel(
-    ny, nz, nx, sums, peaks, ms_ref, cot_ref, table_t, cols, rows_ref, rho_ref, ids_ref, inv_ref,
+    ny, nz, nx, sums, peaks, ms_ref, cot_ref, table, cols, rows_ref, rho_ref, ids_ref, inv_ref,
     cv_ref, top_ref, nbl_ref, nbr_ref, left_ref, right_ref, lst_ref, c_ref, cg_ref,
     cotm_ref, part_ref, zbuf, line, ybuf, xsrc, xbuf, values, tops,
     nb_send, nb_recv, z_send, z_recv, y_send, y_recv, x_send, x_recv, g_send, g_recv, t_send, t_recv,
@@ -324,7 +331,7 @@
         pl.semaphore_signal(barrier, inc=1, device_id={"cat": other}, device_id_type=MESH)
     for b in range(left_ref.shape[0]):
         condense(
-            b, sums, peaks, ms_ref, cot_ref, cotm_ref, table_t, cols, ids_ref, part_ref, left_ref, right_ref, lst_ref,
+            b, sums, peaks, ms_ref, cot_ref, cotm_ref, table, cols, ids_ref, part_ref, left_ref, right_ref, lst_ref,
             c_ref,
         )
     pl.semaphore_wait(barrier, nz + ny + nx - 1)
@@ -408,51 +415,69 @@
 
 def slope_kernel(
     wh_ref, wl_ref, lst_ref, r_ref, c_ref, cv_ref, top_ref, nbl_ref, nbr_ref, left_ref, right_ref, cg_ref, ids_ref,
-    rows_ref, cols, rho_ref, grad_ref, path_ref, hs,
+    rows_ref, cols, rho_ref, grad_ref, path_ref, hs, paths,
 ):
     subs = lst_ref.shape[0]
     blocks = nbl_ref.shape[0]
     width = ids_ref.shape[1]
-    lam, par, irho, ilam = cols[0], cols[2], cols[3], cols[4]
     cats = 16
-    spot = iota((subs, LANES), 1)
-    parents = jnp.where(((spot % cats).astype(F32) == par) & (spot < 3 * cats), 1.0, 0.0).astype(BF16)[:, : 3 * cats]
-    row = iota((subs, LANES), 0).astype(F32)
+    base, narrow = reach(ids_ref[...])
+    paths[...] = jnp.zeros_like(paths)
+
+    def fill(base, count):
+        stretch = pl.ds(base, count)
+        lam, par, irho, ilam = cols[0, stretch, :], cols[2, stretch, :], cols[3, stretch, :], cols[4, stretch, :]
+        spot = iota((count, LANES), 1)
+        parents = jnp.where(((spot % cats).astype(F32) == par) & (spot < 3 * cats), 1.0, 0.0).astype(BF16)
+        parents = parents[:, : 3 * cats]
+        row = (iota((count, LANES), 0) + base).astype(F32)
+        for b in range(blocks):
+            at = pl.ds(b * LANES, LANES)
+            from_left, from_right = nbl_ref[b], nbr_ref[b]
+            first_id, last_id = left_ref[b, 2:3, :], right_ref[b, 2:3, :]
+            values, cots = [
+                jnp.concatenate(
+                    pack(cv_ref[2 * b, 8 * k : 8 * k + 8, :], cv_ref[2 * b + 1, 8 * k : 8 * k + 8, :]), axis=0
+                )
+                for k in range(2)
+            ]
+            top = jnp.where(iota((8, LANES), 1) < LANES // 2, top_ref[2 * b], top_ref[2 * b + 1])
+            inclusive = top[0:1]
+            slopes = (1.0 - 1.0 / rho_ref[8:24, :]) * cots - top[1:2] * jnp.exp(values - inclusive)
+            left_hit = (row == first_id) & (from_left[2:3] == first_id)
+            right_hit = (row == last_id) & (from_right[2:3] == last_id)
+            extra = jnp.where(left_hit, from_left[0:1], jnp.where(right_hit, from_right[0:1], NEG))
+            level = lse2(lst_ref[stretch, at], extra)
+            other_cot = jnp.where(left_hit, from_left[1:2], jnp.where(right_hit, from_right[1:2], 0.0))
+            sub_cot = c_ref[stretch, at] + other_cot
+            cat_value = dot(parents, jnp.concatenate(thirds(values), axis=0))
+            d_cat = dot(parents, jnp.concatenate(thirds(slopes), axis=0))
+            log_sub = (lam * level - cat_value) * irho
+            paths[stretch, at] = rows_ref[1:2, at] - level + log_sub + (cat_value - inclusive)
+            d_sub = (irho - ilam) * sub_cot + jnp.exp(log_sub) * d_cat
+            slope = rows_ref[0:1, at] * jnp.exp(r_ref[stretch, at] - level) * d_sub
+            hs[0:count, at], hs[count : 2 * count, at] = halves(slope)
+        for k in range(width // CHUNK):
+            at = pl.ds(k * CHUNK, CHUNK)
+            both = dot(hs[0 : 2 * count, :], wh_ref[:, at])
+            found = both[0:count] + both[count:] + dot(hs[0:count, :], wl_ref[:, at])
+            hit = iota((count, CHUNK), 0) + base == ids_ref[:, at]
+            grad_ref[:, at] = -(jnp.sum(jnp.where(hit, found, 0.0), axis=0, keepdims=True) + cg_ref[:, at])
+
+    @pl.when(narrow)
+    def _():
+        fill(base, WINDOW)
+
+    @pl.when(jnp.logical_not(narrow))
+    def _():
+        fill(0, subs)
+
     for b in range(blocks):
         at = pl.ds(b * LANES, LANES)
-        from_left, from_right = nbl_ref[b], nbr_ref[b]
-        first_id, last_id = left_ref[b, 2:3, :], right_ref[b, 2:3, :]
-        values, cots = [
-            jnp.concatenate(pack(cv_ref[2 * b, 8 * k : 8 * k + 8, :], cv_ref[2 * b + 1, 8 * k : 8 * k + 8, :]), axis=0)
-            for k in range(2)
-        ]
-        top = jnp.where(iota((8, LANES), 1) < LANES // 2, top_ref[2 * b], top_ref[2 * b + 1])
-        inclusive = top[0:1]
-        slopes = (1.0 - 1.0 / rho_ref[8:24, :]) * cots - top[1:2] * jnp.exp(values - inclusive)
-        left_hit = (row == first_id) & (from_left[2:3] == first_id)
-        right_hit = (row == last_id) & (from_right[2:3] == last_id)
-        extra = jnp.where(left_hit, from_left[0:1], jnp.where(right_hit, from_right[0:1], NEG))
-        level = lse2(lst_ref[:, at], extra)
-        sub_cot = c_ref[:, at] + jnp.where(left_hit, from_left[1:2], jnp.where(right_hit, from_right[1:2], 0.0))
-        cat_value = dot(parents, jnp.concatenate(thirds(values), axis=0))
-        d_cat = dot(parents, jnp.concatenate(thirds(slopes), axis=0))
-        log_sub = (lam * level - cat_value) * irho
-        path = rows_ref[1:2, at] - level + log_sub + (cat_value - inclusive)
-        d_sub = (irho - ilam) * sub_cot + jnp.exp(log_sub) * d_cat
-        slope = rows_ref[0:1, at] * jnp.exp(r_ref[:, at] - level) * d_sub
-        hs[0:subs, at], hs[subs:, at] = halves(slope)
-        ph, plo = halves(jnp.transpose(path))
-        path_ref[at, 0:subs] = ph
-        path_ref[at, subs:] = plo
-    for k in range(width // CHUNK):
-        at = pl.ds(k * CHUNK, CHUNK)
-        both = dot(hs[...], wh_ref[:, at])
-        found = both[0:subs] + both[subs:] + dot(hs[0:subs, :], wl_ref[:, at])
-        hit = iota((subs, CHUNK), 0) == ids_ref[:, at]
-        grad_ref[:, at] = -(jnp.sum(jnp.where(hit, found, 0.0), axis=0, keepdims=True) + cg_ref[:, at])
-
-
-ROW_BLOCK = 64
+        path_ref[at, 0:subs], path_ref[at, subs:] = halves(jnp.transpose(paths[:, at]))
+
+
+ROW_BLOCK = 128
 
 
 def demand_kernel(ms_ref, path_ref, table, out_hbm, value_ref, sem):
@@ -504,10 +529,10 @@
     operands = [pltpu.with_memory_space_constraint(x, pltpu.HBM) for x in operands]
     sds = jax.ShapeDtypeStruct
     vmem, dma = pltpu.VMEM, pltpu.SemaphoreType.DMA
-    ms, wh, wl, cot, sums, peaks, table, table_t, cols, rows, rho_rows, ids, inv = pl.pallas_call(
+    ms, wh, wl, cot, sums, peaks, table, cols, rows, rho_rows, ids, inv = pl.pallas_call(
         local_kernel,
         in_specs=[pl.BlockSpec(memory_space=pl.ANY)] * 12,
-        out_specs=[whole()] * 13,
+        out_specs=[whole()] * 12,
         out_shape=[
             sds((markets, width), F32),
             sds((markets, width), BF16),
@@ -516,7 +541,6 @@
             sds((subs, markets), F32),
             sds((subs, markets), F32),
             sds((subs, width), BF16),
-            sds((width, subs), BF16),
             sds((5, subs, LANES), F32),
             sds((8, markets), F32),
             sds((24, LANES), F32),
@@ -534,9 +558,9 @@
             vmem((markets, width), jnp.int32),
             vmem((1, markets), F32),
             vmem((8, CHUNK), F32),
+            vmem((WINDOW, width), BF16),
             dma((8,)),
-            dma,
-            dma((width // CHUNK,)),
+            dma((2,)),
             dma((blocks,)),
             dma,
         ],
@@ -570,14 +594,14 @@
             collective_id=0, has_side_effects=True, vmem_limit_bytes=16 * 1024 * 1024
         ),
         name="swap_nests",
-    )(sums, peaks, ms, cot, table_t, cols, rows, rho_rows, ids, inv)
+    )(sums, peaks, ms, cot, table, cols, rows, rho_rows, ids, inv)
 
     grad, path = pl.pallas_call(
         slope_kernel,
         in_specs=[whole()] * 16,
         out_specs=[whole()] * 2,
         out_shape=[sds((1, width), F32), sds((markets, 2 * subs), BF16)],
-        scratch_shapes=[vmem((2 * subs, markets), BF16)],
+        scratch_shapes=[vmem((2 * subs, markets), BF16), vmem((subs, markets), F32)],
         compiler_params=pltpu.CompilerParams(vmem_limit_bytes=16 * 1024 * 1024),
         name="price_slope",
     )(wh, wl, lst, peaks, c, cv, top, nbl, nbr, left, right, cg, ids, rows, cols, rho_rows)

time: 57.7 us -> 53.6 us (0.929)
  Pallas kernels: 38.2 us -> 34.8 us
  starting transfers between devices: 18.2 us -> 17.4 us
    pallas_call x1, Pallas kernels: 8.65 us -> 6.35 us  [shards(): pl.pallas_call(local_kernel, in_specs=[pl.BlockSpec(memory_space=pl.ANY)]...]
    pallas_call x1, Pallas kernels: 3.27 us -> 2.35 us  [shards(): pl.pallas_call(demand_kernel, in_specs=[whole()] * 3, out_specs=pl.BlockS...]
    ppermute x1, starting transfers between devices: 18.2 us -> 17.4 us  [shards(): other = lax.ppermute(grad, 'mkt', [(0, 1), (1, 0)])]
  transfers between devices with their start and end apart: 1 -> 1, of which waited for: 0 -> 0; matrix products, arithmetic and copies ran while one was open for 0% -> 0% of each run, Pallas kernels for 6% -> 4%
where the time goes in v6:
time: 53.6 us; the launch traced here: 53.5 us
  Pallas kernels  34.8 us (65%)
  starting transfers between devices  17.4 us (32%)
  between operations  0.67 us (1%)
  other arithmetic  0.61 us (1%)
    pallas_call x1, Pallas kernels, shards(): pl.pallas_call(functools.partial(swap_kernel, ny, nz, n_cat), in_specs=[w...  24.8 us
    ppermute x1, starting transfers between devices, shards(): other = lax.ppermute(grad, 'mkt', [(0, 1), (1, 0)])  17.4 us
    pallas_call x1, Pallas kernels, shards(): pl.pallas_call(local_kernel, in_specs=[pl.BlockSpec(memory_space=pl.ANY)]...  6.35 us
    pallas_call x1, Pallas kernels, shards(): pl.pallas_call(demand_kernel, in_specs=[whole()] * 3, out_specs=pl.BlockS...  2.35 us
    pallas_call x1, Pallas kernels, shards(): pl.pallas_call(slope_kernel, in_specs=[whole()] * 16, out_specs=[whole()]...  1.33 us
  transfers between devices with their start and end apart: 1, of which 0 were waited for; matrix products, arithmetic and copies ran while one was open for 0% of the time, Pallas kernels for 4%

profile of v6, /device:TPU:1, one launch (start us, length us, event | category | flops | bytes accessed | tf_op | source)
XLA Modules:
  0.0 53.5 jit_solution(14895280765368618983)
XLA Ops:
  0.6 6.3 %local_nests.1 = (f32[512,2048]{1,0:T(8,128)S(1)}, bf16[512,2048]{1,0:T(8,128)(2,1)S(1)}, bf16[512,2048]{1,0:T(8,128)(2,1)S(1)}, bf16[512,2048]{1,0:T(8,128)(2,1...) custom-call(bf16[512,512]{1,0:T(8,128)(2,1)} %feat_hbm.1, ...), custom_call_target="tpu_custom_call" | custom-call | tf_op jit(solution)/shard_map/local_nests/pallas_call | solution.py:532
  7.0 24.8 %swap_nests.1 = (f32[8,16,128]{2,1,0:T(8,128)S(1)}, f32[8,8,128]{2,1,0:T(8,128)S(1)}, f32[4,8,128]{2,1,0:T(8,128)S(1)}, f32[4,8,128]{2,1,0:T(8,128)S(1)}, f32[4,...) custom-call(f32[128,512]{1,0:T(8,128)S(1)} %get-tuple-element.28.sum, ...), custom_call_target="tpu_custom_call" | custom-call | tf_op jit(solution)/shard_map/swap_nests/pallas_call | solution.py:573
  31.8 1.3 %price_slope.1 = (f32[1,2048]{1,0:T(1,128)S(1)}, bf16[512,256]{1,0:T(8,128)(2,1)S(1)}) custom-call(bf16[512,2048]{1,0:T(8,128)(2,1)S(1)} %get-tuple-element.26.wh_ref, bf16[512,2048]{1,0:T(8,128)(2,1)S(1)} %get-tuple-element.27.wl_ref, f32[128,512]{1,0:T(8,128)S(1)} %get-tuple-element.37.lst_ref, f32[128,512]{1,0:T(8,128)S(1)} %get-tuple-element.29.peaks.r_ref, ...), custom_call_target="tpu_custom_call" | custom-call | tf_op jit(solution)/shard_map/price_slope/pallas_call | solution.py:599
  33.1 17.4 %collective-permute-start = (f32[1,2048]{1,0:T(1,128)S(1)}, f32[1,2048]{1,0:T(1,128)S(1)}, u32[]{:S(2)}, u32[]{:S(2)}) collective-permute-start(f32[1,2048]{1,0:T(1,128)S(1)} %get-tuple-element.47), channel_id=1, source_target_pairs={{0,128},{128,0},{1,129},{129,1},{2,130},{130,2},{3,131},{131,3},{4... | collective-permute-start | bytes 24584 | tf_op jit(solution)/shard_map/ppermute | solution.py:608
  50.5 2.4 %log_demand.1 = f32[512,1,2048]{2,1,0:T(1,128)} custom-call(f32[512,2048]{1,0:T(8,128)S(1)} %get-tuple-element.25.ms_ref, bf16[512,256]{1,0:T(8,128)(2,1)S(1)} %get-tuple-element.46.path_ref, bf16[128,2048]{1,0:T(8,128)(2,1)S(1)} %get-tuple-element.31.table), custom_call_target="tpu_custom_call" | custom-call | flops 536870912 | bytes 8388608 | tf_op jit(solution)/shard_map/log_demand/pallas_call | solution.py:610
  52.9 0.0 collective-permute-done
  52.9 0.6 %add.3 = f32[1,2048]{1,0:T(1,128)} add(f32[1,2048]{1,0:T(1,128)S(1)} %get-tuple-element.47, f32[1,2048]{1,0:T(1,128)S(1)} %collective-permute-done) | non-fusion elementwise | flops 2048 | bytes 24576 | tf_op jit(solution)/shard_map/add | solution.py:622
Async XLA Ops:
  33.1 19.7 %collective-permute-start = (f32[1,2048]{1,0:T(1,128)S(1)}, f32[1,2048]{1,0:T(1,128)S(1)}, u32[]{:S(2)}, u32[]{:S(2)}) collective-permute-start(f32[1,2048]{1,0:T(1,128)S(1)} %get-tuple-element.47), channel_id=1, source_target_pairs={{0,128},{128,0},{1,129},{129,1},{2,130},{130,2},{3,131},{131,3},{4... | collective-permute-start | bytes 24584 | tf_op jit(solution)/shard_map/ppermute | solution.py:608

commit v7 on v6

--- a/solution.py
+++ b/solution.py
@@ -85,7 +85,7 @@
 def local_kernel(
     feat_hbm, taste_hbm, price_hbm, alpha_hbm, size_hbm, lam_hbm, store_hbm, rho_hbm, par_hbm, avail_hbm, mem_hbm,
     cot_hbm,
-    ms_ref, wh_ref, wl_ref, cot_ref, sums, peaks, table, cols, rows_ref, rho_rows, ids_ref, inv_ref,
+    ms_ref, wh_ref, wl_ref, cotm_ref, sums, cot_sums, peaks, table, cols, rows_ref, rho_rows, ids_ref, inv_ref,
     feat, taste, price, lam_row, store_row, rho_row, par_row, avail, size, worst, near,
     small_sem, big_sem, avail_sem, cot_sem,
 ):
@@ -104,17 +104,19 @@
         pltpu.make_async_copy(src, dst, big_sem.at[k])
         for k, (src, dst) in enumerate([(taste_hbm, taste), (feat_hbm, feat)])
     ]
-    whole_cot = pltpu.make_async_copy(cot_hbm, cot_ref, cot_sem)
 
     def fetch(b):
         rows = pl.ds(pl.multiple_of(b * LANES, LANES), LANES)
-        return pltpu.make_async_copy(avail_hbm.at[rows, 0, :], avail.at[rows], avail_sem.at[b])
-
-    for copy in small[:3] + big + [fetch(0)] + small[3:]:
+        return (
+            pltpu.make_async_copy(avail_hbm.at[rows, 0, :], avail.at[rows], avail_sem.at[b]),
+            pltpu.make_async_copy(cot_hbm.at[rows], cotm_ref.at[rows], cot_sem.at[b]),
+        )
+
+    for copy in small[:3] + big + list(fetch(0)) + small[3:]:
         copy.start()
     for b in range(1, blocks):
-        fetch(b).start()
-    whole_cot.start()
+        for copy in fetch(b):
+            copy.start()
     for copy in small:
         copy.wait()
 
@@ -130,6 +132,7 @@
         inv_ref[1:2, at] = inv * price[:, at]
     worst[...] = jnp.zeros_like(worst)
     sums[...] = jnp.zeros_like(sums)
+    cot_sums[...] = jnp.zeros_like(cot_sums)
     peaks[...] = jnp.zeros_like(peaks)
     _, ilam, store, par, irho = nest_columns(lam_row, store_row, rho_row, par_row)
     for k, col in enumerate((lam, store, par, irho, ilam)):
@@ -144,23 +147,28 @@
     @pl.loop(0, blocks)
     def _(b):
         mine = pl.ds(pl.multiple_of(b * LANES, LANES), LANES)
-        fetch(b).wait()
+        for copy in fetch(b):
+            copy.wait()
         alpha = jnp.transpose(jnp.broadcast_to(rows_ref[0:1, mine], (LANES, LANES)))
         alpha2 = jnp.concatenate([alpha, alpha], axis=1)
-        total = jnp.zeros((WINDOW, 2 * LANES), F32)
+        total = jnp.zeros((WINDOW, 3 * LANES), F32)
         most = jnp.zeros((8, CHUNK), F32)
         for k in range(chunks):
             at = pl.ds(k * CHUNK, CHUNK)
             util = dot(feat[mine, :], taste[:, at])
             scaled = util * inv_ref[0:1, at] - alpha2 * inv_ref[1:2, at]
-            masked = jnp.where(avail[mine, at] == 1, scaled, NEG)
+            open_ = avail[mine, at]
+            masked = jnp.where(open_ == 1, scaled, NEG)
             ms_ref[mine, at] = masked
             most = jnp.maximum(most, jnp.max(jnp.abs(scaled).reshape(LANES // 8, 8, CHUNK), axis=0))
             wh, wl = halves(jnp.exp(masked))
             wh_ref[mine, at] = wh
             wl_ref[mine, at] = wl
-            total = total + dot_nt(near[:, at], jnp.concatenate([wh, wl], axis=0))
-        sums[pl.ds(base, WINDOW), mine] = total[:, :LANES] + total[:, LANES:]
+            cotm = cotm_ref[mine, at] * open_.astype(F32).astype(BF16)
+            cotm_ref[mine, at] = cotm
+            total = total + dot_nt(near[:, at], jnp.concatenate([wh, wl, cotm], axis=0))
+        sums[pl.ds(base, WINDOW), mine] = total[:, :LANES] + total[:, LANES : 2 * LANES]
+        cot_sums[pl.ds(base, WINDOW), mine] = total[:, 2 * LANES :]
         worst[...] = jnp.maximum(worst[...], most)
 
     @pl.when(jnp.logical_not(narrow))
@@ -169,8 +177,7 @@
         def _(b):
             mine = pl.ds(pl.multiple_of(b * LANES, LANES), LANES)
             sums[:, mine] = dot_nt(table[...], wh_ref[mine, :]) + dot_nt(table[...], wl_ref[mine, :])
-
-    whole_cot.wait()
+            cot_sums[:, mine] = dot_nt(table[...], cotm_ref[mine, :])
 
     @pl.when(jnp.max(worst[...]) > SAFE)
     def _():
@@ -214,21 +221,17 @@
             sums[:, mine] = total[:, :LANES] + total[:, LANES:]
 
 
-def condense(b, sums, peaks, ms_ref, cot_ref, cotm_ref, table, cols, ids_ref, part_ref, left_ref, right_ref, lst_ref, c_ref):
+def condense(b, sums, cot_sums, peaks, cols, ids_ref, part_ref, left_ref, right_ref, lst_ref):
     cats = 16
     subs = sums.shape[0]
     width = ids_ref.shape[1]
     mine = pl.ds(b * LANES, LANES)
-    for k in range(width // CHUNK):
-        at = pl.ds(k * CHUNK, CHUNK)
-        cotm_ref[mine, at] = cot_ref[mine, at] * jnp.where(ms_ref[mine, at] > EMPTY, 1.0, 0.0).astype(BF16)
     total = sums[:, mine]
     raw = jnp.where(total > 0.0, peaks[:, mine] + jnp.log(jnp.where(total > 0.0, total, 1.0)), NEG)
     lam, store, par, irho = cols[0], cols[1], cols[2], cols[3]
-    cot_total = dot_nt(table[...], cotm_ref[mine, :])
+    cot_total = cot_sums[:, mine]
     full = lse2(raw, store)
     lst_ref[:, mine] = full
-    c_ref[:, mine] = cot_total
     row = iota((subs, LANES), 0)
     first, last = ids_ref[:, 0:1], ids_ref[:, width - 1 :]
     is_first, is_last = row == first, row == last
@@ -309,20 +312,20 @@
 
 
 def swap_kernel(
-    ny, nz, nx, sums, peaks, ms_ref, cot_ref, table, cols, rows_ref, rho_ref, ids_ref, inv_ref,
-    cv_ref, top_ref, nbl_ref, nbr_ref, left_ref, right_ref, lst_ref, c_ref, cg_ref,
-    cotm_ref, part_ref, zbuf, line, ybuf, xsrc, xbuf, values, tops,
+    ny, nz, nx, sums, cot_sums, peaks, cotm_ref, cols, rows_ref, rho_ref, ids_ref, inv_ref,
+    cv_ref, top_ref, nbl_ref, nbr_ref, left_ref, right_ref, lst_ref, cg_ref,
+    part_ref, zbuf, line, ybuf, xsrc, xbuf, values, tops,
     nb_send, nb_recv, z_send, z_recv, y_send, y_recv, x_send, x_recv, g_send, g_recv, t_send, t_recv,
 ):
     sku = lax.axis_index("sku")
     cat = lax.axis_index("cat")
-    y, z = sku // nz, sku % nz
+    y, z = lax.div(sku, nz), lax.rem(sku, nz)
     n = ny * nz
-    to_right, to_left = (sku + 1) % n, (sku + n - 1) % n
-    next_z = [(z + k) % nz for k in range(1, nz)]
+    to_right, to_left = lax.rem(sku + 1, n), lax.rem(sku + n - 1, n)
+    next_z = [lax.rem(z + k, nz) for k in range(1, nz)]
     along_z = [y * nz + other for other in next_z]
-    along_y = [(y + k) % ny * nz + z for k in range(1, ny)]
-    along_x = [(cat + k) % nx for k in range(1, nx)]
+    along_y = [lax.rem(y + k, ny) * nz + z for k in range(1, ny)]
+    along_x = [lax.rem(cat + k, nx) for k in range(1, nx)]
 
     barrier = pltpu.get_barrier_semaphore()
     for other in along_z + along_y + [to_right, to_left]:
@@ -330,10 +333,7 @@
     for other in along_x:
         pl.semaphore_signal(barrier, inc=1, device_id={"cat": other}, device_id_type=MESH)
     for b in range(left_ref.shape[0]):
-        condense(
-            b, sums, peaks, ms_ref, cot_ref, cotm_ref, table, cols, ids_ref, part_ref, left_ref, right_ref, lst_ref,
-            c_ref,
-        )
+        condense(b, sums, cot_sums, peaks, cols, ids_ref, part_ref, left_ref, right_ref, lst_ref)
     pl.semaphore_wait(barrier, nz + ny + nx - 1)
 
     def send(src, dst, send_sem, recv_sem, device):
@@ -529,15 +529,16 @@
     operands = [pltpu.with_memory_space_constraint(x, pltpu.HBM) for x in operands]
     sds = jax.ShapeDtypeStruct
     vmem, dma = pltpu.VMEM, pltpu.SemaphoreType.DMA
-    ms, wh, wl, cot, sums, peaks, table, cols, rows, rho_rows, ids, inv = pl.pallas_call(
+    ms, wh, wl, cotm, sums, c, peaks, table, cols, rows, rho_rows, ids, inv = pl.pallas_call(
         local_kernel,
         in_specs=[pl.BlockSpec(memory_space=pl.ANY)] * 12,
-        out_specs=[whole()] * 12,
+        out_specs=[whole()] * 13,
         out_shape=[
             sds((markets, width), F32),
             sds((markets, width), BF16),
             sds((markets, width), BF16),
             sds((markets, width), BF16),
+            sds((subs, markets), F32),
             sds((subs, markets), F32),
             sds((subs, markets), F32),
             sds((subs, width), BF16),
@@ -562,7 +563,7 @@
             dma((8,)),
             dma((2,)),
             dma((blocks,)),
-            dma,
+            dma((blocks,)),
         ],
         compiler_params=pltpu.CompilerParams(vmem_limit_bytes=32 * 1024 * 1024),
         name="local_nests",
@@ -570,16 +571,15 @@
 
     nz = 2 * blocks
     ny = n_sku // nz
-    cv, top, nbl, nbr, left, right, lst, c, cg = pl.pallas_call(
+    cv, top, nbl, nbr, left, right, lst, cg = pl.pallas_call(
         functools.partial(swap_kernel, ny, nz, n_cat),
-        in_specs=[whole()] * 10,
-        out_specs=[whole()] * 9,
+        in_specs=[whole()] * 9,
+        out_specs=[whole()] * 8,
         out_shape=[sds((nz, 16, LANES), F32), sds((nz, 8, LANES), F32)]
         + [sds((blocks, 8, LANES), F32)] * 4
-        + [sds((subs, markets), F32)] * 2
+        + [sds((subs, markets), F32)]
         + [sds((1, width), F32)],
         scratch_shapes=[
-            vmem((markets, width), BF16),
             vmem((nz, 24, LANES), F32),
             vmem((nz * 24, LANES), F32),
             vmem((24, LANES), F32),
@@ -594,7 +594,7 @@
             collective_id=0, has_side_effects=True, vmem_limit_bytes=16 * 1024 * 1024
         ),
         name="swap_nests",
-    )(sums, peaks, ms, cot, table, cols, rows, rho_rows, ids, inv)
+    )(sums, c, peaks, cotm, cols, rows, rho_rows, ids, inv)
 
     grad, path = pl.pallas_call(
         slope_kernel,

time: 53.6 us -> 55 us (1.026)
  Pallas kernels: 34.8 us -> 36.5 us
    pallas_call x1, Pallas kernels: 6.35 us -> 7.76 us  [shards(): pl.pallas_call(local_kernel, in_specs=[pl.BlockSpec(memory_space=pl.ANY)]...]
where the time goes in v7:
time: 55 us; the launch traced here: 54.9 us
  Pallas kernels  36.5 us (66%)
  starting transfers between devices  17.1 us (31%)
  between operations  0.67 us (1%)
  other arithmetic  0.61 us (1%)
    pallas_call x1, Pallas kernels, shards(): pl.pallas_call(functools.partial(swap_kernel, ny, nz, n_cat), in_specs=[w...  25.1 us
    ppermute x1, starting transfers between devices, shards(): other = lax.ppermute(grad, 'mkt', [(0, 1), (1, 0)])  17.1 us
    pallas_call x1, Pallas kernels, shards(): pl.pallas_call(local_kernel, in_specs=[pl.BlockSpec(memory_space=pl.ANY)]...  7.76 us
    pallas_call x1, Pallas kernels, shards(): pl.pallas_call(demand_kernel, in_specs=[whole()] * 3, out_specs=pl.BlockS...  2.35 us
    pallas_call x1, Pallas kernels, shards(): pl.pallas_call(slope_kernel, in_specs=[whole()] * 16, out_specs=[whole()]...  1.33 us
  transfers between devices with their start and end apart: 1, of which 0 were waited for; matrix products, arithmetic and copies ran while one was open for 0% of the time, Pallas kernels for 4%

profile of v7, /device:TPU:1, one launch (start us, length us, event | category | flops | bytes accessed | tf_op | source)
XLA Modules:
  0.0 54.9 jit_solution(2926793701587715986)
XLA Ops:
  0.6 7.8 %local_nests.1 = (f32[512,2048]{1,0:T(8,128)S(1)}, bf16[512,2048]{1,0:T(8,128)(2,1)S(1)}, bf16[512,2048]{1,0:T(8,128)(2,1)S(1)}, bf16[512,2048]{1,0:T(8,128)(2,1...) custom-call(bf16[512,512]{1,0:T(8,128)(2,1)} %feat_hbm.1, ...), custom_call_target="tpu_custom_call" | custom-call | tf_op jit(solution)/shard_map/local_nests/pallas_call | solution.py:532
  8.4 25.1 %swap_nests.1 = (f32[8,16,128]{2,1,0:T(8,128)S(1)}, f32[8,8,128]{2,1,0:T(8,128)S(1)}, f32[4,8,128]{2,1,0:T(8,128)S(1)}, f32[4,8,128]{2,1,0:T(8,128)S(1)}, f32[4,...) custom-call(f32[128,512]{1,0:T(8,128)S(1)} %get-tuple-element.28.sums, ...), custom_call_target="tpu_custom_call" | custom-call | tf_op jit(solution)/shard_map/swap_nests/pallas_call | solution.py:574
  33.5 1.3 %price_slope.1 = (f32[1,2048]{1,0:T(1,128)S(1)}, bf16[512,256]{1,0:T(8,128)(2,1)S(1)}) custom-call(bf16[512,2048]{1,0:T(8,128)(2,1)S(1)} %get-tuple-element.26.wh_ref, bf16[512,2048]{1,0:T(8,128)(2,1)S(1)} %get-tuple-element.27.wl_ref, f32[128,512]{1,0:T(8,128)S(1)} %get-tuple-element.37.lst_ref, f32[128,512]{1,0:T(8,128)S(1)} %get-tuple-element.30.peaks.r_ref, ...), custom_call_target="tpu_custom_call" | custom-call | tf_op jit(solution)/shard_map/price_slope/pallas_call | solution.py:599
  34.8 17.1 %collective-permute-start = (f32[1,2048]{1,0:T(1,128)S(1)}, f32[1,2048]{1,0:T(1,128)S(1)}, u32[]{:S(2)}, u32[]{:S(2)}) collective-permute-start(f32[1,2048]{1,0:T(1,128)S(1)} %get-tuple-element.47), channel_id=1, source_target_pairs={{0,128},{128,0},{1,129},{129,1},{2,130},{130,2},{3,131},{131,3},{4... | collective-permute-start | bytes 24584 | tf_op jit(solution)/shard_map/ppermute | solution.py:608
  51.9 2.4 %log_demand.1 = f32[512,1,2048]{2,1,0:T(1,128)} custom-call(f32[512,2048]{1,0:T(8,128)S(1)} %get-tuple-element.25.ms_ref, bf16[512,256]{1,0:T(8,128)(2,1)S(1)} %get-tuple-element.45.path_ref, bf16[128,2048]{1,0:T(8,128)(2,1)S(1)} %get-tuple-element.46.table), custom_call_target="tpu_custom_call" | custom-call | flops 536870912 | bytes 8388608 | tf_op jit(solution)/shard_map/log_demand/pallas_call | solution.py:610
  54.2 0.0 collective-permute-done
  54.3 0.6 %add.3 = f32[1,2048]{1,0:T(1,128)} add(f32[1,2048]{1,0:T(1,128)S(1)} %get-tuple-element.47, f32[1,2048]{1,0:T(1,128)S(1)} %collective-permute-done) | non-fusion elementwise | flops 2048 | bytes 24576 | tf_op jit(solution)/shard_map/add | solution.py:622
Async XLA Ops:
  34.8 19.4 %collective-permute-start = (f32[1,2048]{1,0:T(1,128)S(1)}, f32[1,2048]{1,0:T(1,128)S(1)}, u32[]{:S(2)}, u32[]{:S(2)}) collective-permute-start(f32[1,2048]{1,0:T(1,128)S(1)} %get-tuple-element.47), channel_id=1, source_target_pairs={{0,128},{128,0},{1,129},{129,1},{2,130},{130,2},{3,131},{131,3},{4... | collective-permute-start | bytes 24584 | tf_op jit(solution)/shard_map/ppermute | solution.py:608

commit v8 on v6

--- a/solution.py
+++ b/solution.py
@@ -110,12 +110,12 @@
         rows = pl.ds(pl.multiple_of(b * LANES, LANES), LANES)
         return pltpu.make_async_copy(avail_hbm.at[rows, 0, :], avail.at[rows], avail_sem.at[b])
 
-    for copy in small[:3] + big + [fetch(0)] + small[3:]:
+    for copy in small[:3] + big + small[3:] + [fetch(0)]:
         copy.start()
     for b in range(1, blocks):
         fetch(b).start()
     whole_cot.start()
-    for copy in small:
+    for copy in small[:3]:
         copy.wait()
 
     base, narrow = reach(ids_ref[...])
@@ -131,6 +131,8 @@
     worst[...] = jnp.zeros_like(worst)
     sums[...] = jnp.zeros_like(sums)
     peaks[...] = jnp.zeros_like(peaks)
+    for copy in small[3:]:
+        copy.wait()
     _, ilam, store, par, irho = nest_columns(lam_row, store_row, rho_row, par_row)
     for k, col in enumerate((lam, store, par, irho, ilam)):
         cols[k] = jnp.broadcast_to(col, (subs, LANES))
@@ -316,13 +318,13 @@
 ):
     sku = lax.axis_index("sku")
     cat = lax.axis_index("cat")
-    y, z = sku // nz, sku % nz
+    y, z = lax.div(sku, nz), lax.rem(sku, nz)
     n = ny * nz
-    to_right, to_left = (sku + 1) % n, (sku + n - 1) % n
-    next_z = [(z + k) % nz for k in range(1, nz)]
+    to_right, to_left = lax.rem(sku + 1, n), lax.rem(sku + n - 1, n)
+    next_z = [lax.rem(z + k, nz) for k in range(1, nz)]
     along_z = [y * nz + other for other in next_z]
-    along_y = [(y + k) % ny * nz + z for k in range(1, ny)]
-    along_x = [(cat + k) % nx for k in range(1, nx)]
+    along_y = [lax.rem(y + k, ny) * nz + z for k in range(1, ny)]
+    along_x = [lax.rem(cat + k, nx) for k in range(1, nx)]
 
     barrier = pltpu.get_barrier_semaphore()
     for other in along_z + along_y + [to_right, to_left]:

time: 53.6 us -> 53.4 us (level)
  no operation moved by 1% of the time
where the time goes in v8:
time: 53.4 us; the launch traced here: 53.3 us
  Pallas kernels  34.8 us (65%)
  starting transfers between devices  17.2 us (32%)
  between operations  0.67 us (1%)
  other arithmetic  0.61 us (1%)
    pallas_call x1, Pallas kernels, shards(): pl.pallas_call(functools.partial(swap_kernel, ny, nz, n_cat), in_specs=[w...  24.9 us
    ppermute x1, starting transfers between devices, shards(): other = lax.ppermute(grad, 'mkt', [(0, 1), (1, 0)])  17.2 us
    pallas_call x1, Pallas kernels, shards(): pl.pallas_call(local_kernel, in_specs=[pl.BlockSpec(memory_space=pl.ANY)]...  6.22 us
    pallas_call x1, Pallas kernels, shards(): pl.pallas_call(demand_kernel, in_specs=[whole()] * 3, out_specs=pl.BlockS...  2.35 us
    pallas_call x1, Pallas kernels, shards(): pl.pallas_call(slope_kernel, in_specs=[whole()] * 16, out_specs=[whole()]...  1.33 us
  transfers between devices with their start and end apart: 1, of which 0 were waited for; matrix products, arithmetic and copies ran while one was open for 0% of the time, Pallas kernels for 4%

profile of v8, /device:TPU:1, one launch (start us, length us, event | category | flops | bytes accessed | tf_op | source)
XLA Modules:
  0.0 53.3 jit_solution(17334573134300198316)
XLA Ops:
  0.6 6.2 %local_nests.1 = (f32[512,2048]{1,0:T(8,128)S(1)}, bf16[512,2048]{1,0:T(8,128)(2,1)S(1)}, bf16[512,2048]{1,0:T(8,128)(2,1)S(1)}, bf16[512,2048]{1,0:T(8,128)(2,1...) custom-call(bf16[512,512]{1,0:T(8,128)(2,1)} %feat_hbm.1, ...), custom_call_target="tpu_custom_call" | custom-call | tf_op jit(solution)/shard_map/local_nests/pallas_call | solution.py:534
  6.9 24.9 %swap_nests.1 = (f32[8,16,128]{2,1,0:T(8,128)S(1)}, f32[8,8,128]{2,1,0:T(8,128)S(1)}, f32[4,8,128]{2,1,0:T(8,128)S(1)}, f32[4,8,128]{2,1,0:T(8,128)S(1)}, f32[4,...) custom-call(f32[128,512]{1,0:T(8,128)S(1)} %get-tuple-element.28.sum, ...), custom_call_target="tpu_custom_call" | custom-call | tf_op jit(solution)/shard_map/swap_nests/pallas_call | solution.py:575
  31.8 1.3 %price_slope.1 = (f32[1,2048]{1,0:T(1,128)S(1)}, bf16[512,256]{1,0:T(8,128)(2,1)S(1)}) custom-call(bf16[512,2048]{1,0:T(8,128)(2,1)S(1)} %get-tuple-element.26.wh_ref, bf16[512,2048]{1,0:T(8,128)(2,1)S(1)} %get-tuple-element.27.wl_ref, f32[128,512]{1,0:T(8,128)S(1)} %get-tuple-element.37.lst_ref, f32[128,512]{1,0:T(8,128)S(1)} %get-tuple-element.29.peaks.r_ref, ...), custom_call_target="tpu_custom_call" | custom-call | tf_op jit(solution)/shard_map/price_slope/pallas_call | solution.py:601
  33.1 17.2 %collective-permute-start = (f32[1,2048]{1,0:T(1,128)S(1)}, f32[1,2048]{1,0:T(1,128)S(1)}, u32[]{:S(2)}, u32[]{:S(2)}) collective-permute-start(f32[1,2048]{1,0:T(1,128)S(1)} %get-tuple-element.47), channel_id=1, source_target_pairs={{0,128},{128,0},{1,129},{129,1},{2,130},{130,2},{3,131},{131,3},{4... | collective-permute-start | bytes 24584 | tf_op jit(solution)/shard_map/ppermute | solution.py:610
  50.3 2.4 %log_demand.1 = f32[512,1,2048]{2,1,0:T(1,128)} custom-call(f32[512,2048]{1,0:T(8,128)S(1)} %get-tuple-element.25.ms_ref, bf16[512,256]{1,0:T(8,128)(2,1)S(1)} %get-tuple-element.46.path_ref, bf16[128,2048]{1,0:T(8,128)(2,1)S(1)} %get-tuple-element.31.table), custom_call_target="tpu_custom_call" | custom-call | flops 536870912 | bytes 8388608 | tf_op jit(solution)/shard_map/log_demand/pallas_call | solution.py:612
  52.7 0.0 collective-permute-done
  52.7 0.6 %add.3 = f32[1,2048]{1,0:T(1,128)} add(f32[1,2048]{1,0:T(1,128)S(1)} %get-tuple-element.47, f32[1,2048]{1,0:T(1,128)S(1)} %collective-permute-done) | non-fusion elementwise | flops 2048 | bytes 24576 | tf_op jit(solution)/shard_map/add | solution.py:624
Async XLA Ops:
  33.1 19.6 %collective-permute-start = (f32[1,2048]{1,0:T(1,128)S(1)}, f32[1,2048]{1,0:T(1,128)S(1)}, u32[]{:S(2)}, u32[]{:S(2)}) collective-permute-start(f32[1,2048]{1,0:T(1,128)S(1)} %get-tuple-element.47), channel_id=1, source_target_pairs={{0,128},{128,0},{1,129},{129,1},{2,130},{130,2},{3,131},{131,3},{4... | collective-permute-start | bytes 24584 | tf_op jit(solution)/shard_map/ppermute | solution.py:610
